TPU v7x, 32 devices: a whole 2x2x4 slice. The times are simulated.
32 devices in a mesh: chan: 4 (over x, core), fam: 8 (over z, y).
Axes of the slice: x: 2, y: 2, z: 4, core: 2. Of those that a mesh axis runs over, the one named last changes fastest.
Arguments:
- waveforms: bfloat16 [1024, 256, 256], P('fam', 'chan'), may hold values from -18 to 18
- family_of: int32 [1024], P('fam'), may hold values from 0 to 7, as said below
- channel_mask: int32 [8, 256], P('fam', 'chan'), may hold values 0 or 1
Outputs:
- correlation: float32 [8, 128, 65, 128], P('fam', 'chan')
Inputs may be any that keep to these rules, and one draw needn't show every extreme that they name: `family_of`: in each aligned block of 128 events (the events of one index of fam) at most 16 events share a family, and some family has exactly 16 of them.
All inputs are finite; a program needn't handle non-finite values. No bound on the sum of `channel_mask` on one device may be relied on, other than what follows from the above.
Results may differ from a plain program's by a relative error of at most 0.0003.
Values may be sent and summed in bfloat16 or wider, within the bound.
No kernel may reach another device: no remote copies, remote signals or barrier semaphores. Data moves between devices by JAX's collectives and lax.ppermute only.
A program may use at most 192 MiB of HBM per device.

v0:
```python
import math

import jax
import jax.numpy as jnp
from jax import lax
from jax.sharding import PartitionSpec as P

MAXLAG = 32
CAP = 16


HIGH = lax.Precision.HIGHEST


def transform_table(length):
    bins = length // 2
    times = jnp.arange(length, dtype=jnp.int32)
    freqs = jnp.arange(bins, dtype=jnp.int32)
    phase = times[:, None] * freqs[None, :] % length
    angle = phase.astype(jnp.float32) * (2.0 * math.pi / length)
    return jnp.concatenate([jnp.cos(angle), -jnp.sin(angle)], axis=1)


def smoothing_table(bins):
    index = jnp.arange(bins, dtype=jnp.int32)
    near = (jnp.abs(index[:, None] - index[None, :]) <= 4).astype(jnp.float32)
    return near / jnp.sum(near, axis=0, keepdims=True)


def lag_table(bins, maxlag, length):
    freqs = jnp.arange(bins, dtype=jnp.int32)
    shifts = jnp.arange(2 * maxlag + 1, dtype=jnp.int32) - maxlag
    phase = shifts[:, None] * freqs[None, :] % length
    angle = phase.astype(jnp.float32) * (2.0 * math.pi / length)
    return jnp.concatenate([jnp.cos(angle), -jnp.sin(angle)], axis=1)


def whiten(windows):
    length = windows.shape[-1]
    bins = length // 2
    flat = windows.reshape(-1, length).astype(jnp.float32)
    spec = jnp.dot(
        flat, transform_table(length), precision=HIGH, preferred_element_type=jnp.float32
    )
    real = spec[:, :bins]
    imag = spec[:, bins:]
    power = real * real + imag * imag
    smooth = jnp.dot(
        power, smoothing_table(bins), precision=HIGH, preferred_element_type=jnp.float32
    )
    level = jnp.mean(power, axis=1, keepdims=True)
    scale = jnp.sqrt(smooth + 0.1 * level + 1e-05)
    white = spec / jnp.concatenate([scale, scale], axis=1)
    return white.reshape(windows.shape[:-1] + (length,))


def paired_columns(cols):
    bins = cols.shape[-1] // 2
    right = cols.reshape(cols.shape[0], cols.shape[1], 2, bins)
    swapped = jnp.stack([-right[:, :, 1], right[:, :, 0]], axis=2)
    return jnp.stack([right, swapped], axis=2)


def pair_terms(rows, both, table):
    bins = rows.shape[-1] // 2
    left = rows.reshape(rows.shape[0], rows.shape[1], 2, bins)
    cross = jnp.einsum("icpk,jcqpk->iqkj", left, both, precision=HIGH)
    cross = cross.reshape(rows.shape[0], 2 * bins, both.shape[0])
    return jnp.einsum("tq,iqj->itj", table, cross, precision=HIGH)


def local(waveforms, family_of, channel_mask):
    owners = lax.axis_size("fam")
    groups = lax.axis_size("chan")
    flags = (family_of[:, None] == jnp.arange(owners, dtype=jnp.int32)[None, :]).astype(jnp.int32)
    rank = jnp.sum(jnp.cumsum(flags, axis=0) * flags, axis=1) - 1
    target = family_of * CAP + rank
    trailing = waveforms.shape[1:]
    white = whiten(waveforms)
    outbox = jnp.zeros((owners * CAP,) + trailing, jnp.float32).at[target].set(white)
    inbox = lax.all_to_all(
        outbox.reshape((owners, CAP) + trailing), "fam", split_axis=0, concat_axis=0, tiled=True
    )
    spectra = inbox.reshape((owners * CAP,) + trailing)
    mask = channel_mask[0].astype(jnp.float32)
    member = spectra * mask[None, :, None]
    slots = member.shape[0]
    energy = lax.psum(jnp.sum(member * member, axis=(1, 2)), "chan")
    lags = lag_table(member.shape[2] // 2, MAXLAG, member.shape[2])
    both = paired_columns(member)
    rows = slots // groups
    block = math.gcd(rows * lax.axis_size("chan"), 64)

    def one_block(index):
        piece = lax.dynamic_slice_in_dim(member, index * block, block, 0)
        return pair_terms(piece, both, lags)

    blocks_out = lax.map(
        one_block, jnp.arange(rows * lax.axis_size("chan") // block, dtype=jnp.int32)
    )
    total = lax.psum_scatter(
        blocks_out.reshape((rows * lax.axis_size("chan"),) + blocks_out.shape[2:]),
        "chan",
        scatter_dimension=0,
        tiled=True,
    )
    norm = jnp.sqrt(energy + 1e-05)
    own_norm = lax.dynamic_slice_in_dim(norm, lax.axis_index("chan") * rows, rows, 0)
    result = total / (own_norm[:, None, None] * norm[None, None, :])
    return result[None]


def solution(mesh):
    in_specs = (P("fam", "chan", None), P("fam"), P("fam", "chan"))
    out_specs = P("fam", "chan", None, None)
    return jax.shard_map(local, mesh=mesh, in_specs=in_specs, out_specs=out_specs, check_vma=False)
```

profile of v0, /device:TPU:0, one launch (start us, length us, event | category | flops | bytes accessed | tf_op | source)
XLA Modules:
  0.0 514.1 jit_solution(3330973732212881556)
XLA Ops:
  9.5 8.6 %convolution_bitcast_fusion.2 = f32[8192,256]{0,1:T(8,128)S(1)} fusion(bf16[8192,256]{1,0:T(8,128)(2,1)} %bitcast.63, f32[256,128]{1,0:T(8,128)S(1)} %get-tuple-element.66, f32[256,128]{1,0:T(8,128)S(1)} %get-tuple-element.67), kind=kOutput, calls=%fused_computation.7 | convolution fusion | flops 6442516480 | bytes 12845056 | tf_op jit(solution)/shard_map/dot_general | solution.py:42
  18.9 5.8 %fusion.2 = f32[8192,128]{0,1:T(8,128)S(1)} fusion(f32[8192]{0:T(1024)S(1)} %broadcast_multiply_fusion.2, f32[8192,256]{0,1:T(8,128)S(1)} %convolution_bitcast_fusion.2, f32[128]{0:T(128)S(1)} %convert_reduce_fusion), kind=kOutput, calls=%fused_computation.10 | convolution fusion | flops 1615937536 | bytes 12616192 | tf_op jit(solution)/shard_map/dot_general | solution.py:48
  28.8 9.2 %copy.12 = f32[8192,256]{1,0:T(8,128)} copy(f32[8192,256]{0,1:T(8,128)} %maximum_divide_fusion) | data formatting | bytes 16777216 | tf_op jit(solution)/shard_map/div | solution.py:53
  42.4 23.2 %scatter_fusion = f32[128,64,256]{2,1,0:T(8,128)} fusion(f32[128,64,256]{2,1,0:T(8,128)} %broadcast_in_dim.12, s32[128]{0:T(128)S(1)} %compare_select_fusion, f32[128,64,256]{2,1,0:T(8,128)} %bitcast.59), kind=kCustom, calls=%fused_computation | custom fusion | bytes 25166336 | tf_op jit(solution)/shard_map/scatter | solution.py:80
  65.6 7.5 %all-to-all-start = ((f32[8,16,64,256]{3,2,1,0:T(8,128)}), f32[8,16,64,256]{3,2,1,0:T(8,128)}, u32[]{:S(2)}, u32[]{:S(2)}) async-start(f32[8,16,64,256]{3,2,1,0:T(8,128)} %bitcast.58), calls=%async_computation | async-start | bytes 16777216 | tf_op jit(solution)/shard_map/all_to_all | solution.py:81
  73.4 182.8 %all-to-all-done = f32[8,16,64,256]{3,2,1,0:T(8,128)} async-done(((f32[8,16,64,256]{3,2,1,0:T(8,128)}), f32[8,16,64,256]{3,2,1,0:T(8,128)}, u32[]{:S(2)}, u32[]{:S(2)}) %all-to-all-start) | async-done | bytes 8388640 | tf_op jit(solution)/shard_map/all_to_all | solution.py:81
  256.2 10.8 %reshape.89 = f32[128,64,2,128]{3,2,1,0:T(2,128)} reshape(f32[8,16,64,256]{3,2,1,0:T(8,128)} %all-to-all-done) | data formatting | bytes 16777216 | tf_op jit(solution)/shard_map/reshape | solution.py:84
  267.0 7.1 %broadcast_multiply_fusion = f32[128,64,2,128]{3,2,1,0:T(2,128)S(1)} fusion(f32[128,64,2,128]{3,2,1,0:T(2,128)} %reshape.89, f32[64]{0:T(128)S(1)} %convert_bitcast_fusion), kind=kLoop, calls=%fused_computation.15 | loop fusion | flops 2097152 | bytes 16777472 | tf_op jit(solution)/shard_map/mul | solution.py:86
  274.1 9.8 %slice_negate_fusion = (f32[128,64,1,128]{3,2,1,0:T(1,128)}, f32[128,64,1,128]{3,2,1,0:T(1,128)}) fusion(f32[128,64,2,128]{3,2,1,0:T(2,128)S(1)} %broadcast_multiply_fusion), kind=kLoop, calls=%fused_computation.17 | loop fusion | flops 1048576 | bytes 16777216 | tf_op jit(solution)/shard_map/neg | solution.py:60
  283.8 10.8 %reshape.88 = f32[128,64,1,2,128]{4,3,1,0,2:T(2,128)} reshape(f32[8,16,64,256]{3,2,1,0:T(8,128)} %all-to-all-done) | data formatting | bytes 16777216 | tf_op jit(solution)/shard_map/reshape | solution.py:84
  294.6 8.3 %broadcast_multiply_fusion.1 = f32[128,64,1,2,128]{4,3,1,0,2:T(2,128)S(1)} fusion(f32[128,64,1,2,128]{4,3,1,0,2:T(2,128)} %reshape.88, f32[64]{0:T(128)S(1)} %convert_bitcast_fusion), kind=kLoop, calls=%fused_computation.16 | loop fusion | flops 2097152 | bytes 16777472 | tf_op jit(solution)/shard_map/mul | solution.py:86
  302.9 7.7 %maximum_bitcast_fusion = f32[128,64,1,2,128]{4,3,1,0,2:T(2,128)S(1)} fusion(f32[128,64,1,128]{3,2,1,0:T(1,128)S(1)} %copy-done.1, f32[128,64,1,128]{3,2,1,0:T(1,128)S(1)} %copy-done), kind=kLoop, calls=%fused_computation.12 | loop fusion | flops 2097152 | bytes 16777216 | tf_op jit(solution)/shard_map/stack | solution.py:61
  310.7 9.5 %pad_maximum_fusion = f32[128,64,2,2,128]{4,3,1,0,2:T(2,128)} fusion(f32[128,64,1,2,128]{4,3,1,0,2:T(2,128)S(1)} %maximum_bitcast_fusion, f32[128,64,1,2,128]{4,3,1,0,2:T(2,128)S(1)} %broadcast_multiply_fusion.1), kind=kLoop, calls=%fused_computation.6 | loop fusion | flops 4194304 | bytes 33554432 | tf_op jit(solution)/shard_map/stack | solution.py:61
  320.2 20.9 %copy.13 = f32[128,64,2,2,128]{0,1,3,2,4:T(8,128)} copy(f32[128,64,2,2,128]{4,3,1,0,2:T(2,128)} %pad_maximum_fusion) | data formatting | bytes 33554432 | tf_op jit(solution)/shard_map/while | solution.py:98
  341.1 8.3 %bitcast_multiply_fusion = f32[128,64,256]{2,1,0:T(8,128)} fusion(f32[8,16,64,256]{3,2,1,0:T(8,128)} %all-to-all-done, f32[64]{0:T(128)S(1)} %convert_bitcast_fusion), kind=kLoop, calls=%fused_computation.13 | loop fusion | flops 2097152 | bytes 16777472 | tf_op jit(solution)/shard_map/mul | solution.py:86
  349.4 111.1 %while.10 = (s32[]{:T(128)}, f32[2,64,65,128]{3,1,0,2:T(8,128)}, s32[2]{0:T(128)S(1)}, f32[128,64,256]{2,1,0:T(8,128)}, f32[128,64,2,2,128]{0,1,3,2,4:T(8,128)},...) while((s32[]{:T(128)}, f32[2,64,65,128]{3,1,0,2:T(8,128)}, ...), condition=%wide.region_6.7_spmd, body=%wide.region_5.6_spmd.sunk | while | flops 4857004032 | bytes 116196592 | solution.py:98
  367.1 5.8 %reshape.104 = f32[64,64,2,128]{3,2,1,0:T(2,128)} reshape(f32[64,64,256]{2,1,0:T(8,128)} %constant_dynamic-slice_fusion.2) | data formatting | bytes 8388608 | tf_op jit(solution)/shard_map/while/body/eval_jaxpr/reshape | solution.py:66
  372.8 8.7 %copy.29 = f32[64,64,2,128,1]{1,0,2,4,3:T(8,128)} copy(f32[64,64,2,128,1]{3,2,1,0,4:T(2,128)} %bitcast.57) | data formatting | bytes 8388608 | tf_op jit(solution)/shard_map/while/body/eval_jaxpr/reshape | solution.py:66
  381.6 16.1 %convolution_bitcast_fusion.5 = f32[64,2,128,128]{3,0,1,2:T(8,128)S(1)} fusion(f32[64,64,2,128,1]{1,0,2,4,3:T(8,128)} %copy.29, f32[128,64,2,2,128]{0,1,3,2,4:T(8,128)} %get-tuple-element.129), kind=kOutput, calls=%fused_computation.1.clone.1 | convolution fusion | flops 3221225472 | bytes 29360128 | tf_op jit(solution)/shard_map/while/body/eval_jaxpr/icpk,jcqpk->iqkj/dot_general | solution.py:67
  416.7 5.8 %reshape.104 = f32[64,64,2,128]{3,2,1,0:T(2,128)} reshape(f32[64,64,256]{2,1,0:T(8,128)} %constant_dynamic-slice_fusion.2) | data formatting | bytes 8388608 | tf_op jit(solution)/shard_map/while/body/eval_jaxpr/reshape | solution.py:66
  422.5 8.7 %copy.29 = f32[64,64,2,128,1]{1,0,2,4,3:T(8,128)} copy(f32[64,64,2,128,1]{3,2,1,0,4:T(2,128)} %bitcast.57) | data formatting | bytes 8388608 | tf_op jit(solution)/shard_map/while/body/eval_jaxpr/reshape | solution.py:66
  431.2 16.1 %convolution_bitcast_fusion.5 = f32[64,2,128,128]{3,0,1,2:T(8,128)S(1)} fusion(f32[64,64,2,128,1]{1,0,2,4,3:T(8,128)} %copy.29, f32[128,64,2,2,128]{0,1,3,2,4:T(8,128)} %get-tuple-element.129), kind=kOutput, calls=%fused_computation.1.clone.1 | convolution fusion | flops 3221225472 | bytes 29360128 | tf_op jit(solution)/shard_map/while/body/eval_jaxpr/icpk,jcqpk->iqkj/dot_general | solution.py:67
  465.1 5.6 %psum.7 = f32[128]{0:T(128)S(1)} all-reduce(f32[128]{0:T(128)S(1)} %reduce_sum.42), channel_id=1, replica_groups=mesh['chan'=4,'fam'=8] {'chan'}, use_global_device_ids=true, to_apply=%region_9.10 | all-reduce | flops 128 | bytes 1024 | tf_op jit(solution)/shard_map/psum | solution.py:88
  470.9 33.8 %reduce-scatter.2.cloned.1.call-done = f32[32,65,128]{2,0,1:T(8,128)} async-done(((f32[128,65,128]{2,0,1:T(8,128)}), f32[32,65,128]{2,0,1:T(8,128)}) %reduce-scatter.2.cloned.1.call-update) | async-done | bytes 1064976 | tf_op jit(solution)/shard_map/reduce_scatter | solution.py:101
  (54 shorter events, 56.3 us)
Async XLA Ops:
  65.6 7.8 %copy-start.3 = (s32[1,64]{1,0:T(1,128)S(1)}, s32[1,64]{1,0:T(1,128)}, u32[]{:S(2)}) copy-start(s32[1,64]{1,0:T(1,128)} %param.7) | copy-start | bytes 772
  65.6 190.6 %all-to-all-start = ((f32[8,16,64,256]{3,2,1,0:T(8,128)}), f32[8,16,64,256]{3,2,1,0:T(8,128)}, u32[]{:S(2)}, u32[]{:S(2)}) async-start(f32[8,16,64,256]{3,2,1,0:T(8,128)} %bitcast.58), calls=%async_computation | async-start | bytes 16777216 | tf_op jit(solution)/shard_map/all_to_all | solution.py:81
  73.1 431.7 %reduce-scatter.2.cloned.1.call-start = ((), (), s32[]{:S(2)}) async-start(), calls=%async_computation.2 | async-start | bytes 5324800 | tf_op jit(solution)/shard_map/reduce_scatter | solution.py:101
  294.6 8.3 %copy-start = (f32[128,64,1,128]{3,2,1,0:T(1,128)S(1)}, f32[128,64,1,128]{3,2,1,0:T(1,128)}, u32[]{:S(2)}) copy-start(f32[128,64,1,128]{3,2,1,0:T(1,128)} %get-tuple-element.62) | copy-start | bytes 12582916
  294.6 8.3 %copy-start.1 = (f32[128,64,1,128]{3,2,1,0:T(1,128)S(1)}, f32[128,64,1,128]{3,2,1,0:T(1,128)}, u32[]{:S(2)}) copy-start(f32[128,64,1,128]{3,2,1,0:T(1,128)} %get-tuple-element.63) | copy-start | bytes 12582916
  402.5 5.6 %slice-start = ((s8[4259840]{0:T(1024)(128)(4,1)}), s8[4194304]{0:T(1024)(128)(4,1)S(1)}, s32[]{:S(2)}) async-start(s8[4259840]{0:T(1024)(128)(4,1)} %bitcast.60), calls=%async_computation.3 | async-start | bytes 8388608 | tf_op jit(solution)/shard_map/while
  402.5 5.6 %slice-start.1 = ((s8[4259840]{0:T(1024)(128)(4,1)}), s8[65536]{0:T(1024)(128)(4,1)S(1)}, s32[]{:S(2)}) async-start(s8[4259840]{0:T(1024)(128)(4,1)} %bitcast.60), calls=%async_computation.4 | async-start | bytes 131072 | tf_op jit(solution)/shard_map/while
  408.9 1.9 copy-start.2
  452.2 5.6 %slice-start = ((s8[4259840]{0:T(1024)(128)(4,1)}), s8[4194304]{0:T(1024)(128)(4,1)S(1)}, s32[]{:S(2)}) async-start(s8[4259840]{0:T(1024)(128)(4,1)} %bitcast.60), calls=%async_computation.3 | async-start | bytes 8388608 | tf_op jit(solution)/shard_map/while
  452.2 5.6 %slice-start.1 = ((s8[4259840]{0:T(1024)(128)(4,1)}), s8[65536]{0:T(1024)(128)(4,1)S(1)}, s32[]{:S(2)}) async-start(s8[4259840]{0:T(1024)(128)(4,1)} %bitcast.60), calls=%async_computation.4 | async-start | bytes 131072 | tf_op jit(solution)/shard_map/while
  458.6 1.9 copy-start.2
Sparse Core Ops, SparseCore 0:
  460.7 44.0 reduce-scatter.1
where the time goes:
time: 519 us; the launch traced here: 514 us
  waiting for transfers between devices  217 us (42%)
  local copies, waits for them, and re-layouts  134 us (26%)
  other arithmetic  65.7 us (13%)
  matrix products  57.8 us (11%)
  between operations  13.7 us (3%)
  loops' own time  13.2 us (3%)
  starting transfers between devices  7.5 us (1%)
  blocking collectives  5.64 us (1%)
    all_to_all x1, waiting for transfers between devices, local(): lax.all_to_all(outbox.reshape((owners, CAP) + trailing), 'fam', split_axi...  183 us
    reduce_scatter x1, waiting for transfers between devices, local(): lax.psum_scatter(blocks_out.reshape((rows * lax.axis_size('chan'),) + blo...  33.8 us
    dot_general x2, matrix products, pair_terms(): cross = jnp.einsum('icpk,jcqpk->iqkj', left, both, precision=HIGH)  32.2 us
    reshape x4, local copies, waits for them, and re-layouts, pair_terms(): left = rows.reshape(rows.shape[0], rows.shape[1], 2, bins)  29 us
    mul x3, other arithmetic, local(): member = spectra * mask[None, :, None]  23.7 us
    scatter x1, local copies, waits for them, and re-layouts, local(): jnp.zeros((owners * CAP,) + trailing, jnp.float32).at[target].set(white)  23.2 us
    reshape x2, local copies, waits for them, and re-layouts, local(): spectra = inbox.reshape((owners * CAP,) + trailing)  21.5 us
    while x1, local copies, waits for them, and re-layouts, local(): lax.map(one_block, jnp.arange(rows * lax.axis_size('chan') // block, dtyp...  20.9 us
  transfers between devices with their start and end apart: 2, of which 2 were waited for; matrix products, arithmetic and copies ran while one was open for 1% of the time, Pallas kernels for 0%

commit v1 on v0

v1 whole, which is shorter than its diff:
```python
import functools
import math

import jax
import jax.numpy as jnp
import numpy as np
from jax import lax
from jax.experimental import pallas as pl
from jax.experimental.pallas import tpu as pltpu
from jax.sharding import PartitionSpec as P

MAXLAG = 32
CAP = 16
LANES = 128
F16_SCALE = 16384.0
TINY = 1.2e-38
VMEM_LIMIT = 56 * 2**20
PITCH_PAD = 8
LONG = pl.CostEstimate(flops=10**14, bytes_accessed=1, transcendentals=0)
SHORT = pl.CostEstimate(flops=1, bytes_accessed=1, transcendentals=0)
FINISH_LIMIT = 40 * 2**20
F32 = jnp.float32
BF16 = jnp.bfloat16
IN_VMEM = pl.BlockSpec(memory_space=pltpu.VMEM)
IN_SMEM = pl.BlockSpec(memory_space=pltpu.SMEM)
IN_HBM = pl.BlockSpec(memory_space=pltpu.HBM)


def split(x):
    high = x.astype(BF16)
    return high, (x - high.astype(F32)).astype(BF16)


def split_table(table):
    high = table.astype(np.float32).astype(BF16)
    return high, (table - high.astype(np.float64)).astype(np.float32).astype(BF16)


def dot(a, b):
    return lax.dot_general(a, b, (((1,), (0,)), ((), ())), preferred_element_type=F32)


def dot_rows(a, b):
    return lax.dot_general(a, b, (((1,), (1,)), ((), ())), preferred_element_type=F32)


def transform_table(length):
    bins = length // 2
    angle = (np.arange(bins)[:, None] * np.arange(length)[None, :] % length) * (2.0 * math.pi / length)
    return np.concatenate(split_table(np.concatenate([np.cos(angle), -np.sin(angle)], axis=0)), axis=0)


def lag_rows():
    return (2 * MAXLAG + 1 + 7) // 8 * 8


def lag_table(length):
    bins = length // 2
    rows = lag_rows()
    shifts = np.arange(rows) - MAXLAG
    angle = (shifts[:, None] * np.arange(bins)[None, :] % length) * (2.0 * math.pi / length)
    table = np.concatenate([np.cos(angle), -np.sin(angle)], axis=1)
    high, low = split_table(table * (shifts <= MAXLAG)[:, None])
    return np.concatenate([high, low], axis=0)


def gather_kernel(owners, dests, me_ref, family_ref, wave_ref, *rest):
    outs = dict(zip(dests, rest[-5 - len(dests) : -5]))
    count, zero, buf, arrived, sent = rest[-5:]
    index = {d: n for n, d in enumerate(dests)}
    me = me_ref[0]
    zero[...] = jnp.zeros_like(zero)
    for f in range(owners):
        count[f] = 0

    def place(e, carry):
        f = family_ref[e]
        r = count[f]
        count[f] = r + 1
        d = jnp.bitwise_xor(f, me)
        spot = jnp.where(r < CAP // 2, 2 * r, 2 * r - CAP + 1)
        slot = d - dests[0]

        @pl.when((d >= dests[0]) & (d <= dests[-1]))
        def _():
            pltpu.make_async_copy(wave_ref.at[e], buf.at[slot, spot], arrived.at[slot]).start()

        return carry

    lax.fori_loop(0, family_ref.shape[0], place, 0, unroll=4)
    for d in dests:

        def fill(r, carry):
            spot = jnp.where(r < CAP // 2, 2 * r, 2 * r - CAP + 1)
            pltpu.make_async_copy(zero, buf.at[index[d], spot], arrived.at[index[d]]).start()
            return carry

        lax.fori_loop(count[jnp.bitwise_xor(me, d)], CAP, fill, 0)
    for d in dests:
        n = index[d]
        pltpu.make_async_copy(buf.at[n], buf.at[n], arrived.at[n]).wait()
        pltpu.make_async_copy(buf.at[n], outs[d], sent.at[n]).start()
    for d in dests:
        n = index[d]
        pltpu.make_async_copy(buf.at[n], outs[d], sent.at[n]).wait()


def gather(me, family_of, waveforms, owners, dests, after):
    shape = (CAP,) + waveforms.shape[1:]
    count = len(dests)
    return pl.pallas_call(
        functools.partial(gather_kernel, owners, dests),
        out_shape=[jax.ShapeDtypeStruct(shape, waveforms.dtype)] * count,
        in_specs=[IN_SMEM, IN_SMEM, IN_HBM] + [IN_HBM] * len(after),
        out_specs=[IN_HBM] * count,
        scratch_shapes=[
            pltpu.SMEM((owners,), jnp.int32),
            pltpu.VMEM(waveforms.shape[1:], waveforms.dtype),
            pltpu.VMEM((count,) + shape, waveforms.dtype),
            pltpu.SemaphoreType.DMA((count,)),
            pltpu.SemaphoreType.DMA((count,)),
        ],
        cost_estimate=SHORT,
        compiler_params=pltpu.CompilerParams(vmem_limit_bytes=VMEM_LIMIT),
        name="gather_slots",
    )(me, family_of, waveforms, *after)


def spot_of(event):
    return event % 2 * (CAP // 2) + event // 2


def code_of(tile):
    exponent = jnp.floor(jnp.log2(jnp.maximum(tile, TINY)))
    mantissa = tile * jnp.exp2(-exponent)
    high = mantissa.astype(BF16).astype(F32)
    return high, mantissa - high, exponent * (1.0 / 64.0)


def whiten_body(x_ref, table_ref, mask_ref, scratch, write):
    events, chans, length = x_ref.shape
    bins = length // 2
    cols = 2 * LANES
    step = cols // chans
    groups = events * chans // LANES
    row = lax.broadcasted_iota(jnp.int32, (bins, cols), 0)
    col = lax.broadcasted_iota(jnp.int32, (bins, cols), 1)
    near = (jnp.abs(row - jnp.bitwise_and(col, bins - 1)) <= 4).astype(F32).astype(BF16)
    count = jnp.minimum(row + 4, bins - 1) - jnp.maximum(row - 4, 0) + 1
    inverse = 1.0 / count.astype(F32)
    row = lax.broadcasted_iota(jnp.int32, (cols, cols), 0) // chans
    col = lax.broadcasted_iota(jnp.int32, (cols, cols), 1) // chans
    same = (row == col).astype(F32).astype(BF16)
    lane = jnp.bitwise_and(lax.broadcasted_iota(jnp.int32, (8, LANES), 1), CAP - 1)
    tile = jnp.zeros((8, LANES), F32)
    for n in range(events // step):
        x = x_ref[n * step : (n + 1) * step].reshape(cols, length)
        spec = dot_rows(table_ref[:length], x) + dot_rows(table_ref[length:], x)
        re = spec[:bins]
        im = spec[bins:]
        power = re * re + im * im
        high, low = split(power)
        smooth = dot(near, jnp.concatenate([high, low], axis=0))
        level = jnp.sum(power, axis=0, keepdims=True) * (0.1 / bins) + 1e-5
        scale = lax.rsqrt(smooth * inverse + level) * mask_ref[...]
        lane_energy = jnp.sum(power * (scale * scale), axis=0, keepdims=True)
        high, low = split(lane_energy)
        rest = (lane_energy - high.astype(F32) - low.astype(F32)).astype(BF16)
        parts = jnp.concatenate([high, low, rest] + [jnp.zeros_like(high)] * 13, axis=0)
        energy = jnp.sum(dot(parts, same), axis=0, keepdims=True)
        for e in range(step):
            value = jnp.broadcast_to(energy[:, e * chans : e * chans + 1], (8, LANES))
            tile = jnp.where(lane == spot_of(n * step + e), value, tile)
        unit = jnp.where(energy > TINY, lax.rsqrt(jnp.maximum(energy, TINY)), 0.0)
        factor = scale * unit
        re = re * factor
        im = im * factor
        for h in range(2):
            g = 2 * n + h
            scratch[g * bins : (g + 1) * bins] = re[:, h * LANES : (h + 1) * LANES]
            scratch[(groups + g) * bins : (groups + g + 1) * bins] = im[:, h * LANES : (h + 1) * LANES]
    first = lax.broadcasted_iota(jnp.int32, (groups, LANES), 1) < LANES // 2

    def relayout(k, carry):
        re = scratch[pl.ds(k, groups, stride=bins), :]
        im = scratch[pl.ds(groups * bins + k, groups, stride=bins), :]
        re_rolled = pltpu.roll(re, LANES // 2, 1)
        im_rolled = pltpu.roll(im, LANES // 2, 1)
        member = jnp.concatenate([jnp.where(first, re, im_rolled), jnp.where(first, re_rolled, im)], axis=0)
        write(k, *split(member))
        return carry

    lax.fori_loop(0, bins, relayout, 0, unroll=16)
    return tile


def whiten_kernel(count, table_hbm, mask_ref, *refs):
    x_hbm = refs[:count]
    m_hbm, e_ref = refs[-7 - 2 * count : -7 - count], refs[-7 - count : -7]
    x_ref, table_ref, m_ref, scratch, sem, x_sem, out_sem = refs[-7:]
    load = pltpu.make_async_copy(table_hbm, table_ref, sem)
    load.start()
    loads = [pltpu.make_async_copy(x_hbm[n], x_ref.at[n], x_sem.at[n]) for n in range(count)]
    for c in loads:
        c.start()
    load.wait()
    outs = []
    for n in range(count):
        loads[n].wait()

        def write(k, high, low):
            m_ref[n, k, :, :LANES] = high
            m_ref[n, k, :, LANES:] = low

        e_ref[n][...] = whiten_body(x_ref.at[n], table_ref, mask_ref, scratch.at[n % 2], write)
        outs.append(pltpu.make_async_copy(m_ref.at[n], m_hbm[n], out_sem.at[n]))
        outs[-1].start()
    for c in outs:
        c.wait()


def member_shapes(x):
    events, chans, length = x.shape
    bins = length // 2
    m = jax.ShapeDtypeStruct((bins, events, 2 * LANES), BF16)
    return m, (2 * events * chans // LANES * bins, LANES)


ENERGY = jax.ShapeDtypeStruct((8, LANES), F32)


def whiten(xs, table, mask, after):
    count = len(xs)
    m, scratch = member_shapes(xs[0])
    out = pl.pallas_call(
        functools.partial(whiten_kernel, count),
        out_shape=[m] * count + [ENERGY] * count,
        in_specs=[IN_HBM, IN_VMEM] + [IN_HBM] * (count + len(after)),
        out_specs=[IN_HBM] * count + [IN_VMEM] * count,
        scratch_shapes=[
            pltpu.VMEM((count,) + xs[0].shape, xs[0].dtype),
            pltpu.VMEM(table.shape, table.dtype),
            pltpu.VMEM((count,) + m.shape, m.dtype),
            pltpu.VMEM((2,) + scratch, F32),
            pltpu.SemaphoreType.DMA,
            pltpu.SemaphoreType.DMA((count,)),
            pltpu.SemaphoreType.DMA((count,)),
        ],
        cost_estimate=SHORT,
        compiler_params=pltpu.CompilerParams(vmem_limit_bytes=VMEM_LIMIT),
        name="whiten",
    )(table, mask, *xs, *after)
    return out[:count], out[count:]


def turn(m):
    half = LANES // 2
    return jnp.concatenate([m[:, half:LANES], -m[:, :half]], axis=1)


def pairs_body(me, new, members, table_ref, cross_ref, emit):
    bins, slots, _ = members.shape
    tiles = slots // LANES
    taus = table_ref.shape[0] // 2
    n = len(new) * CAP
    pitch = 2 * bins + PITCH_PAD

    def cross(k, carry):
        both = members[k]
        left = [members[k, pl.ds(place(me, d), CAP), :] for d in new]
        left = jnp.concatenate(left, axis=0)
        high = left[:, :LANES]
        low = left[:, LANES:]
        left = jnp.concatenate([high, turn(high), low, turn(low)], axis=0)
        right = jnp.concatenate([both[:, :LANES], both[:, LANES:]], axis=0)
        out = dot_rows(left, right)
        total = out[: 2 * n, :slots] + (out[: 2 * n, slots:] + out[2 * n :, :slots])
        for q in range(2):
            for t in range(tiles):
                part = total[q * n : (q + 1) * n, t * LANES : (t + 1) * LANES]
                cross_ref[t, pl.ds(q * bins + k, n, stride=pitch), :] = part
        return carry

    lax.fori_loop(0, bins, cross, 0, unroll=16 if n <= 32 else 8)
    table = table_ref[...]

    def lag(i, carry):
        for t in range(tiles):
            pair = cross_ref[t, pl.ds(pl.multiple_of(2 * i * pitch, 8), 2 * pitch), :]
            pair = jnp.concatenate([pair[: 2 * bins], pair[pitch : pitch + 2 * bins]], axis=1)
            high, low = split(pair)
            out = dot(table, high)
            out = out[:taus] + (out[taus:] + dot(table[:taus], low))
            for h in range(2):
                emit(2 * i + h, t, out[:, h * LANES : (h + 1) * LANES])
        return carry

    lax.fori_loop(0, n // 2, lag, 0, unroll=4)


def turn_lines(lines, codes, chan, turned, taus):
    tiles = lines.shape[0] // (CAP * taus)
    groups, parts = turned.shape[0], taus // 8
    rows = turned.shape[1] // parts
    for g in range(parts):
        for t in range(tiles):
            pieces = []
            for u in range(7, -1, -1):
                tau = 2 * MAXLAG - 8 * g - u
                if tau >= 0:
                    pieces.append(lines[pl.ds(t * CAP * taus + tau, CAP, stride=taus), :])
                else:
                    pieces.append(codes[min(-tau, len(codes)) - 1])
            value = jnp.concatenate(pieces, axis=0).T
            for c in range(LANES // rows):
                target = jnp.bitwise_xor(chan, t * (LANES // rows) + c)
                turned[target, g * rows : (g + 1) * rows] = value[c * rows : (c + 1) * rows]


def place(me, d):
    return pl.multiple_of(jnp.bitwise_xor(me, d) * CAP, CAP)


def load_members(me, ms, old, members, sem):
    copies = [
        pltpu.make_async_copy(ms[i], members.at[:, pl.ds(place(me, d), CAP), :], sem.at[i]) for i, d in enumerate(old)
    ]
    for c in copies:
        c.start()
    return copies


def slot_vector(me, tiles, slots):
    lane = lax.broadcasted_iota(jnp.int32, (8, slots), 1) // CAP
    value = jnp.zeros((8, slots), F32)
    for d, tile in tiles.items():
        value = jnp.where(lane == jnp.bitwise_xor(me, d), jnp.concatenate([tile] * (slots // LANES), axis=1), value)
    return value


def as_rows(value, ref):
    for t in range(value.shape[1] // LANES):
        part = jnp.broadcast_to(value[0:1, t * LANES : (t + 1) * LANES], (LANES, LANES))
        ref[t * LANES : (t + 1) * LANES] = part.T


def whiten_and_load(new, old, me, x_hbm, ms, tables, buffers, sems, keep):
    table_hbm, mask_ref = tables
    x_ref, table_ref, scratch, members = buffers
    load, x_sem, sem = sems
    table_load = pltpu.make_async_copy(table_hbm, table_ref, load)
    table_load.start()
    loads = [pltpu.make_async_copy(x_hbm[n], x_ref.at[n], x_sem.at[n]) for n in range(len(new))]
    for c in loads:
        c.start()
    copies = load_members(me, ms, old, members, sem)
    table_load.wait()
    tiles = {}
    for n, d in enumerate(new):
        where = place(me, d)
        loads[n].wait()

        def write(k, high, low):
            members[k, pl.ds(where, CAP), :LANES] = high
            members[k, pl.ds(where, CAP), LANES:] = low

        tiles[d] = whiten_body(x_ref.at[n], table_ref, mask_ref, scratch.at[n % 2], write)
        keep(n, members.at[:, pl.ds(where, CAP), :])
    for c in copies:
        c.wait()
    return tiles


def shared_scratch(x, new, old, table, slots, n):
    m, scratch = member_shapes(x)
    bins = m.shape[0]
    return [
        pltpu.VMEM((len(new),) + x.shape, x.dtype),
        pltpu.VMEM(table.shape, table.dtype),
        pltpu.VMEM((min(2, len(new)),) + scratch, F32),
        pltpu.VMEM((bins, slots, 2 * LANES), BF16),
        pltpu.VMEM((slots // LANES, n * (2 * bins + PITCH_PAD), LANES), F32),
        pltpu.SemaphoreType.DMA,
        pltpu.SemaphoreType.DMA((len(new),)),
        pltpu.SemaphoreType.DMA((len(old),)),
        pltpu.SemaphoreType.DMA((24,)),
    ]


def square_kernel(old, new, lines_of, more, me_ref, table_hbm, mask_ref, lag_ref, *refs):
    count = len(new)
    x_hbm, refs = refs[:count], refs[count:]
    ms, refs = refs[: len(old)], refs[len(old) :]
    given, refs = refs[: len(old)], refs[len(old) :]
    x_ref, table_ref, scratch, members, cross_ref, load, x_sem, sem, out_sem, rows_ref = refs[-10:]
    outs = refs[-10 - 1 - count * (1 + more) : -10]
    me, own = me_ref[0], me_ref[2]
    slots = members.shape[1]
    done = []

    def keep(n, block):
        if more:
            done.append(pltpu.make_async_copy(block, outs[1 + count + n], out_sem.at[8 + n]))
            done[-1].start()

    buffers = (x_ref, table_ref, scratch, members)
    tiles = whiten_and_load(new, old, me, x_hbm, ms, (table_hbm, mask_ref), buffers, (load, x_sem, sem), keep)
    for n, d in enumerate(new):
        outs[1 + n][...] = tiles[d]
    for d, ref in zip(old, given):
        tiles[d] = ref[...]
    codes = code_of(slot_vector(me, tiles, slots))

    def emit(row, t, part):
        rows_ref[row, :, t * LANES : (t + 1) * LANES] = part

    pairs_body(me, lines_of, members, lag_ref, cross_ref, emit)
    groups, rows = outs[0].shape[:2]
    first = lines_of[0] * CAP // rows
    for n in range(rows_ref.shape[0] // rows):
        for c, code in enumerate(codes):
            rows_ref[n * rows, 2 * MAXLAG + 1 + c : 2 * MAXLAG + 2 + c] = code[0:1]
        target = jnp.bitwise_xor(first + n, own)
        done.append(pltpu.make_async_copy(rows_ref.at[n * rows : (n + 1) * rows], outs[0].at[target], out_sem.at[n]))
        done[-1].start()
    if first + rows_ref.shape[0] // rows == groups - 1:
        target = jnp.bitwise_xor(groups - 1, own)
        done.append(pltpu.make_async_copy(rows_ref.at[:rows], outs[0].at[target], out_sem.at[groups - 1]))
        done[-1].start()
    for c in done:
        c.wait()


def square(me, xs, table, mask, lags, ms, energy, lines_of, slots, groups, more, after, filled):
    old, new = sorted(ms), sorted(xs)
    taus = lags.shape[0] // 2
    x = xs[new[0]]
    m, _ = member_shapes(x)
    n = len(lines_of) * CAP
    rows = jax.ShapeDtypeStruct((groups, slots // groups, taus, slots), F32)
    return pl.pallas_call(
        functools.partial(square_kernel, old, new, lines_of, more),
        out_shape=[rows] + [ENERGY] * len(new) + [m] * (more * len(new)),
        in_specs=[IN_SMEM, IN_HBM, IN_VMEM, IN_VMEM]
        + [IN_HBM] * (len(new) + len(old))
        + [IN_VMEM] * len(old)
        + [IN_HBM] * (len(after) + len(filled)),
        out_specs=[IN_HBM] + [IN_VMEM] * len(new) + [IN_HBM] * (more * len(new)),
        scratch_shapes=shared_scratch(x, new, old, table, slots, n)
        + [pltpu.VMEM((n, taus, slots), F32)],
        cost_estimate=SHORT,
        compiler_params=pltpu.CompilerParams(vmem_limit_bytes=VMEM_LIMIT),
        input_output_aliases={4 + len(new) + 2 * len(old) + len(after): 0} if filled else {},
        name="square",
    )(me, table, mask, lags, *[xs[d] for d in new], *[ms[d] for d in old], *[energy[d] for d in old], *after, *filled)


def step_kernel(old, new, final, me_ref, table_hbm, mask_ref, lag_ref, x_hbm, *refs):
    ms, refs = refs[: len(old)], refs[len(old) :]
    lines, turned_ref = refs[-2:]
    x_ref, table_ref, scratch, members, cross_ref, load, x_sem, sem, out_sem = refs[-11:-2]
    outs = refs[-11 - (2 if final else 4) : -11]
    me, chan = me_ref[0], me_ref[1]
    slots = members.shape[1]
    taus = lag_ref.shape[0] // 2
    done = []

    def start(source, target):
        done.append(pltpu.make_async_copy(source, target, out_sem.at[len(done)]))
        done[-1].start()

    def keep(n, block):
        if not final:
            start(block, outs[2])

    full_lines, full_turned = lines, turned_ref
    if final:
        kept_lines, kept_turned = refs[:2]
        cut, turned_cut = kept_lines.shape[0], kept_turned.shape[1]
        start(kept_lines, lines.at[:cut])
        start(kept_turned, turned_ref.at[:, :turned_cut])
        lines, turned_ref = lines.at[cut:], turned_ref.at[:, turned_cut:]
    buffers = (x_ref, table_ref, scratch, members)
    tiles = whiten_and_load([new], old, me, [x_hbm], ms, (table_hbm, mask_ref), buffers, (load, x_sem, sem), keep)
    tile = tiles[new]
    column = jnp.broadcast_to(tile[0:1], (LANES, LANES)).T[:CAP]

    def emit(row, t, part):
        lines[pl.ds(pl.multiple_of((t * CAP + row) * taus, 8), taus), :] = part

    pairs_body(me, [new], members, lag_ref, cross_ref, emit)
    if final:
        for c in done:
            c.wait()
    else:
        outs[3][...] = tile
    start(full_lines, outs[0])
    turn_lines(lines, code_of(column), chan, turned_ref, taus)
    start(full_turned, outs[1])
    for c in done[2:] if final else done:
        c.wait()


def step(me, x, table, mask, lags, ms, new, slots, groups, kept, after):
    old = sorted(ms)
    taus = lags.shape[0] // 2
    m, _ = member_shapes(x)
    final = len(kept) > 0
    count = 1 + (kept[0].shape[0] // (slots // LANES * CAP * taus) if final else 0)
    lines = jax.ShapeDtypeStruct((count * (slots // LANES) * CAP * taus, LANES), F32)
    turned = jax.ShapeDtypeStruct((groups, count * (taus // 8) * (slots // groups), LANES), F32)
    return pl.pallas_call(
        functools.partial(step_kernel, old, new, final),
        out_shape=[lines, turned] + ([] if final else [m, ENERGY]),
        in_specs=[IN_SMEM, IN_HBM, IN_VMEM, IN_VMEM] + [IN_HBM] * (1 + len(old) + len(kept) + len(after)),
        out_specs=[IN_HBM] * 2 + ([] if final else [IN_HBM, IN_VMEM]),
        scratch_shapes=shared_scratch(x, [new], old, table, slots, CAP)
        + [pltpu.VMEM(lines.shape, F32), pltpu.VMEM(turned.shape, F32)],
        cost_estimate=LONG if final else SHORT,
        compiler_params=pltpu.CompilerParams(vmem_limit_bytes=VMEM_LIMIT),
        name="step",
    )(me, table, mask, lags, x, *[ms[d] for d in old], *kept, *after)


def hold_kernel(*refs):
    del refs


def hold(xs, after):
    n = len(xs)
    return pl.pallas_call(
        hold_kernel,
        out_shape=[jax.ShapeDtypeStruct(x.shape, x.dtype) for x in xs],
        in_specs=[IN_HBM] * (n + len(after)),
        out_specs=[IN_HBM] * n,
        input_output_aliases={i: i for i in range(n)},
        cost_estimate=SHORT,
        name="hold",
    )(*xs, *after)


def finish_kernel(last, blocks, me_ref, *refs):
    out_hbm, out_ref, lines_sum, rows_ref, sem = refs[-5:]
    me, chan, own = me_ref[0], me_ref[1], me_ref[2]
    rows, lags, slots = out_ref.shape
    tiles = slots // LANES
    groups = slots // rows
    taus = lag_rows()
    parts = taus // 8
    base, late, turned = refs[:groups], refs[groups : 2 * groups], refs[2 * groups : 3 * groups]
    scale = [1.0] + [1.0 / F16_SCALE] * (groups - 1)
    lane = lax.broadcasted_iota(jnp.int32, (8, LANES), 1)

    def spread(line, v):
        part = jnp.where(lane < CAP, pltpu.roll(line, LANES - v * CAP, 1), 0.0)
        for shift in (CAP, 2 * CAP, 4 * CAP):
            part = part + pltpu.roll(part, shift, 1)
        return part

    def energy_of(high, low, exponent, e):
        return (high + low) * scale[e] * jnp.exp2(jnp.round(exponent * (64.0 * scale[e])))

    block_of = lax.broadcasted_iota(jnp.int32, (8, slots), 1) // CAP
    every, local = [], []
    for e in range(groups):
        local.append({})
        for n, d in enumerate(last):
            start = (n * parts + parts - 1) * rows
            line = turned[e][start : start + 8]
            local[e][d] = energy_of(spread(line, 6), spread(line, 5), spread(line, 4), e)
        codes = base[e][0, taus - 8 : taus]
        vector = jnp.broadcast_to(energy_of(codes[1:2], codes[2:3], codes[3:4], e), (8, slots))
        for d in last:
            wide = jnp.concatenate([local[e][d]] * tiles, axis=1)
            vector = jnp.where(block_of == jnp.bitwise_xor(me, d), wide, vector)
        every.append(vector)
    norm = lax.rsqrt(sum(every) + 1e-05)
    every = [jnp.sqrt(x) * norm for x in every]
    norms = {d: lax.rsqrt(sum(x[d] for x in local) + 1e-05) for d in last}
    local = [{d: jnp.sqrt(x[d]) * norms[d] for d in last} for x in local]
    for e in range(groups):
        as_rows(every[e] * scale[e], rows_ref.at[e])
    mine = [rows_ref[e, pl.ds(pl.multiple_of(chan * rows, 8), rows), :] for e in range(groups)]
    for n, d in enumerate(last):
        weight = [mine[e] * local[e][d][0:1] for e in range(groups)]
        shift = (jnp.bitwise_xor(me, d) * CAP + LANES - 7 * CAP) % LANES
        for g in range(parts):
            total = 0.0
            for e in range(groups):
                start = (n * parts + g) * rows
                total = total + turned[e][start : start + rows] * weight[e]
            lines_sum[n, g] = pltpu.roll(total, shift, 1)

    def emit(h, from_base):
        d_row = own * blocks + h
        b_row = jnp.bitwise_and(jnp.bitwise_xor(me, d_row), blocks - 1)
        d_late = last[h]

        def one_row(r, carry):
            target = b_row * CAP + r
            slot = jnp.bitwise_xor(me, d_row) * CAP + r
            weight = []
            for e in range(groups):
                row = rows_ref[e, pl.ds(slot, 1), :]
                weight.append(jnp.concatenate([row] * tiles, axis=1) * every[e][0:1])
            for g in range(parts):
                value = 0.0
                for e in range(groups):
                    if from_base:
                        part = base[e][h * CAP + r, 8 * g : 8 * g + 8]
                    else:
                        pieces = []
                        for t in range(tiles):
                            start = pl.multiple_of(((h * tiles + t) * CAP + r) * taus + 8 * g, 8)
                            pieces.append(late[e][pl.ds(start, 8), :])
                        part = jnp.concatenate(pieces, axis=1)
                    value = value + part * weight[e]
                for n, d in enumerate(last):
                    if not from_base and d <= d_late:
                        continue
                    line = jnp.broadcast_to(lines_sum[n, g, pl.ds(target, 1), :], (8, LANES))
                    line = pltpu.roll(line, 0, 1, stride=CAP, stride_axis=0)
                    line = jnp.concatenate([line] * tiles, axis=1)
                    value = jnp.where(block_of == jnp.bitwise_xor(me, d), line, value)
                stop = min(8, lags - 8 * g)
                out_ref[target, 8 * g : 8 * g + stop] = value[:stop]
            return carry

        lax.fori_loop(0, CAP, one_row, 0, unroll=2)

    copies = []
    for h in range(blocks):

        @pl.when(own < groups - 1)
        def _():
            emit(h, True)

        @pl.when(own == groups - 1)
        def _():
            emit(h, False)

        b_row = jnp.bitwise_and(jnp.bitwise_xor(me, own * blocks + h), blocks - 1)
        part = pl.ds(b_row * CAP, CAP)
        copies.append(pltpu.make_async_copy(out_ref.at[part], out_hbm.at[part], sem.at[h]))
        copies[-1].start()
    for c in copies:
        c.wait()


def finish(me, base, late, turned, last, blocks):
    rows, taus, slots = base[0].shape
    groups = slots // rows
    shape = (rows, 2 * MAXLAG + 1, slots)
    return pl.pallas_call(
        functools.partial(finish_kernel, last, blocks),
        out_shape=jax.ShapeDtypeStruct(shape, F32),
        in_specs=[IN_SMEM] + [IN_VMEM] * (3 * groups),
        out_specs=IN_HBM,
        scratch_shapes=[
            pltpu.VMEM(shape, F32),
            pltpu.VMEM((len(last), taus // 8, rows, LANES), F32),
            pltpu.VMEM((groups, slots, LANES), F32),
            pltpu.SemaphoreType.DMA((blocks,)),
        ],
        cost_estimate=SHORT,
        compiler_params=pltpu.CompilerParams(vmem_limit_bytes=FINISH_LIMIT),
        name="finish",
    )(me, *base, *late, *turned)


def local(waveforms, family_of, channel_mask):
    owners = lax.axis_size("fam")
    groups = lax.axis_size("chan")
    blocks = owners // groups
    slots = owners * CAP
    rows = blocks * CAP
    chans, length = waveforms.shape[1:]
    fam = lax.axis_index("fam")
    chan = lax.axis_index("chan")
    own = jnp.bitwise_xor(chan, fam // blocks)
    me = jnp.stack([fam, chan, own, fam // blocks]).astype(jnp.int32)

    half_lanes = LANES // 2
    mask = jnp.pad(channel_mask.astype(F32), ((0, 0), (0, half_lanes - chans)))
    mask = jnp.tile(mask, (1, 4))
    table = jnp.asarray(transform_table(length))
    lags = jnp.asarray(lag_table(length))
    taus = lag_rows()

    half = owners // 2
    last = list(range(owners - blocks, owners))
    early = [d for d in range(owners) if d not in last]
    first = list(range(half, half + blocks))
    sends, inbox, ms, energy = {}, {}, {}, {}
    widen = ((0, 0), (0, half_lanes - chans), (0, 0))

    def collect(dests, after):
        sends.update(zip(dests, gather(me, family_of, waveforms, owners, dests, after)))

    def post(d):
        inbox[d] = jnp.pad(lax.ppermute(sends[d], "fam", [(i, i ^ d) for i in range(owners)]), widen)

    def chan_permute(x, e):
        return lax.ppermute(x, "chan", [(i, i ^ e) for i in range(groups)])

    partners = list(range(groups - 1, 0, -1))

    collect(first, [])
    for d in first:
        post(d)
    collect(list(range(half)), [sends[first[0]]])
    for d in range(1, half):
        post(d)
    inbox[0] = jnp.pad(sends[0], widen)
    remaining = list(range(half + blocks, owners))
    collect(remaining, [inbox[d] for d in range(1, half)])
    for d in remaining:
        post(d)
    after = [sends[first[0]]]
    middle = [d for d in early if d >= half]
    rest = [d for d in early if d < half]
    for start in [0, 1] + list(range(4, half, 4)):
        if start == 1:
            after = after + [sends[remaining[0]]]
        part = list(range(start, min({0: 1, 1: 4}.get(start, start + 4), half)))
        got_m, got_e = whiten([inbox[d] for d in part], table, mask, after)
        ms.update(zip(part, got_m))
        energy.update(zip(part, got_e))
        after = [got_e[0]]

    limit = max(1, 16 * 2**20 // (CAP * length * slots * 4))
    per_call = max(n for n in range(blocks, len(early) + 1, blocks) if len(early) % n == 0 and n <= max(limit, blocks))
    held = {d: ms[d] for d in rest}
    filled = []
    for start in range(0, len(early), per_call):
        lines_of = early[start : start + per_call]
        xs = {d: inbox[d] for d in middle}
        more = int(start == 0)
        result = square(me, xs, table, mask, lags, held, energy, lines_of, slots, groups, more, after, filled)
        filled = [result[0]]
        if more:
            known = dict(zip(middle, result[1:]))
            ms.update(zip(middle, result[1 + len(middle) :]))
            after = [result[1]]
    energy.update(known)

    def narrow(x):
        return (x * F16_SCALE).astype(jnp.float16)

    early_rows = filled[0].reshape(groups, rows * taus, slots)
    sent = {e: chan_permute(narrow(early_rows[e]), e) for e in partners}

    kept = []
    for n, d in enumerate(last):
        result = step(me, inbox[d], table, mask, lags, ms, d, slots, groups, kept, after)
        kept = result[:2]
        after = []
        if n < len(last) - 1:
            ms[d], energy[d] = result[2:]
    late, turned = hold(kept, [sum(sent[e][:8].astype(F32) for e in partners)])

    def widen_f32(x, shape):
        return x.astype(F32).reshape(shape)

    base_parts, late_parts, turned_parts = [filled[0][0]], [late], [turned[0]]
    small = narrow(late)
    got_late, got_turned = {}, {}
    for e in partners:
        to_owner = []
        for f in range(owners):
            owner = (f // blocks) ^ (groups - 1)
            to_owner.append(((owner ^ e) * owners + f, owner * owners + f))
        got_late[e] = lax.ppermute(small, ("chan", "fam"), to_owner).astype(F32)
        got_turned[e] = chan_permute(narrow(turned[e]), e).astype(F32)
    for e in range(1, groups):
        base_parts.append(widen_f32(sent[e], (rows, taus, slots)))
        late_parts.append(got_late[e])
        turned_parts.append(got_turned[e])
    return finish(me, base_parts, late_parts, turned_parts, last, blocks)[None]


def solution(mesh):
    in_specs = (P("fam", "chan", None), P("fam"), P("fam", "chan"))
    out_specs = P("fam", "chan", None, None)
    return jax.shard_map(local, mesh=mesh, in_specs=in_specs, out_specs=out_specs, check_vma=False)
```

time: 519 us -> 182 us (0.35)
  waiting for transfers between devices: 217 us -> 54.1 us
  local copies, waits for them, and re-layouts: 134 us -> 5.58 us
  Pallas kernels: 0 us -> 86.5 us
  matrix products: 57.8 us -> 0 us
  other arithmetic: 65.7 us -> 11 us
  starting transfers between devices: 7.5 us -> 23.3 us
  between operations: 13.7 us -> 0.31 us
  loops' own time: 13.2 us -> 0 us
  blocking collectives: 5.64 us -> 0 us
    all_to_all x1 -> x0, waiting for transfers between devices: 183 us -> none  [local(): lax.all_to_all(outbox.reshape((owners, CAP) + trailing), 'fam', split_axi...]
    pallas_call x0 -> x10, Pallas kernels: none -> 86.5 us  [the longest x2 27.3 us: step(): pl.pallas_call(functools.partial(step_kernel, old, new, final), out_shape...]
    dot_general x6 -> x0, matrix products: 57.8 us -> none  [the longest x2 32.2 us: pair_terms(): cross = jnp.einsum('icpk,jcqpk->iqkj', left, both, precision=HIGH)]
    ppermute x0 -> x16, waiting for transfers between devices: none -> 54.1 us  [the longest x7 40.3 us: post(): lax.ppermute(sends[d], 'fam', [(i, i ^ d) for i in range(owners)])]
    reshape x6 -> x0, local copies, waits for them, and re-layouts: 50.5 us -> none  [the longest x4 29 us: pair_terms(): left = rows.reshape(rows.shape[0], rows.shape[1], 2, bins)]
    reduce_scatter x1 -> x0, waiting for transfers between devices: 33.8 us -> none  [local(): lax.psum_scatter(blocks_out.reshape((rows * lax.axis_size('chan'),) + blo...]
    while x13 -> x0, local copies, waits for them, and re-layouts: 24.8 us -> none  [the longest x1 20.9 us: local(): lax.map(one_block, jnp.arange(rows * lax.axis_size('chan') // block, dtyp...]
    mul x5 -> x0, other arithmetic: 23.8 us -> none  [the longest x3 23.7 us: local(): member = spectra * mask[None, :, None]]
  transfers between devices with their start and end apart: 2 -> 16, of which waited for: 2 -> 6; matrix products, arithmetic and copies ran while one was open for 1% -> 5% of each run, Pallas kernels for 0% -> 42%
where the time goes in v1:
time: 182 us; the launch traced here: 181 us
  Pallas kernels  86.5 us (48%)
  waiting for transfers between devices  54.1 us (30%)
  starting transfers between devices  23.3 us (13%)
  other arithmetic  11 us (6%)
  local copies, waits for them, and re-layouts  5.58 us (3%)
    ppermute x7, waiting for transfers between devices, post(): lax.ppermute(sends[d], 'fam', [(i, i ^ d) for i in range(owners)])  40.3 us
    pallas_call x2, Pallas kernels, step(): pl.pallas_call(functools.partial(step_kernel, old, new, final), out_shape...  27.3 us
    pallas_call x1, Pallas kernels, square(): pl.pallas_call(functools.partial(square_kernel, old, new, lines_of, more)...  25.9 us
    pallas_call x2, Pallas kernels, whiten(): pl.pallas_call(functools.partial(whiten_kernel, count), out_shape=[m] * c...  19.4 us
    ppermute x7, starting transfers between devices, post(): lax.ppermute(sends[d], 'fam', [(i, i ^ d) for i in range(owners)])  14.8 us
    ppermute x6, waiting for transfers between devices, chan_permute(): return lax.ppermute(x, 'chan', [(i, i ^ e) for i in range(groups)])  13.8 us
    pallas_call x3, Pallas kernels, gather(): pl.pallas_call(functools.partial(gather_kernel, owners, dests), out_shape...  11 us
    ppermute x3, starting transfers between devices, local(): got_late[e] = lax.ppermute(small, ('chan', 'fam'), to_owner).astype(F32)  5.94 us
  transfers between devices with their start and end apart: 16, of which 6 were waited for; matrix products, arithmetic and copies ran while one was open for 5% of the time, Pallas kernels for 42%

profile of v1, /device:TPU:0, one launch (start us, length us, event | category | flops | bytes accessed | tf_op | source)
XLA Modules:
  0.0 180.8 jit_solution(69531578301090871)
XLA Ops:
  0.7 3.4 %gather_slots.3 = (bf16[16,64,256]{2,1,0:T(8,128)(2,1)}, bf16[16,64,256]{2,1,0:T(8,128)(2,1)}) custom-call(s32[4]{0:T(128)} %pad_add_fusion.me_ref, s32[128]{0:T(128)} %family_ref.5, bf16[128,64,256]{2,1,0:T(8,128)(2,1)} %wave_ref.5), custom_call_target="tpu_custom_call" | custom-call | flops 1 | bytes 1 | tf_op jit(solution)/shard_map/gather_slots/pallas_call | solution.py:111
  4.0 4.1 %gather_slots.4 = (bf16[16,64,256]{2,1,0:T(8,128)(2,1)}, bf16[16,64,256]{2,1,0:T(8,128)(2,1)}, bf16[16,64,256]{2,1,0:T(8,128)(2,1)}, bf16[16,64,256]{2,1,0:T(8,128)(2,1)}) custom-call(s32[4]{0:T(128)} %pad_add_fusion.me_ref, s32[128]{0:T(128)} %family_ref.5, bf16[128,64,256]{2,1,0:T(8,128)(2,1)} %wave_ref.5, ...), custom_call_target="tpu_custom_call" | custom-call | flops 1 | bytes 1 | tf_op jit(solution)/shard_map/gather_slots/pallas_call | solution.py:111
  8.1 3.1 %collective-permute-start.2 = (bf16[16,64,256]{2,1,0:T(8,128)(2,1)}, bf16[16,64,256]{2,1,0:T(8,128)(2,1)S(1)}, u32[]{:S(2)}, u32[]{:S(2)}) collective-permute-start(bf16[16,64,256]{2,1,0:T(8,128)(2,1)} %get-tuple-element.36), channel_id=1, source_target_pairs={{0,1},{1,0},{2,3},{3,2},{4,5},{5,4},{6,7},{7,6},{8,9},{9,8},{10,11... | collective-permute-start | bytes 1572872 | tf_op jit(solution)/shard_map/ppermute | solution.py:701
  11.2 1.5 collective-permute-start.3
  12.8 3.1 %collective-permute-start = (bf16[16,64,256]{2,1,0:T(8,128)(2,1)S(1)}, bf16[16,64,256]{2,1,0:T(8,128)(2,1)S(1)}, u32[]{:S(2)}, u32[]{:S(2)}) collective-permute-start(bf16[16,64,256]{2,1,0:T(8,128)(2,1)S(1)} %copy-done.3), channel_id=1, source_target_pairs={{0,4},{1,5},{2,6},{3,7},{4,0},{5,1},{6,2},{7,3},{8,12},{9,13},{10,... | collective-permute-start | bytes 1572872 | tf_op jit(solution)/shard_map/ppermute | solution.py:701
  17.1 6.3 %collective-permute-done.2.rest_0_.refs_0_ = bf16[16,64,256]{2,1,0:T(8,128)(2,1)S(1)} collective-permute-done((bf16[16,64,256]{2,1,0:T(8,128)(2,1)}, bf16[16,64,256]{2,1,0:T(8,128)(2,1)S(1)}, u32[]{:S(2)}, u32[]{:S(2)}) %collective-permute-start.2) | collective-permute-done | bytes 524320 | tf_op jit(solution)/shard_map/ppermute | solution.py:701
  23.4 25.4 %collective-permute-done.3.rest_1_.refs_1_ = bf16[16,64,256]{2,1,0:T(8,128)(2,1)S(1)} collective-permute-done((bf16[16,64,256]{2,1,0:T(8,128)(2,1)}, bf16[16,64,256]{2,1,0:T(8,128)(2,1)S(1)}, u32[]{:S(2)}, u32[]{:S(2)}) %collective-permute-start.3) | collective-permute-done | bytes 524320 | tf_op jit(solution)/shard_map/ppermute | solution.py:701
  48.7 8.6 %collective-permute-done.4.rest_2_.refs_2_ = bf16[16,64,256]{2,1,0:T(8,128)(2,1)S(1)} collective-permute-done((bf16[16,64,256]{2,1,0:T(8,128)(2,1)}, bf16[16,64,256]{2,1,0:T(8,128)(2,1)S(1)}, u32[]{:S(2)}, u32[]{:S(2)}) %collective-permute-start.4) | collective-permute-done | bytes 524320 | tf_op jit(solution)/shard_map/ppermute | solution.py:701
  58.1 3.5 %gather_slots.5 = (bf16[16,64,256]{2,1,0:T(8,128)(2,1)}, bf16[16,64,256]{2,1,0:T(8,128)(2,1)}) custom-call(s32[4]{0:T(128)} %pad_add_fusion.me_ref, s32[128]{0:T(128)} %family_ref.5, bf16[128,64,256]{2,1,0:T(8,128)(2,1)} %wave_ref.5, bf16[16,64,256]{2,1,0:T(8,128)(2,1)} %copy-done.4, bf16[16,64,256]{2,1,0:T(8,128)(2,1)} %copy-done.5, ...), custom_call_target="tpu_custom_call" | custom-call | flops 1 | bytes 1 | tf_op jit(solution)/shard_map/gather_slots/pallas_call | solution.py:111
  61.7 1.5 collective-permute-start.9
  63.2 4.3 %collective-permute-start.8 = (bf16[16,64,256]{2,1,0:T(8,128)(2,1)}, bf16[16,64,256]{2,1,0:T(8,128)(2,1)}, u32[]{:S(2)}, u32[]{:S(2)}) collective-permute-start(bf16[16,64,256]{2,1,0:T(8,128)(2,1)} %get-tuple-element.48), channel_id=1, source_target_pairs={{0,7},{1,6},{2,5},{3,4},{4,3},{5,2},{6,1},{7,0},{8,15},{9,14},{10,... | collective-permute-start | bytes 1572872 | tf_op jit(solution)/shard_map/ppermute | solution.py:701
  68.2 6.4 %whiten.2 = (bf16[128,16,256]{2,1,0:T(8,128)(2,1)}, f32[8,128]{1,0:T(8,128)}) custom-call(bf16[512,256]{1,0:T(8,128)(2,1)} %constant.32.clone.table_hbm, f32[1,256]{1,0:T(1,128)} %tile.13.mask_ref, bf16[16,64,256]{2,1,0:T(8,128)(2,1)} %get-tuple-element.34.refs_0_, bf16[16,64,256]{2,1,0:T(8,128)(2,1)} %get-tuple-element.32.rest_0_.refs_1_), custom_call_target="tpu_custom_call" | custom-call | flops 1 | bytes 1 | tf_op jit(solution)/shard_map/whiten/pallas_call | solution.py:235
  74.7 12.9 %whiten.3 = (bf16[128,16,256]{2,1,0:T(8,128)(2,1)}, bf16[128,16,256]{2,1,0:T(8,128)(2,1)}, bf16[128,16,256]{2,1,0:T(8,128)(2,1)}, f32[8,128]{1,0:T(8,128)}, f32[8,128]{1,0:T(8,128)}, /*index=5*/f32[8,128]{1,0:T(8,128)}) custom-call(bf16[512,256]{1,0:T(8,128)(2,1)} %constant.32.clone.table_hbm, f32[1,256]{1,0:T(1,128)} %tile.13.mask_ref, ...), custom_call_target="tpu_custom_call" | custom-call | flops 1 | bytes 1 | tf_op jit(solution)/shard_map/whiten/pallas_call | solution.py:235
  88.6 25.9 %square.1 = (f32[4,32,72,128]{3,2,1,0:T(8,128)}, f32[8,128]{1,0:T(8,128)}, f32[8,128]{1,0:T(8,128)}, bf16[128,16,256]{2,1,0:T(8,128)(2,1)}, bf16[128,16,256]{2,1,0:T(8,128)(2,1)}) custom-call(s32[4]{0:T(128)} %pad_add_fusion.me_ref, bf16[512,256]{1,0:T(8,128)(2,1)} %constant.32.clone.table_hbm, f32[1,256]{1,0:T(1,128)} %tile.13.mask_ref, ...), custom_call_target="tpu_custom_call" | custom-call | flops 1 | bytes 1 | tf_op jit(solution)/shard_map/square/pallas_call | solution.py:441
  114.5 3.7 %multiply_convert_fusion.1 = (f16[1,32,72,128]{3,2,1,0:T(8,128)(2,1)}, f16[1,32,72,128]{3,2,1,0:T(8,128)(2,1)}, f16[1,32,72,128]{3,2,1,0:T(8,128)(2,1)}, f32[32,72,128]{2,1,0:T(8,128)S(1)}) fusion(f32[4,32,72,128]{3,2,1,0:T(8,128)} %get-tuple-element.47), kind=kLoop, calls=%fused_computation.1 | loop fusion | flops 1769472 | bytes 7667712 | tf_op jit(solution)/shard_map/convert_element_type | solution.py:748
  118.2 1.5 collective-permute-start.6
  120.9 13.4 %step.2 = (f32[1152,128]{1,0:T(8,128)}, f32[4,288,128]{2,1,0:T(8,128)}, bf16[128,16,256]{2,1,0:T(8,128)(2,1)}, f32[8,128]{1,0:T(8,128)}) custom-call(s32[4]{0:T(128)} %pad_add_fusion.me_ref, bf16[512,256]{1,0:T(8,128)(2,1)} %constant.32.clone.table_hbm, f32[1,256]{1,0:T(1,128)} %tile.13.mask_ref, bf16[144,256]{1,0:T(8,128)(2,1)} %constant.33.clone.lag_ref, ...), custom_call_target="tpu_custom_call" | custom-call | flops 1 | bytes 1 | tf_op jit(solution)/shard_map/step/pallas_call | solution.py:512
  134.3 13.9 %step.3 = (f32[2304,128]{1,0:T(8,128)}, f32[4,576,128]{2,1,0:T(8,128)}) custom-call(s32[4]{0:T(128)} %pad_add_fusion.me_ref, bf16[512,256]{1,0:T(8,128)(2,1)} %constant.32.clone.table_hbm, f32[1,256]{1,0:T(1,128)} %tile.13.mask_ref, bf16[144,256]{1,0:T(8,128)(2,1)} %constant.33.clone.lag_ref, bf16[16,64,256]{2,1,0:T(8,128)(2,1)} %collective-permute-done.8.x_hbm, ...), custom_call_target="tpu_custom_call" | custom-call | flops 100000000376832 | bytes 1 | tf_op jit(solution)/shard_map/step/pallas_call | solution.py:512
  149.5 1.5 multiply_convert_fusion
  152.4 4.5 %collective-permute-start.12 = (f16[2304,128]{1,0:T(8,128)(2,1)S(1)}, f16[2304,128]{1,0:T(8,128)(2,1)S(1)}, u32[]{:S(2)}, u32[]{:S(2)}) collective-permute-start(f16[2304,128]{1,0:T(8,128)(2,1)S(1)} %multiply_convert_fusion), channel_id=1, source_target_pairs={{0,24},{1,25},{10,18},{11,19},{20,12},{21,13},{30,6},{31,7}} | collective-permute-start | bytes 1769480 | tf_op jit(solution)/shard_map/ppermute | solution.py:773
  157.3 1.3 collective-permute-done.13
  162.5 11.0 %collective-permute-done.14 = f16[576,128]{1,0:T(8,128)(2,1)S(1)} collective-permute-done((f16[576,128]{1,0:T(8,128)(2,1)S(1)}, f16[576,128]{1,0:T(8,128)(2,1)S(1)}, u32[]{:S(2)}, u32[]{:S(2)}) %collective-permute-start.14) | collective-permute-done | bytes 147488 | tf_op jit(solution)/shard_map/ppermute | solution.py:704
  173.6 1.6 collective-permute-done.15
  176.6 3.0 %finish.1 = f32[32,65,128]{2,1,0:T(8,128)S(1)} custom-call(s32[4]{0:T(128)S(1)} %copy-done.1, f32[32,72,128]{2,1,0:T(8,128)S(1)} %get-tuple-element.62.refs_0_, f32[32,72,128]{2,1,0:T(8,128)S(1)} %convert.3.refs_1_, f32[32,72,128]{2,1,0:T(8,128)S(1)} %convert.4.refs_2_, f32[32,72,128]{2,1,0:T(8,128)S(1)} %convert.5.refs_3_, f32[2304,128]{1,0:T(8,128)S(1)} %copy-done, ...), custom_call_target="tpu_custom_call" | custom-call | flops 1 | bytes 1 | tf_op jit(solution)/shard_map/finish/pallas_call | solution.py:654
  (58 shorter events, 15.0 us)
Async XLA Ops:
  4.0 8.7 %copy-start.3 = (bf16[16,64,256]{2,1,0:T(8,128)(2,1)S(1)}, bf16[16,64,256]{2,1,0:T(8,128)(2,1)}, u32[]{:S(2)}) copy-start(bf16[16,64,256]{2,1,0:T(8,128)(2,1)} %get-tuple-element.32.rest_0_.refs_1_) | copy-start | bytes 1572868
  8.1 15.2 %collective-permute-start.2 = (bf16[16,64,256]{2,1,0:T(8,128)(2,1)}, bf16[16,64,256]{2,1,0:T(8,128)(2,1)S(1)}, u32[]{:S(2)}, u32[]{:S(2)}) collective-permute-start(bf16[16,64,256]{2,1,0:T(8,128)(2,1)} %get-tuple-element.36), channel_id=1, source_target_pairs={{0,1},{1,0},{2,3},{3,2},{4,5},{5,4},{6,7},{7,6},{8,9},{9,8},{10,11... | collective-permute-start | bytes 1572872 | tf_op jit(solution)/shard_map/ppermute | solution.py:701
  11.2 37.5 %collective-permute-start.3 = (bf16[16,64,256]{2,1,0:T(8,128)(2,1)}, bf16[16,64,256]{2,1,0:T(8,128)(2,1)S(1)}, u32[]{:S(2)}, u32[]{:S(2)}) collective-permute-start(bf16[16,64,256]{2,1,0:T(8,128)(2,1)} %get-tuple-element.37), channel_id=1, source_target_pairs={{0,2},{1,3},{2,0},{3,1},{4,6},{5,7},{6,4},{7,5},{8,10},{9,11},{10,... | collective-permute-start | bytes 1572872 | tf_op jit(solution)/shard_map/ppermute | solution.py:701
  12.8 44.6 %collective-permute-start.4 = (bf16[16,64,256]{2,1,0:T(8,128)(2,1)}, bf16[16,64,256]{2,1,0:T(8,128)(2,1)S(1)}, u32[]{:S(2)}, u32[]{:S(2)}) collective-permute-start(bf16[16,64,256]{2,1,0:T(8,128)(2,1)} %get-tuple-element.38), channel_id=1, source_target_pairs={{0,3},{1,2},{2,1},{3,0},{4,7},{5,6},{6,5},{7,4},{8,11},{9,10},{10,... | collective-permute-start | bytes 1572872 | tf_op jit(solution)/shard_map/ppermute | solution.py:701
  12.8 74.8 %collective-permute-start = (bf16[16,64,256]{2,1,0:T(8,128)(2,1)S(1)}, bf16[16,64,256]{2,1,0:T(8,128)(2,1)S(1)}, u32[]{:S(2)}, u32[]{:S(2)}) collective-permute-start(bf16[16,64,256]{2,1,0:T(8,128)(2,1)S(1)} %copy-done.3), channel_id=1, source_target_pairs={{0,4},{1,5},{2,6},{3,7},{4,0},{5,1},{6,2},{7,3},{8,12},{9,13},{10,... | collective-permute-start | bytes 1572872 | tf_op jit(solution)/shard_map/ppermute | solution.py:701
  15.9 51.7 %copy-start.10 = (s32[1,64]{1,0:T(1,128)S(1)}, s32[1,64]{1,0:T(1,128)}, u32[]{:S(2)}) copy-start(s32[1,64]{1,0:T(1,128)} %param.7) | copy-start | bytes 772
  15.9 71.8 %collective-permute-start.1 = (bf16[16,64,256]{2,1,0:T(8,128)(2,1)}, bf16[16,64,256]{2,1,0:T(8,128)(2,1)S(1)}, u32[]{:S(2)}, u32[]{:S(2)}) collective-permute-start(bf16[16,64,256]{2,1,0:T(8,128)(2,1)} %get-tuple-element.33), channel_id=1, source_target_pairs={{0,5},{1,4},{2,7},{3,6},{4,1},{5,0},{6,3},{7,2},{8,13},{9,12},{10,... | collective-permute-start | bytes 1572872 | tf_op jit(solution)/shard_map/ppermute | solution.py:701
  23.4 34.0 %copy-start.4 = (bf16[16,64,256]{2,1,0:T(8,128)(2,1)}, bf16[16,64,256]{2,1,0:T(8,128)(2,1)S(1)}, u32[]{:S(2)}) copy-start(bf16[16,64,256]{2,1,0:T(8,128)(2,1)S(1)} %collective-permute-done.2.rest_0_.refs_0_) | copy-start | bytes 1572868
  48.7 8.6 %copy-start.5 = (bf16[16,64,256]{2,1,0:T(8,128)(2,1)}, bf16[16,64,256]{2,1,0:T(8,128)(2,1)S(1)}, u32[]{:S(2)}) copy-start(bf16[16,64,256]{2,1,0:T(8,128)(2,1)S(1)} %collective-permute-done.3.rest_1_.refs_1_) | copy-start | bytes 1572868
  61.7 58.4 %collective-permute-start.9 = (bf16[16,64,256]{2,1,0:T(8,128)(2,1)}, bf16[16,64,256]{2,1,0:T(8,128)(2,1)S(1)}, u32[]{:S(2)}, u32[]{:S(2)}) collective-permute-start(bf16[16,64,256]{2,1,0:T(8,128)(2,1)} %get-tuple-element.40.refs_4_), channel_id=1, source_target_pairs={{0,6},{1,7},{2,4},{3,5},{4,2},{5,3},{6,0},{7,1},{8,14},{9,15},{10,... | collective-permute-start | bytes 1572872 | tf_op jit(solution)/shard_map/ppermute | solution.py:701
  63.2 71.1 %collective-permute-start.8 = (bf16[16,64,256]{2,1,0:T(8,128)(2,1)}, bf16[16,64,256]{2,1,0:T(8,128)(2,1)}, u32[]{:S(2)}, u32[]{:S(2)}) collective-permute-start(bf16[16,64,256]{2,1,0:T(8,128)(2,1)} %get-tuple-element.48), channel_id=1, source_target_pairs={{0,7},{1,6},{2,5},{3,4},{4,3},{5,2},{6,1},{7,0},{8,15},{9,14},{10,... | collective-permute-start | bytes 1572872 | tf_op jit(solution)/shard_map/ppermute | solution.py:701
  87.6 1.0 copy-start.9
  118.2 30.0 %collective-permute-start.5 = (f16[2304,128]{1,0:T(8,128)(2,1)}, f16[2304,128]{1,0:T(8,128)(2,1)}, u32[]{:S(2)}, u32[]{:S(2)}) collective-permute-start(f16[2304,128]{1,0:T(8,128)(2,1)} %bitcast.6), channel_id=1, source_target_pairs={{0,8},{8,0},{16,24},{24,16},{1,9},{9,1},{17,25},{25,17},{2,10},{10... | collective-permute-start | bytes 1769480 | tf_op jit(solution)/shard_map/ppermute | solution.py:704
  118.2 30.0 %collective-permute-start.6 = (f16[2304,128]{1,0:T(8,128)(2,1)}, f16[2304,128]{1,0:T(8,128)(2,1)}, u32[]{:S(2)}, u32[]{:S(2)}) collective-permute-start(f16[2304,128]{1,0:T(8,128)(2,1)} %bitcast.8), channel_id=1, source_target_pairs={{0,16},{8,24},{16,0},{24,8},{1,17},{9,25},{17,1},{25,9},{2,18},{10... | collective-permute-start | bytes 1769480 | tf_op jit(solution)/shard_map/ppermute | solution.py:704
  119.8 28.5 %collective-permute-start.7 = (f16[2304,128]{1,0:T(8,128)(2,1)}, f16[2304,128]{1,0:T(8,128)(2,1)}, u32[]{:S(2)}, u32[]{:S(2)}) collective-permute-start(f16[2304,128]{1,0:T(8,128)(2,1)} %bitcast.10), channel_id=1, source_target_pairs={{0,24},{8,16},{16,8},{24,0},{1,25},{9,17},{17,9},{25,1},{2,26},{10... | collective-permute-start | bytes 1769480 | tf_op jit(solution)/shard_map/ppermute | solution.py:704
  149.5 7.5 %copy-start.2 = (f32[4,576,128]{2,1,0:T(8,128)S(1)}, f32[4,576,128]{2,1,0:T(8,128)}, u32[]{:S(2)}) copy-start(f32[4,576,128]{2,1,0:T(8,128)} %get-tuple-element.58) | copy-start | bytes 3538948
  151.0 24.1 %collective-permute-start.10 = (f16[2304,128]{1,0:T(8,128)(2,1)S(1)}, f16[2304,128]{1,0:T(8,128)(2,1)S(1)}, u32[]{:S(2)}, u32[]{:S(2)}) collective-permute-start(f16[2304,128]{1,0:T(8,128)(2,1)S(1)} %multiply_convert_fusion), channel_id=1, source_target_pairs={{16,24},{17,25},{26,18},{27,19},{4,12},{5,13},{14,6},{15,7}} | collective-permute-start | bytes 1769480 | tf_op jit(solution)/shard_map/ppermute | solution.py:773
  151.7 23.5 %collective-permute-start.11 = (f16[2304,128]{1,0:T(8,128)(2,1)S(1)}, f16[2304,128]{1,0:T(8,128)(2,1)S(1)}, u32[]{:S(2)}, u32[]{:S(2)}) collective-permute-start(f16[2304,128]{1,0:T(8,128)(2,1)S(1)} %multiply_convert_fusion), channel_id=1, source_target_pairs={{8,24},{9,25},{2,18},{3,19},{28,12},{29,13},{22,6},{23,7}} | collective-permute-start | bytes 1769480 | tf_op jit(solution)/shard_map/ppermute | solution.py:773
  152.4 22.9 %collective-permute-start.12 = (f16[2304,128]{1,0:T(8,128)(2,1)S(1)}, f16[2304,128]{1,0:T(8,128)(2,1)S(1)}, u32[]{:S(2)}, u32[]{:S(2)}) collective-permute-start(f16[2304,128]{1,0:T(8,128)(2,1)S(1)} %multiply_convert_fusion), channel_id=1, source_target_pairs={{0,24},{1,25},{10,18},{11,19},{20,12},{21,13},{30,6},{31,7}} | collective-permute-start | bytes 1769480 | tf_op jit(solution)/shard_map/ppermute | solution.py:773
  157.1 1.4 collective-permute-start.13
  157.2 16.3 %collective-permute-start.14 = (f16[576,128]{1,0:T(8,128)(2,1)S(1)}, f16[576,128]{1,0:T(8,128)(2,1)S(1)}, u32[]{:S(2)}, u32[]{:S(2)}) collective-permute-start(f16[576,128]{1,0:T(8,128)(2,1)S(1)} %get-tuple-element.64), channel_id=1, source_target_pairs={{0,16},{8,24},{16,0},{24,8},{1,17},{9,25},{17,1},{25,9},{2,18},{10... | collective-permute-start | bytes 442376 | tf_op jit(solution)/shard_map/ppermute | solution.py:704
  158.5 16.6 %collective-permute-start.15 = (f16[576,128]{1,0:T(8,128)(2,1)S(1)}, f16[576,128]{1,0:T(8,128)(2,1)S(1)}, u32[]{:S(2)}, u32[]{:S(2)}) collective-permute-start(f16[576,128]{1,0:T(8,128)(2,1)S(1)} %get-tuple-element.63), channel_id=1, source_target_pairs={{0,24},{8,16},{16,8},{24,0},{1,25},{9,17},{17,9},{25,1},{2,26},{10... | collective-permute-start | bytes 442376 | tf_op jit(solution)/shard_map/ppermute | solution.py:704
  175.3 1.3 copy-start
  175.3 1.3 copy-start.1
  (3 other events, 2.4 us)

commit v2 on v1

--- a/solution.py
+++ b/solution.py
@@ -16,6 +16,7 @@
 TINY = 1.2e-38
 VMEM_LIMIT = 56 * 2**20
 PITCH_PAD = 8
+LOAD_PARTS = 4
 LONG = pl.CostEstimate(flops=10**14, bytes_accessed=1, transcendentals=0)
 SHORT = pl.CostEstimate(flops=1, bytes_accessed=1, transcendentals=0)
 FINISH_LIMIT = 40 * 2**20
@@ -190,13 +191,14 @@
         write(k, *split(member))
         return carry
 
-    lax.fori_loop(0, bins, relayout, 0, unroll=16)
+    lax.fori_loop(0, bins, relayout, 0, unroll=32)
     return tile
 
 
-def whiten_kernel(count, table_hbm, mask_ref, *refs):
+def whiten_kernel(ds, table_hbm, mask_ref, *refs):
+    count = len(ds)
     x_hbm = refs[:count]
-    m_hbm, e_ref = refs[-7 - 2 * count : -7 - count], refs[-7 - count : -7]
+    m_hbm, e_ref = refs[-8 - count], refs[-7 - count : -7]
     x_ref, table_ref, m_ref, scratch, sem, x_sem, out_sem = refs[-7:]
     load = pltpu.make_async_copy(table_hbm, table_ref, sem)
     load.start()
@@ -205,7 +207,7 @@
         c.start()
     load.wait()
     outs = []
-    for n in range(count):
+    for n, d in enumerate(ds):
         loads[n].wait()
 
         def write(k, high, low):
@@ -213,7 +215,7 @@
             m_ref[n, k, :, LANES:] = low
 
         e_ref[n][...] = whiten_body(x_ref.at[n], table_ref, mask_ref, scratch.at[n % 2], write)
-        outs.append(pltpu.make_async_copy(m_ref.at[n], m_hbm[n], out_sem.at[n]))
+        outs.append(pltpu.make_async_copy(m_ref.at[n], m_hbm.at[d], out_sem.at[n]))
         outs[-1].start()
     for c in outs:
         c.wait()
@@ -229,16 +231,17 @@
 ENERGY = jax.ShapeDtypeStruct((8, LANES), F32)
 
 
-def whiten(xs, table, mask, after):
-    count = len(xs)
-    m, scratch = member_shapes(xs[0])
+def whiten(xs, table, mask, owners, filled, after):
+    ds = sorted(xs)
+    count = len(ds)
+    m, scratch = member_shapes(xs[ds[0]])
     out = pl.pallas_call(
-        functools.partial(whiten_kernel, count),
-        out_shape=[m] * count + [ENERGY] * count,
-        in_specs=[IN_HBM, IN_VMEM] + [IN_HBM] * (count + len(after)),
-        out_specs=[IN_HBM] * count + [IN_VMEM] * count,
+        functools.partial(whiten_kernel, ds),
+        out_shape=[jax.ShapeDtypeStruct((owners,) + m.shape, m.dtype)] + [ENERGY] * count,
+        in_specs=[IN_HBM, IN_VMEM] + [IN_HBM] * (count + len(after) + len(filled)),
+        out_specs=[IN_HBM] + [IN_VMEM] * count,
         scratch_shapes=[
-            pltpu.VMEM((count,) + xs[0].shape, xs[0].dtype),
+            pltpu.VMEM((count,) + xs[ds[0]].shape, xs[ds[0]].dtype),
             pltpu.VMEM(table.shape, table.dtype),
             pltpu.VMEM((count,) + m.shape, m.dtype),
             pltpu.VMEM((2,) + scratch, F32),
@@ -247,10 +250,11 @@
             pltpu.SemaphoreType.DMA((count,)),
         ],
         cost_estimate=SHORT,
+        input_output_aliases={2 + count + len(after): 0} if filled else {},
         compiler_params=pltpu.CompilerParams(vmem_limit_bytes=VMEM_LIMIT),
         name="whiten",
-    )(table, mask, *xs, *after)
-    return out[:count], out[count:]
+    )(table, mask, *[xs[d] for d in ds], *after, *filled)
+    return out[0], dict(zip(ds, out[1:]))
 
 
 def turn(m):
@@ -258,17 +262,17 @@
     return jnp.concatenate([m[:, half:LANES], -m[:, :half]], axis=1)
 
 
-def pairs_body(me, new, members, table_ref, cross_ref, emit):
-    bins, slots, _ = members.shape
+def pairs_body(me, new, members, table_ref, cross_ref, copies, emit, ready):
+    count, bins, _, _ = members.shape
+    slots = count * CAP
     tiles = slots // LANES
     taus = table_ref.shape[0] // 2
     n = len(new) * CAP
     pitch = 2 * bins + PITCH_PAD
 
     def cross(k, carry):
-        both = members[k]
-        left = [members[k, pl.ds(place(me, d), CAP), :] for d in new]
-        left = jnp.concatenate(left, axis=0)
+        both = jnp.concatenate([members[jnp.bitwise_xor(me, b), k] for b in range(count)], axis=0)
+        left = jnp.concatenate([members[d, k] for d in new], axis=0)
         high = left[:, :LANES]
         low = left[:, LANES:]
         left = jnp.concatenate([high, turn(high), low, turn(low)], axis=0)
@@ -281,7 +285,10 @@
                 cross_ref[t, pl.ds(q * bins + k, n, stride=pitch), :] = part
         return carry
 
-    lax.fori_loop(0, bins, cross, 0, unroll=16 if n <= 32 else 8)
+    step = bins // LOAD_PARTS
+    for p in range(LOAD_PARTS):
+        copies[p].wait()
+        lax.fori_loop(p * step, (p + 1) * step, cross, 0, unroll=16)
     table = table_ref[...]
 
     def lag(i, carry):
@@ -295,7 +302,10 @@
                 emit(2 * i + h, t, out[:, h * LANES : (h + 1) * LANES])
         return carry
 
-    lax.fori_loop(0, n // 2, lag, 0, unroll=4)
+    for start in range(0, n // 2, CAP):
+        stop = min(start + CAP, n // 2)
+        lax.fori_loop(start, stop, lag, 0, unroll=8)
+        ready(2 * stop)
 
 
 def turn_lines(lines, codes, chan, turned, taus):
@@ -321,12 +331,14 @@
     return pl.multiple_of(jnp.bitwise_xor(me, d) * CAP, CAP)
 
 
-def load_members(me, ms, old, members, sem):
-    copies = [
-        pltpu.make_async_copy(ms[i], members.at[:, pl.ds(place(me, d), CAP), :], sem.at[i]) for i, d in enumerate(old)
-    ]
-    for c in copies:
-        c.start()
+def load_members(m_hbm, count, members, sem):
+    step = members.shape[1] // LOAD_PARTS
+    copies = []
+    for p in range(LOAD_PARTS):
+        part = pl.ds(p * step, step)
+        source, target = m_hbm.at[pl.ds(0, count), part], members.at[pl.ds(0, count), part]
+        copies.append(pltpu.make_async_copy(source, target, sem.at[p]))
+        copies[-1].start()
     return copies
 
 
@@ -344,7 +356,7 @@
         ref[t * LANES : (t + 1) * LANES] = part.T
 
 
-def whiten_and_load(new, old, me, x_hbm, ms, tables, buffers, sems, keep):
+def whiten_and_load(new, count, me, x_hbm, m_hbm, tables, buffers, sems, keep):
     table_hbm, mask_ref = tables
     x_ref, table_ref, scratch, members = buffers
     load, x_sem, sem = sems
@@ -353,36 +365,33 @@
     loads = [pltpu.make_async_copy(x_hbm[n], x_ref.at[n], x_sem.at[n]) for n in range(len(new))]
     for c in loads:
         c.start()
-    copies = load_members(me, ms, old, members, sem)
+    copies = load_members(m_hbm, count, members, sem)
     table_load.wait()
     tiles = {}
     for n, d in enumerate(new):
-        where = place(me, d)
         loads[n].wait()
 
         def write(k, high, low):
-            members[k, pl.ds(where, CAP), :LANES] = high
-            members[k, pl.ds(where, CAP), LANES:] = low
+            members[d, k, :, :LANES] = high
+            members[d, k, :, LANES:] = low
 
         tiles[d] = whiten_body(x_ref.at[n], table_ref, mask_ref, scratch.at[n % 2], write)
-        keep(n, members.at[:, pl.ds(where, CAP), :])
-    for c in copies:
-        c.wait()
-    return tiles
-
-
-def shared_scratch(x, new, old, table, slots, n):
+        keep(d, members.at[d])
+    return tiles, copies
+
+
+def shared_scratch(x, new, table, slots, n):
     m, scratch = member_shapes(x)
     bins = m.shape[0]
     return [
         pltpu.VMEM((len(new),) + x.shape, x.dtype),
         pltpu.VMEM(table.shape, table.dtype),
         pltpu.VMEM((min(2, len(new)),) + scratch, F32),
-        pltpu.VMEM((bins, slots, 2 * LANES), BF16),
+        pltpu.VMEM((slots // CAP, bins, CAP, 2 * LANES), BF16),
         pltpu.VMEM((slots // LANES, n * (2 * bins + PITCH_PAD), LANES), F32),
         pltpu.SemaphoreType.DMA,
         pltpu.SemaphoreType.DMA((len(new),)),
-        pltpu.SemaphoreType.DMA((len(old),)),
+        pltpu.SemaphoreType.DMA((LOAD_PARTS,)),
         pltpu.SemaphoreType.DMA((24,)),
     ]
 
@@ -390,21 +399,23 @@
 def square_kernel(old, new, lines_of, more, me_ref, table_hbm, mask_ref, lag_ref, *refs):
     count = len(new)
     x_hbm, refs = refs[:count], refs[count:]
-    ms, refs = refs[: len(old)], refs[len(old) :]
+    m_hbm, refs = refs[0], refs[1:]
     given, refs = refs[: len(old)], refs[len(old) :]
     x_ref, table_ref, scratch, members, cross_ref, load, x_sem, sem, out_sem, rows_ref = refs[-10:]
-    outs = refs[-10 - 1 - count * (1 + more) : -10]
+    outs = refs[-10 - 1 - count - more : -10]
     me, own = me_ref[0], me_ref[2]
-    slots = members.shape[1]
+    slots = members.shape[0] * CAP
     done = []
 
-    def keep(n, block):
+    def keep(d, block):
         if more:
-            done.append(pltpu.make_async_copy(block, outs[1 + count + n], out_sem.at[8 + n]))
+            done.append(pltpu.make_async_copy(block, outs[1 + count].at[d], out_sem.at[8 + len(done)]))
             done[-1].start()
 
     buffers = (x_ref, table_ref, scratch, members)
-    tiles = whiten_and_load(new, old, me, x_hbm, ms, (table_hbm, mask_ref), buffers, (load, x_sem, sem), keep)
+    sems = (load, x_sem, sem)
+    tables = (table_hbm, mask_ref)
+    tiles, copies = whiten_and_load(new, len(old), me, x_hbm, m_hbm, tables, buffers, sems, keep)
     for n, d in enumerate(new):
         outs[1 + n][...] = tiles[d]
     for d, ref in zip(old, given):
@@ -414,15 +425,20 @@
     def emit(row, t, part):
         rows_ref[row, :, t * LANES : (t + 1) * LANES] = part
 
-    pairs_body(me, lines_of, members, lag_ref, cross_ref, emit)
     groups, rows = outs[0].shape[:2]
     first = lines_of[0] * CAP // rows
-    for n in range(rows_ref.shape[0] // rows):
-        for c, code in enumerate(codes):
-            rows_ref[n * rows, 2 * MAXLAG + 1 + c : 2 * MAXLAG + 2 + c] = code[0:1]
-        target = jnp.bitwise_xor(first + n, own)
-        done.append(pltpu.make_async_copy(rows_ref.at[n * rows : (n + 1) * rows], outs[0].at[target], out_sem.at[n]))
-        done[-1].start()
+
+    def ready(stop):
+        if stop % rows == 0:
+            n = stop // rows - 1
+            for c, code in enumerate(codes):
+                rows_ref[n * rows, 2 * MAXLAG + 1 + c : 2 * MAXLAG + 2 + c] = code[0:1]
+            target = jnp.bitwise_xor(first + n, own)
+            part = rows_ref.at[n * rows : (n + 1) * rows]
+            done.append(pltpu.make_async_copy(part, outs[0].at[target], out_sem.at[n]))
+            done[-1].start()
+
+    pairs_body(me, lines_of, members, lag_ref, cross_ref, copies, emit, ready)
     if first + rows_ref.shape[0] // rows == groups - 1:
         target = jnp.bitwise_xor(groups - 1, own)
         done.append(pltpu.make_async_copy(rows_ref.at[:rows], outs[0].at[target], out_sem.at[groups - 1]))
@@ -432,36 +448,37 @@
 
 
 def square(me, xs, table, mask, lags, ms, energy, lines_of, slots, groups, more, after, filled):
-    old, new = sorted(ms), sorted(xs)
+    old, new = sorted(energy), sorted(xs)
     taus = lags.shape[0] // 2
     x = xs[new[0]]
-    m, _ = member_shapes(x)
     n = len(lines_of) * CAP
     rows = jax.ShapeDtypeStruct((groups, slots // groups, taus, slots), F32)
+    members = jax.ShapeDtypeStruct(ms.shape, ms.dtype)
+    aliases = {4 + len(new): 1 + len(new)} if more else {}
+    if filled:
+        aliases[5 + len(new) + len(old) + len(after)] = 0
     return pl.pallas_call(
         functools.partial(square_kernel, old, new, lines_of, more),
-        out_shape=[rows] + [ENERGY] * len(new) + [m] * (more * len(new)),
+        out_shape=[rows] + [ENERGY] * len(new) + [members] * more,
         in_specs=[IN_SMEM, IN_HBM, IN_VMEM, IN_VMEM]
-        + [IN_HBM] * (len(new) + len(old))
+        + [IN_HBM] * (len(new) + 1)
         + [IN_VMEM] * len(old)
         + [IN_HBM] * (len(after) + len(filled)),
-        out_specs=[IN_HBM] + [IN_VMEM] * len(new) + [IN_HBM] * (more * len(new)),
-        scratch_shapes=shared_scratch(x, new, old, table, slots, n)
-        + [pltpu.VMEM((n, taus, slots), F32)],
+        out_specs=[IN_HBM] + [IN_VMEM] * len(new) + [IN_HBM] * more,
+        scratch_shapes=shared_scratch(x, new, table, slots, n) + [pltpu.VMEM((n, taus, slots), F32)],
         cost_estimate=SHORT,
+        input_output_aliases=aliases,
         compiler_params=pltpu.CompilerParams(vmem_limit_bytes=VMEM_LIMIT),
-        input_output_aliases={4 + len(new) + 2 * len(old) + len(after): 0} if filled else {},
         name="square",
-    )(me, table, mask, lags, *[xs[d] for d in new], *[ms[d] for d in old], *[energy[d] for d in old], *after, *filled)
-
-
-def step_kernel(old, new, final, me_ref, table_hbm, mask_ref, lag_ref, x_hbm, *refs):
-    ms, refs = refs[: len(old)], refs[len(old) :]
+    )(me, table, mask, lags, *[xs[d] for d in new], ms, *[energy[d] for d in old], *after, *filled)
+
+
+def step_kernel(new, final, me_ref, table_hbm, mask_ref, lag_ref, x_hbm, m_hbm, *refs):
     lines, turned_ref = refs[-2:]
     x_ref, table_ref, scratch, members, cross_ref, load, x_sem, sem, out_sem = refs[-11:-2]
     outs = refs[-11 - (2 if final else 4) : -11]
     me, chan = me_ref[0], me_ref[1]
-    slots = members.shape[1]
+    slots = members.shape[0] * CAP
     taus = lag_ref.shape[0] // 2
     done = []
 
@@ -469,9 +486,9 @@
         done.append(pltpu.make_async_copy(source, target, out_sem.at[len(done)]))
         done[-1].start()
 
-    def keep(n, block):
+    def keep(d, block):
         if not final:
-            start(block, outs[2])
+            start(block, outs[2].at[d])
 
     full_lines, full_turned = lines, turned_ref
     if final:
@@ -481,14 +498,15 @@
         start(kept_turned, turned_ref.at[:, :turned_cut])
         lines, turned_ref = lines.at[cut:], turned_ref.at[:, turned_cut:]
     buffers = (x_ref, table_ref, scratch, members)
-    tiles = whiten_and_load([new], old, me, [x_hbm], ms, (table_hbm, mask_ref), buffers, (load, x_sem, sem), keep)
+    sems = (load, x_sem, sem)
+    tiles, copies = whiten_and_load([new], new, me, [x_hbm], m_hbm, (table_hbm, mask_ref), buffers, sems, keep)
     tile = tiles[new]
     column = jnp.broadcast_to(tile[0:1], (LANES, LANES)).T[:CAP]
 
     def emit(row, t, part):
         lines[pl.ds(pl.multiple_of((t * CAP + row) * taus, 8), taus), :] = part
 
-    pairs_body(me, [new], members, lag_ref, cross_ref, emit)
+    pairs_body(me, [new], members, lag_ref, cross_ref, copies, emit, lambda stop: None)
     if final:
         for c in done:
             c.wait()
@@ -502,24 +520,24 @@
 
 
 def step(me, x, table, mask, lags, ms, new, slots, groups, kept, after):
-    old = sorted(ms)
     taus = lags.shape[0] // 2
-    m, _ = member_shapes(x)
     final = len(kept) > 0
     count = 1 + (kept[0].shape[0] // (slots // LANES * CAP * taus) if final else 0)
     lines = jax.ShapeDtypeStruct((count * (slots // LANES) * CAP * taus, LANES), F32)
     turned = jax.ShapeDtypeStruct((groups, count * (taus // 8) * (slots // groups), LANES), F32)
+    members = jax.ShapeDtypeStruct(ms.shape, ms.dtype)
     return pl.pallas_call(
-        functools.partial(step_kernel, old, new, final),
-        out_shape=[lines, turned] + ([] if final else [m, ENERGY]),
-        in_specs=[IN_SMEM, IN_HBM, IN_VMEM, IN_VMEM] + [IN_HBM] * (1 + len(old) + len(kept) + len(after)),
+        functools.partial(step_kernel, new, final),
+        out_shape=[lines, turned] + ([] if final else [members, ENERGY]),
+        in_specs=[IN_SMEM, IN_HBM, IN_VMEM, IN_VMEM] + [IN_HBM] * (2 + len(kept) + len(after)),
         out_specs=[IN_HBM] * 2 + ([] if final else [IN_HBM, IN_VMEM]),
-        scratch_shapes=shared_scratch(x, [new], old, table, slots, CAP)
+        scratch_shapes=shared_scratch(x, [new], table, slots, CAP)
         + [pltpu.VMEM(lines.shape, F32), pltpu.VMEM(turned.shape, F32)],
         cost_estimate=LONG if final else SHORT,
+        input_output_aliases={} if final else {5: 2},
         compiler_params=pltpu.CompilerParams(vmem_limit_bytes=VMEM_LIMIT),
         name="step",
-    )(me, table, mask, lags, x, *[ms[d] for d in old], *kept, *after)
+    )(me, table, mask, lags, x, ms, *kept, *after)
 
 
 def hold_kernel(*refs):
@@ -542,7 +560,8 @@
 def finish_kernel(last, blocks, me_ref, *refs):
     out_hbm, out_ref, lines_sum, rows_ref, sem = refs[-5:]
     me, chan, own = me_ref[0], me_ref[1], me_ref[2]
-    rows, lags, slots = out_ref.shape
+    lags, rows, slots = out_hbm.shape
+    pitch = rows + PITCH_PAD
     tiles = slots // LANES
     groups = slots // rows
     taus = lag_rows()
@@ -623,25 +642,31 @@
                     line = jnp.concatenate([line] * tiles, axis=1)
                     value = jnp.where(block_of == jnp.bitwise_xor(me, d), line, value)
                 stop = min(8, lags - 8 * g)
-                out_ref[target, 8 * g : 8 * g + stop] = value[:stop]
+                for t in range(tiles):
+                    part = value[:stop, t * LANES : (t + 1) * LANES]
+                    if stop < 8:
+                        out_ref[t, 8 * g : 8 * g + stop, pl.ds(target, 1), :] = part.reshape(stop, 1, LANES)
+                    else:
+                        flat = out_ref.at[t].reshape(lags * pitch, LANES)
+                        flat[pl.ds(8 * g * pitch + target, stop, stride=pitch), :] = part
             return carry
 
         lax.fori_loop(0, CAP, one_row, 0, unroll=2)
 
+    @pl.when(own < groups - 1)
+    def _():
+        for h in range(blocks):
+            emit(h, True)
+
+    @pl.when(own == groups - 1)
+    def _():
+        for h in range(blocks):
+            emit(h, False)
+
     copies = []
-    for h in range(blocks):
-
-        @pl.when(own < groups - 1)
-        def _():
-            emit(h, True)
-
-        @pl.when(own == groups - 1)
-        def _():
-            emit(h, False)
-
-        b_row = jnp.bitwise_and(jnp.bitwise_xor(me, own * blocks + h), blocks - 1)
-        part = pl.ds(b_row * CAP, CAP)
-        copies.append(pltpu.make_async_copy(out_ref.at[part], out_hbm.at[part], sem.at[h]))
+    for t in range(tiles):
+        target = out_hbm.at[:, :, t * LANES : (t + 1) * LANES]
+        copies.append(pltpu.make_async_copy(out_ref.at[t, :, :rows], target, sem.at[t]))
         copies[-1].start()
     for c in copies:
         c.wait()
@@ -650,22 +675,23 @@
 def finish(me, base, late, turned, last, blocks):
     rows, taus, slots = base[0].shape
     groups = slots // rows
-    shape = (rows, 2 * MAXLAG + 1, slots)
-    return pl.pallas_call(
+    lags = 2 * MAXLAG + 1
+    out = pl.pallas_call(
         functools.partial(finish_kernel, last, blocks),
-        out_shape=jax.ShapeDtypeStruct(shape, F32),
+        out_shape=jax.ShapeDtypeStruct((lags, rows, slots), F32),
         in_specs=[IN_SMEM] + [IN_VMEM] * (3 * groups),
         out_specs=IN_HBM,
         scratch_shapes=[
-            pltpu.VMEM(shape, F32),
+            pltpu.VMEM((slots // LANES, lags, rows + PITCH_PAD, LANES), F32),
             pltpu.VMEM((len(last), taus // 8, rows, LANES), F32),
             pltpu.VMEM((groups, slots, LANES), F32),
-            pltpu.SemaphoreType.DMA((blocks,)),
+            pltpu.SemaphoreType.DMA((slots // LANES,)),
         ],
         cost_estimate=SHORT,
         compiler_params=pltpu.CompilerParams(vmem_limit_bytes=FINISH_LIMIT),
         name="finish",
     )(me, *base, *late, *turned)
+    return jnp.transpose(out, (1, 0, 2))
 
 
 def local(waveforms, family_of, channel_mask):
@@ -691,7 +717,7 @@
     last = list(range(owners - blocks, owners))
     early = [d for d in range(owners) if d not in last]
     first = list(range(half, half + blocks))
-    sends, inbox, ms, energy = {}, {}, {}, {}
+    sends, inbox = {}, {}
     widen = ((0, 0), (0, half_lanes - chans), (0, 0))
 
     def collect(dests, after):
@@ -705,44 +731,37 @@
 
     partners = list(range(groups - 1, 0, -1))
 
-    collect(first, [])
-    for d in first:
-        post(d)
-    collect(list(range(half)), [sends[first[0]]])
-    for d in range(1, half):
+    collect(list(range(half + blocks)), [])
+    for d in first + list(range(1, half)):
         post(d)
     inbox[0] = jnp.pad(sends[0], widen)
+    ms, energy = whiten({0: inbox[0]}, table, mask, owners, [], [])
+    ms, got = whiten({1: inbox[1]}, table, mask, owners, [ms], [])
+    energy.update(got)
     remaining = list(range(half + blocks, owners))
-    collect(remaining, [inbox[d] for d in range(1, half)])
+    collect(remaining, [got[1]] + [inbox[d] for d in range(1, half)])
     for d in remaining:
         post(d)
-    after = [sends[first[0]]]
+    after = [sends[remaining[0]]]
+    for start in range(2, half, 4):
+        ds = range(start, min(start + 4, half))
+        ms, got = whiten({d: inbox[d] for d in ds}, table, mask, owners, [ms], after)
+        energy.update(got)
+        after = []
+
     middle = [d for d in early if d >= half]
-    rest = [d for d in early if d < half]
-    for start in [0, 1] + list(range(4, half, 4)):
-        if start == 1:
-            after = after + [sends[remaining[0]]]
-        part = list(range(start, min({0: 1, 1: 4}.get(start, start + 4), half)))
-        got_m, got_e = whiten([inbox[d] for d in part], table, mask, after)
-        ms.update(zip(part, got_m))
-        energy.update(zip(part, got_e))
-        after = [got_e[0]]
-
     limit = max(1, 16 * 2**20 // (CAP * length * slots * 4))
     per_call = max(n for n in range(blocks, len(early) + 1, blocks) if len(early) % n == 0 and n <= max(limit, blocks))
-    held = {d: ms[d] for d in rest}
     filled = []
     for start in range(0, len(early), per_call):
         lines_of = early[start : start + per_call]
         xs = {d: inbox[d] for d in middle}
         more = int(start == 0)
-        result = square(me, xs, table, mask, lags, held, energy, lines_of, slots, groups, more, after, filled)
+        result = square(me, xs, table, mask, lags, ms, energy, lines_of, slots, groups, more, after, filled)
         filled = [result[0]]
+        after = [result[1]]
         if more:
-            known = dict(zip(middle, result[1:]))
-            ms.update(zip(middle, result[1 + len(middle) :]))
-            after = [result[1]]
-    energy.update(known)
+            ms = result[-1]
 
     def narrow(x):
         return (x * F16_SCALE).astype(jnp.float16)
@@ -756,8 +775,9 @@
         kept = result[:2]
         after = []
         if n < len(last) - 1:
-            ms[d], energy[d] = result[2:]
-    late, turned = hold(kept, [sum(sent[e][:8].astype(F32) for e in partners)])
+            ms = result[2]
+    late = kept[0]
+    (turned,) = hold(kept[1:], [sum(sent[e][:8].astype(F32) for e in partners)])
 
     def widen_f32(x, shape):
         return x.astype(F32).reshape(shape)

time: 182 us -> 161 us (0.88)
  waiting for transfers between devices: 54.1 us -> 37.7 us
  Pallas kernels: 86.5 us -> 81.1 us
    ppermute x7, waiting for transfers between devices: 40.3 us -> 26.4 us  [post(): lax.ppermute(sends[d], 'fam', [(i, i ^ d) for i in range(owners)])]
    pallas_call x1, Pallas kernels: 25.9 us -> 22 us  [square(): pl.pallas_call(functools.partial(square_kernel, old, new, lines_of, more)...]
    pallas_call x3 -> x2, Pallas kernels: 11 us -> 7.92 us  [gather(): pl.pallas_call(functools.partial(gather_kernel, owners, dests), out_shape...]
    ppermute x6, waiting for transfers between devices: 13.8 us -> 11.3 us  [chan_permute(): return lax.ppermute(x, 'chan', [(i, i ^ e) for i in range(groups)])]
    unnamed x22 -> x20, local copies, waits for them, and re-layouts: 3.73 us -> 5.32 us
    pallas_call x4 -> x5, Pallas kernels: 46.7 us -> 47.4 us  [the longest x2 26 us: step(): pl.pallas_call(functools.partial(step_kernel, new, final), out_shape=[lin...]
  transfers between devices with their start and end apart: 16 -> 16, of which waited for: 6 -> 5; matrix products, arithmetic and copies ran while one was open for 5% -> 7% of each run, Pallas kernels for 42% -> 45%
where the time goes in v2:
time: 161 us
  Pallas kernels  81.1 us (50%)
  waiting for transfers between devices  37.7 us (23%)
  starting transfers between devices  23.3 us (14%)
  other arithmetic  12 us (7%)
  local copies, waits for them, and re-layouts  5.92 us (4%)
    ppermute x7, waiting for transfers between devices, post(): lax.ppermute(sends[d], 'fam', [(i, i ^ d) for i in range(owners)])  26.4 us
    pallas_call x2, Pallas kernels, step(): pl.pallas_call(functools.partial(step_kernel, new, final), out_shape=[lin...  26 us
    pallas_call x1, Pallas kernels, square(): pl.pallas_call(functools.partial(square_kernel, old, new, lines_of, more)...  22 us
    pallas_call x3, Pallas kernels, whiten(): pl.pallas_call(functools.partial(whiten_kernel, ds), out_shape=[jax.Shape...  21.4 us
    ppermute x7, starting transfers between devices, post(): lax.ppermute(sends[d], 'fam', [(i, i ^ d) for i in range(owners)])  14.9 us
    ppermute x6, waiting for transfers between devices, chan_permute(): return lax.ppermute(x, 'chan', [(i, i ^ e) for i in range(groups)])  11.3 us
    pallas_call x2, Pallas kernels, gather(): pl.pallas_call(functools.partial(gather_kernel, owners, dests), out_shape...  7.92 us
    convert_element_type x3, other arithmetic, narrow(): return (x * F16_SCALE).astype(jnp.float16)  6.43 us
  transfers between devices with their start and end apart: 16, of which 5 were waited for; matrix products, arithmetic and copies ran while one was open for 7% of the time, Pallas kernels for 45%

profile of v2, /device:TPU:0, one launch (start us, length us, event | category | flops | bytes accessed | tf_op | source)
XLA Modules:
  0.0 160.5 jit_solution(594711096223347665)
XLA Ops:
  0.6 4.4 %gather_slots.2 = (bf16[16,64,256]{2,1,0:T(8,128)(2,1)}, bf16[16,64,256]{2,1,0:T(8,128)(2,1)}, bf16[16,64,256]{2,1,0:T(8,128)(2,1)}, bf16[16,64,256]{2,1,0:T(8,1...) custom-call(s32[4]{0:T(128)} %pad_add_fusion.me_ref, s32[128]{0:T(128)} %family_ref.3, ...), custom_call_target="tpu_custom_call" | custom-call | flops 1 | bytes 1 | tf_op jit(solution)/shard_map/gather_slots/pallas_call | solution.py:112
  5.0 3.1 %collective-permute-start.4 = (bf16[16,64,256]{2,1,0:T(8,128)(2,1)}, bf16[16,64,256]{2,1,0:T(8,128)(2,1)S(1)}, u32[]{:S(2)}, u32[]{:S(2)}) collective-permute-start(bf16[16,64,256]{2,1,0:T(8,128)(2,1)} %get-tuple-element.32), channel_id=1, source_target_pairs={{0,1},{1,0},{2,3},{3,2},{4,5},{5,4},{6,7},{7,6},{8,9},{9,8},{10,11... | collective-permute-start | bytes 1572872 | tf_op jit(solution)/shard_map/ppermute | solution.py:727
  8.1 1.6 collective-permute-start.2
  9.7 3.0 %collective-permute-start = (bf16[16,64,256]{2,1,0:T(8,128)(2,1)}, bf16[16,64,256]{2,1,0:T(8,128)(2,1)S(1)}, u32[]{:S(2)}, u32[]{:S(2)}) collective-permute-start(bf16[16,64,256]{2,1,0:T(8,128)(2,1)} %get-tuple-element.28), channel_id=1, source_target_pairs={{0,4},{1,5},{2,6},{3,7},{4,0},{5,1},{6,2},{7,3},{8,12},{9,13},{10,... | collective-permute-start | bytes 1572872 | tf_op jit(solution)/shard_map/ppermute | solution.py:727
  12.6 1.3 collective-permute-start.1
  14.5 6.1 %whiten.3 = (bf16[8,128,16,256]{3,2,1,0:T(8,128)(2,1)}, f32[8,128]{1,0:T(8,128)}) custom-call(bf16[512,256]{1,0:T(8,128)(2,1)} %constant.32.clone.table_hbm, f32[1,256]{1,0:T(1,128)} %tile.13.mask_ref, bf16[16,64,256]{2,1,0:T(8,128)(2,1)} %get-tuple-element.33.refs_0_), custom_call_target="tpu_custom_call" | custom-call | flops 1 | bytes 1 | tf_op jit(solution)/shard_map/whiten/pallas_call | solution.py:238
  21.5 6.1 %whiten.4 = (bf16[8,128,16,256]{3,2,1,0:T(8,128)(2,1)}, f32[8,128]{1,0:T(8,128)}) custom-call(bf16[512,256]{1,0:T(8,128)(2,1)} %constant.32.clone.table_hbm, f32[1,256]{1,0:T(1,128)} %tile.13.mask_ref, bf16[16,64,256]{2,1,0:T(8,128)(2,1)} %copy-done.2, bf16[8,128,16,256]{3,2,1,0:T(8,128)(2,1)} %get-tuple-element.34.refs_1_), custom_call_target="tpu_custom_call", output_to_operand_aliasing={{0}: (3, {})} | custom-call | flops 1 | bytes 1 | tf_op jit(solution)/shard_map/whiten/pallas_call | solution.py:238
  27.6 17.8 %collective-permute-done.2.rest_2_.refs_0_ = bf16[16,64,256]{2,1,0:T(8,128)(2,1)S(1)} collective-permute-done((bf16[16,64,256]{2,1,0:T(8,128)(2,1)}, bf16[16,64,256]{2,1,0:T(8,128)(2,1)S(1)}, u32[]{:S(2)}, u32[]{:S(2)}) %collective-permute-start.2) | collective-permute-done | bytes 524320 | tf_op jit(solution)/shard_map/ppermute | solution.py:727
  45.4 8.6 %collective-permute-done.3.rest_3_.refs_1_ = bf16[16,64,256]{2,1,0:T(8,128)(2,1)S(1)} collective-permute-done((bf16[16,64,256]{2,1,0:T(8,128)(2,1)}, bf16[16,64,256]{2,1,0:T(8,128)(2,1)S(1)}, u32[]{:S(2)}, u32[]{:S(2)}) %collective-permute-start.3) | collective-permute-done | bytes 524320 | tf_op jit(solution)/shard_map/ppermute | solution.py:727
  54.7 3.5 %gather_slots.3 = (bf16[16,64,256]{2,1,0:T(8,128)(2,1)}, bf16[16,64,256]{2,1,0:T(8,128)(2,1)}) custom-call(s32[4]{0:T(128)} %pad_add_fusion.me_ref, s32[128]{0:T(128)} %family_ref.3, bf16[128,64,256]{2,1,0:T(8,128)(2,1)} %wave_ref.3, f32[8,128]{1,0:T(8,128)} %get-tuple-element.35.rest_0_.refs_4_, bf16[16,64,256]{2,1,0:T(8,128)(2,1)} %copy-done.2, ...), custom_call_target="tpu_custom_call" | custom-call | flops 1 | bytes 1 | tf_op jit(solution)/shard_map/gather_slots/pallas_call | solution.py:112
  58.2 1.4 collective-permute-start.9
  59.7 4.6 %collective-permute-start.8 = (bf16[16,64,256]{2,1,0:T(8,128)(2,1)}, bf16[16,64,256]{2,1,0:T(8,128)(2,1)S(1)}, u32[]{:S(2)}, u32[]{:S(2)}) collective-permute-start(bf16[16,64,256]{2,1,0:T(8,128)(2,1)} %get-tuple-element.43), channel_id=1, source_target_pairs={{0,7},{1,6},{2,5},{3,4},{4,3},{5,2},{6,1},{7,0},{8,15},{9,14},{10,... | collective-permute-start | bytes 1572872 | tf_op jit(solution)/shard_map/ppermute | solution.py:727
  64.2 9.1 %whiten.5 = (bf16[8,128,16,256]{3,2,1,0:T(8,128)(2,1)}, f32[8,128]{1,0:T(8,128)}, f32[8,128]{1,0:T(8,128)}) custom-call(bf16[512,256]{1,0:T(8,128)(2,1)} %constant.32.clone.table_hbm, f32[1,256]{1,0:T(1,128)} %tile.13.mask_ref, bf16[16,64,256]{2,1,0:T(8,128)(2,1)} %copy-done.3, bf16[16,64,256]{2,1,0:T(8,128)(2,1)} %copy-done.4, ...), custom_call_target="tpu_custom_call", output_to_operand_aliasing={{0}: (5, {})} | custom-call | flops 1 | bytes 1 | tf_op jit(solution)/shard_map/whiten/pallas_call | solution.py:238
  74.4 22.0 %square.1 = (f32[4,32,72,128]{3,2,1,0:T(8,128)}, f32[8,128]{1,0:T(8,128)}, f32[8,128]{1,0:T(8,128)}, bf16[8,128,16,256]{3,2,1,0:T(8,128)(2,1)}) custom-call(s32[4]{0:T(128)} %pad_add_fusion.me_ref, bf16[512,256]{1,0:T(8,128)(2,1)} %constant.32.clone.table_hbm, f32[1,256]{1,0:T(1,128)} %tile.13.mask_ref, ...), custom_call_target="tpu_custom_call", output_to_operand_aliasing={{3}: (6, {})} | custom-call | flops 1 | bytes 1 | tf_op jit(solution)/shard_map/square/pallas_call | solution.py:460
  96.3 3.7 %multiply_convert_fusion.1 = (f16[1,32,72,128]{3,2,1,0:T(8,128)(2,1)}, f16[1,32,72,128]{3,2,1,0:T(8,128)(2,1)}, f16[1,32,72,128]{3,2,1,0:T(8,128)(2,1)}, f32[32,72,128]{2,1,0:T(8,128)S(1)}) fusion(f32[4,32,72,128]{3,2,1,0:T(8,128)} %get-tuple-element.42), kind=kLoop, calls=%fused_computation.1 | loop fusion | flops 1769472 | bytes 7667712 | tf_op jit(solution)/shard_map/convert_element_type | solution.py:767
  100.1 1.4 collective-permute-start.6
  102.8 12.9 %step.2 = (f32[1152,128]{1,0:T(8,128)}, f32[4,288,128]{2,1,0:T(8,128)}, bf16[8,128,16,256]{3,2,1,0:T(8,128)(2,1)}, f32[8,128]{1,0:T(8,128)}) custom-call(s32[4]{0:T(128)} %pad_add_fusion.me_ref, bf16[512,256]{1,0:T(8,128)(2,1)} %constant.32.clone.table_hbm, f32[1,256]{1,0:T(1,128)} %tile.13.mask_ref, ...), custom_call_target="tpu_custom_call", output_to_operand_aliasing={{2}: (5, {})} | custom-call | flops 1 | bytes 1 | tf_op jit(solution)/shard_map/step/pallas_call | solution.py:529
  116.5 13.1 %step.3 = (f32[2304,128]{1,0:T(8,128)}, f32[4,576,128]{2,1,0:T(8,128)}) custom-call(s32[4]{0:T(128)} %pad_add_fusion.me_ref, bf16[512,256]{1,0:T(8,128)(2,1)} %constant.32.clone.table_hbm, f32[1,256]{1,0:T(1,128)} %tile.13.mask_ref, bf16[144,256]{1,0:T(8,128)(2,1)} %constant.33.clone.lag_ref, bf16[16,64,256]{2,1,0:T(8,128)(2,1)} %copy-done.8, ...), custom_call_target="tpu_custom_call" | custom-call | flops 100000000376832 | bytes 1 | tf_op jit(solution)/shard_map/step/pallas_call | solution.py:529
  129.6 1.4 multiply_convert_fusion
  132.4 4.5 %collective-permute-start.12 = (f16[2304,128]{1,0:T(8,128)(2,1)S(1)}, f16[2304,128]{1,0:T(8,128)(2,1)S(1)}, u32[]{:S(2)}, u32[]{:S(2)}) collective-permute-start(f16[2304,128]{1,0:T(8,128)(2,1)S(1)} %multiply_convert_fusion), channel_id=1, source_target_pairs={{0,24},{1,25},{10,18},{11,19},{20,12},{21,13},{30,6},{31,7}} | collective-permute-start | bytes 1769480 | tf_op jit(solution)/shard_map/ppermute | solution.py:793
  138.2 1.3 fusion.5
  144.9 8.5 %collective-permute-done.14 = f16[576,128]{1,0:T(8,128)(2,1)S(1)} collective-permute-done((f16[576,128]{1,0:T(8,128)(2,1)S(1)}, f16[576,128]{1,0:T(8,128)(2,1)S(1)}, u32[]{:S(2)}, u32[]{:S(2)}) %collective-permute-start.14) | collective-permute-done | bytes 147488 | tf_op jit(solution)/shard_map/ppermute | solution.py:730
  153.4 1.6 collective-permute-done.15
  156.5 3.9 %finish.1 = f32[65,32,128]{2,1,0:T(8,128)} custom-call(s32[4]{0:T(128)S(1)} %copy-done.1, f32[32,72,128]{2,1,0:T(8,128)S(1)} %get-tuple-element.54.refs_0_, f32[32,72,128]{2,1,0:T(8,128)S(1)} %convert.3.refs_1_, f32[32,72,128]{2,1,0:T(8,128)S(1)} %convert.4.refs_2_, f32[32,72,128]{2,1,0:T(8,128)S(1)} %convert.5.refs_3_, f32[2304,128]{1,0:T(8,128)S(1)} %copy-done, ...), custom_call_target="tpu_custom_call" | custom-call | flops 1 | bytes 1 | tf_op jit(solution)/shard_map/finish/pallas_call | solution.py:679
  (55 shorter events, 15.3 us)
Async XLA Ops:
  0.6 13.4 %copy-start.9 = (s32[1,64]{1,0:T(1,128)S(1)}, s32[1,64]{1,0:T(1,128)}, u32[]{:S(2)}) copy-start(s32[1,64]{1,0:T(1,128)} %param.7) | copy-start | bytes 772
  5.0 15.7 %collective-permute-start.4 = (bf16[16,64,256]{2,1,0:T(8,128)(2,1)}, bf16[16,64,256]{2,1,0:T(8,128)(2,1)S(1)}, u32[]{:S(2)}, u32[]{:S(2)}) collective-permute-start(bf16[16,64,256]{2,1,0:T(8,128)(2,1)} %get-tuple-element.32), channel_id=1, source_target_pairs={{0,1},{1,0},{2,3},{3,2},{4,5},{5,4},{6,7},{7,6},{8,9},{9,8},{10,11... | collective-permute-start | bytes 1572872 | tf_op jit(solution)/shard_map/ppermute | solution.py:727
  8.1 37.3 %collective-permute-start.2 = (bf16[16,64,256]{2,1,0:T(8,128)(2,1)}, bf16[16,64,256]{2,1,0:T(8,128)(2,1)S(1)}, u32[]{:S(2)}, u32[]{:S(2)}) collective-permute-start(bf16[16,64,256]{2,1,0:T(8,128)(2,1)} %get-tuple-element.30), channel_id=1, source_target_pairs={{0,2},{1,3},{2,0},{3,1},{4,6},{5,7},{6,4},{7,5},{8,10},{9,11},{10,... | collective-permute-start | bytes 1572872 | tf_op jit(solution)/shard_map/ppermute | solution.py:727
  9.7 44.3 %collective-permute-start.3 = (bf16[16,64,256]{2,1,0:T(8,128)(2,1)}, bf16[16,64,256]{2,1,0:T(8,128)(2,1)S(1)}, u32[]{:S(2)}, u32[]{:S(2)}) collective-permute-start(bf16[16,64,256]{2,1,0:T(8,128)(2,1)} %get-tuple-element.31), channel_id=1, source_target_pairs={{0,3},{1,2},{2,1},{3,0},{4,7},{5,6},{6,5},{7,4},{8,11},{9,10},{10,... | collective-permute-start | bytes 1572872 | tf_op jit(solution)/shard_map/ppermute | solution.py:727
  9.7 63.7 %collective-permute-start = (bf16[16,64,256]{2,1,0:T(8,128)(2,1)}, bf16[16,64,256]{2,1,0:T(8,128)(2,1)S(1)}, u32[]{:S(2)}, u32[]{:S(2)}) collective-permute-start(bf16[16,64,256]{2,1,0:T(8,128)(2,1)} %get-tuple-element.28), channel_id=1, source_target_pairs={{0,4},{1,5},{2,6},{3,7},{4,0},{5,1},{6,2},{7,3},{8,12},{9,13},{10,... | collective-permute-start | bytes 1572872 | tf_op jit(solution)/shard_map/ppermute | solution.py:727
  12.6 60.8 %collective-permute-start.1 = (bf16[16,64,256]{2,1,0:T(8,128)(2,1)}, bf16[16,64,256]{2,1,0:T(8,128)(2,1)S(1)}, u32[]{:S(2)}, u32[]{:S(2)}) collective-permute-start(bf16[16,64,256]{2,1,0:T(8,128)(2,1)} %get-tuple-element.29), channel_id=1, source_target_pairs={{0,5},{1,4},{2,7},{3,6},{4,1},{5,0},{6,3},{7,2},{8,13},{9,12},{10,... | collective-permute-start | bytes 1572872 | tf_op jit(solution)/shard_map/ppermute | solution.py:727
  20.7 0.8 copy-start.2
  45.4 8.6 %copy-start.3 = (bf16[16,64,256]{2,1,0:T(8,128)(2,1)}, bf16[16,64,256]{2,1,0:T(8,128)(2,1)S(1)}, u32[]{:S(2)}) copy-start(bf16[16,64,256]{2,1,0:T(8,128)(2,1)S(1)} %collective-permute-done.2.rest_2_.refs_0_) | copy-start | bytes 1572868
  58.2 43.7 %collective-permute-start.9 = (bf16[16,64,256]{2,1,0:T(8,128)(2,1)}, bf16[16,64,256]{2,1,0:T(8,128)(2,1)S(1)}, u32[]{:S(2)}, u32[]{:S(2)}) collective-permute-start(bf16[16,64,256]{2,1,0:T(8,128)(2,1)} %get-tuple-element.36.refs_2_), channel_id=1, source_target_pairs={{0,6},{1,7},{2,4},{3,5},{4,2},{5,3},{6,0},{7,1},{8,14},{9,15},{10,... | collective-permute-start | bytes 1572872 | tf_op jit(solution)/shard_map/ppermute | solution.py:727
  59.7 56.0 %collective-permute-start.8 = (bf16[16,64,256]{2,1,0:T(8,128)(2,1)}, bf16[16,64,256]{2,1,0:T(8,128)(2,1)S(1)}, u32[]{:S(2)}, u32[]{:S(2)}) collective-permute-start(bf16[16,64,256]{2,1,0:T(8,128)(2,1)} %get-tuple-element.43), channel_id=1, source_target_pairs={{0,7},{1,6},{2,5},{3,4},{4,3},{5,2},{6,1},{7,0},{8,15},{9,14},{10,... | collective-permute-start | bytes 1572872 | tf_op jit(solution)/shard_map/ppermute | solution.py:727
  73.4 0.9 copy-start.6
  100.0 32.4 %collective-permute-start.5 = (f16[2304,128]{1,0:T(8,128)(2,1)}, f16[2304,128]{1,0:T(8,128)(2,1)}, u32[]{:S(2)}, u32[]{:S(2)}) collective-permute-start(f16[2304,128]{1,0:T(8,128)(2,1)} %bitcast.6), channel_id=1, source_target_pairs={{0,8},{8,0},{16,24},{24,16},{1,9},{9,1},{17,25},{25,17},{2,10},{10... | collective-permute-start | bytes 1769480 | tf_op jit(solution)/shard_map/ppermute | solution.py:730
  100.1 36.8 %collective-permute-start.6 = (f16[2304,128]{1,0:T(8,128)(2,1)}, f16[2304,128]{1,0:T(8,128)(2,1)}, u32[]{:S(2)}, u32[]{:S(2)}) collective-permute-start(f16[2304,128]{1,0:T(8,128)(2,1)} %bitcast.8), channel_id=1, source_target_pairs={{0,16},{8,24},{16,0},{24,8},{1,17},{9,25},{17,1},{25,9},{2,18},{10... | collective-permute-start | bytes 1769480 | tf_op jit(solution)/shard_map/ppermute | solution.py:730
  101.5 35.4 %collective-permute-start.7 = (f16[2304,128]{1,0:T(8,128)(2,1)}, f16[2304,128]{1,0:T(8,128)(2,1)}, u32[]{:S(2)}, u32[]{:S(2)}) collective-permute-start(f16[2304,128]{1,0:T(8,128)(2,1)} %bitcast.10), channel_id=1, source_target_pairs={{0,24},{8,16},{16,8},{24,0},{1,25},{9,17},{17,9},{25,1},{2,26},{10... | collective-permute-start | bytes 1769480 | tf_op jit(solution)/shard_map/ppermute | solution.py:730
  101.9 0.8 copy-start.7
  115.7 0.8 copy-start.8
  131.0 24.0 %collective-permute-start.10 = (f16[2304,128]{1,0:T(8,128)(2,1)S(1)}, f16[2304,128]{1,0:T(8,128)(2,1)S(1)}, u32[]{:S(2)}, u32[]{:S(2)}) collective-permute-start(f16[2304,128]{1,0:T(8,128)(2,1)S(1)} %multiply_convert_fusion), channel_id=1, source_target_pairs={{16,24},{17,25},{26,18},{27,19},{4,12},{5,13},{14,6},{15,7}} | collective-permute-start | bytes 1769480 | tf_op jit(solution)/shard_map/ppermute | solution.py:793
  131.7 23.4 %collective-permute-start.11 = (f16[2304,128]{1,0:T(8,128)(2,1)S(1)}, f16[2304,128]{1,0:T(8,128)(2,1)S(1)}, u32[]{:S(2)}, u32[]{:S(2)}) collective-permute-start(f16[2304,128]{1,0:T(8,128)(2,1)S(1)} %multiply_convert_fusion), channel_id=1, source_target_pairs={{8,24},{9,25},{2,18},{3,19},{28,12},{29,13},{22,6},{23,7}} | collective-permute-start | bytes 1769480 | tf_op jit(solution)/shard_map/ppermute | solution.py:793
  132.4 22.8 %collective-permute-start.12 = (f16[2304,128]{1,0:T(8,128)(2,1)S(1)}, f16[2304,128]{1,0:T(8,128)(2,1)S(1)}, u32[]{:S(2)}, u32[]{:S(2)}) collective-permute-start(f16[2304,128]{1,0:T(8,128)(2,1)S(1)} %multiply_convert_fusion), channel_id=1, source_target_pairs={{0,24},{1,25},{10,18},{11,19},{20,12},{21,13},{30,6},{31,7}} | collective-permute-start | bytes 1769480 | tf_op jit(solution)/shard_map/ppermute | solution.py:793
  139.5 1.4 collective-permute-start.13
  139.6 13.8 %collective-permute-start.14 = (f16[576,128]{1,0:T(8,128)(2,1)S(1)}, f16[576,128]{1,0:T(8,128)(2,1)S(1)}, u32[]{:S(2)}, u32[]{:S(2)}) collective-permute-start(f16[576,128]{1,0:T(8,128)(2,1)S(1)} %get-tuple-element.56), channel_id=1, source_target_pairs={{0,16},{8,24},{16,0},{24,8},{1,17},{9,25},{17,1},{25,9},{2,18},{10... | collective-permute-start | bytes 442376 | tf_op jit(solution)/shard_map/ppermute | solution.py:730
  140.9 14.0 %collective-permute-start.15 = (f16[576,128]{1,0:T(8,128)(2,1)S(1)}, f16[576,128]{1,0:T(8,128)(2,1)S(1)}, u32[]{:S(2)}, u32[]{:S(2)}) collective-permute-start(f16[576,128]{1,0:T(8,128)(2,1)S(1)} %get-tuple-element.55), channel_id=1, source_target_pairs={{0,24},{8,16},{16,8},{24,0},{1,25},{9,17},{17,9},{25,1},{2,26},{10... | collective-permute-start | bytes 442376 | tf_op jit(solution)/shard_map/ppermute | solution.py:730
  155.2 1.3 copy-start
  155.2 1.3 copy-start.1
  (2 other events, 1.6 us)

commit v3 on v2

--- a/solution.py
+++ b/solution.py
@@ -10,13 +10,14 @@
 from jax.sharding import PartitionSpec as P
 
 MAXLAG = 32
+LAGS = 2 * MAXLAG + 1
 CAP = 16
 LANES = 128
 F16_SCALE = 16384.0
 TINY = 1.2e-38
 VMEM_LIMIT = 56 * 2**20
 PITCH_PAD = 8
-LOAD_PARTS = 4
+LOAD_PARTS = 1
 LONG = pl.CostEstimate(flops=10**14, bytes_accessed=1, transcendentals=0)
 SHORT = pl.CostEstimate(flops=1, bytes_accessed=1, transcendentals=0)
 FINISH_LIMIT = 40 * 2**20
@@ -277,8 +278,12 @@
         low = left[:, LANES:]
         left = jnp.concatenate([high, turn(high), low, turn(low)], axis=0)
         right = jnp.concatenate([both[:, :LANES], both[:, LANES:]], axis=0)
-        out = dot_rows(left, right)
-        total = out[: 2 * n, :slots] + (out[: 2 * n, slots:] + out[2 * n :, :slots])
+        if n <= 32:
+            out = dot_rows(left, right)
+            total = out[: 2 * n, :slots] + (out[: 2 * n, slots:] + out[2 * n :, :slots])
+        else:
+            out = dot_rows(left[: 2 * n], right)
+            total = out[:, :slots] + (out[:, slots:] + dot_rows(left[2 * n :], right[:slots]))
         for q in range(2):
             for t in range(tiles):
                 part = total[q * n : (q + 1) * n, t * LANES : (t + 1) * LANES]
@@ -288,7 +293,7 @@
     step = bins // LOAD_PARTS
     for p in range(LOAD_PARTS):
         copies[p].wait()
-        lax.fori_loop(p * step, (p + 1) * step, cross, 0, unroll=16)
+        lax.fori_loop(p * step, (p + 1) * step, cross, 0, unroll=32 if n <= 32 else 16)
     table = table_ref[...]
 
     def lag(i, carry):
@@ -309,7 +314,7 @@
 
 
 def turn_lines(lines, codes, chan, turned, taus):
-    tiles = lines.shape[0] // (CAP * taus)
+    tiles = lines.shape[0] // (CAP * LAGS)
     groups, parts = turned.shape[0], taus // 8
     rows = turned.shape[1] // parts
     for g in range(parts):
@@ -318,7 +323,7 @@
             for u in range(7, -1, -1):
                 tau = 2 * MAXLAG - 8 * g - u
                 if tau >= 0:
-                    pieces.append(lines[pl.ds(t * CAP * taus + tau, CAP, stride=taus), :])
+                    pieces.append(lines[pl.ds(t * CAP * LAGS + tau, CAP, stride=LAGS), :])
                 else:
                     pieces.append(codes[min(-tau, len(codes)) - 1])
             value = jnp.concatenate(pieces, axis=0).T
@@ -490,13 +495,12 @@
         if not final:
             start(block, outs[2].at[d])
 
-    full_lines, full_turned = lines, turned_ref
+    full_turned = turned_ref
     if final:
-        kept_lines, kept_turned = refs[:2]
-        cut, turned_cut = kept_lines.shape[0], kept_turned.shape[1]
-        start(kept_lines, lines.at[:cut])
+        kept_turned = refs[0]
+        turned_cut = kept_turned.shape[1]
         start(kept_turned, turned_ref.at[:, :turned_cut])
-        lines, turned_ref = lines.at[cut:], turned_ref.at[:, turned_cut:]
+        turned_ref = turned_ref.at[:, turned_cut:]
     buffers = (x_ref, table_ref, scratch, members)
     sems = (load, x_sem, sem)
     tiles, copies = whiten_and_load([new], new, me, [x_hbm], m_hbm, (table_hbm, mask_ref), buffers, sems, keep)
@@ -504,7 +508,7 @@
     column = jnp.broadcast_to(tile[0:1], (LANES, LANES)).T[:CAP]
 
     def emit(row, t, part):
-        lines[pl.ds(pl.multiple_of((t * CAP + row) * taus, 8), taus), :] = part
+        lines[pl.ds((t * CAP + row) * LAGS, LAGS), :] = part[:LAGS]
 
     pairs_body(me, [new], members, lag_ref, cross_ref, copies, emit, lambda stop: None)
     if final:
@@ -512,19 +516,19 @@
             c.wait()
     else:
         outs[3][...] = tile
-    start(full_lines, outs[0])
+    start(lines, outs[0])
     turn_lines(lines, code_of(column), chan, turned_ref, taus)
     start(full_turned, outs[1])
-    for c in done[2:] if final else done:
+    for c in done[1:] if final else done:
         c.wait()
 
 
 def step(me, x, table, mask, lags, ms, new, slots, groups, kept, after):
     taus = lags.shape[0] // 2
     final = len(kept) > 0
-    count = 1 + (kept[0].shape[0] // (slots // LANES * CAP * taus) if final else 0)
-    lines = jax.ShapeDtypeStruct((count * (slots // LANES) * CAP * taus, LANES), F32)
-    turned = jax.ShapeDtypeStruct((groups, count * (taus // 8) * (slots // groups), LANES), F32)
+    parts = taus // 8 * (slots // groups)
+    lines = jax.ShapeDtypeStruct((slots // LANES * CAP * LAGS, LANES), F32)
+    turned = jax.ShapeDtypeStruct((groups, parts + (kept[0].shape[1] if final else 0), LANES), F32)
     members = jax.ShapeDtypeStruct(ms.shape, ms.dtype)
     return pl.pallas_call(
         functools.partial(step_kernel, new, final),
@@ -566,7 +570,8 @@
     groups = slots // rows
     taus = lag_rows()
     parts = taus // 8
-    base, late, turned = refs[:groups], refs[groups : 2 * groups], refs[2 * groups : 3 * groups]
+    base, turned = refs[:groups], refs[groups : 2 * groups]
+    late = [refs[(2 + n) * groups : (3 + n) * groups] for n in range(len(last))]
     scale = [1.0] + [1.0 / F16_SCALE] * (groups - 1)
     lane = lax.broadcasted_iota(jnp.int32, (8, LANES), 1)
 
@@ -621,29 +626,26 @@
             weight = []
             for e in range(groups):
                 row = rows_ref[e, pl.ds(slot, 1), :]
-                weight.append(jnp.concatenate([row] * tiles, axis=1) * every[e][0:1])
+                weight.append(jnp.concatenate([row] * tiles, axis=1) * every[e])
             for g in range(parts):
+                stop = min(8, lags - 8 * g)
                 value = 0.0
                 for e in range(groups):
                     if from_base:
-                        part = base[e][h * CAP + r, 8 * g : 8 * g + 8]
+                        part = base[e][h * CAP + r, 8 * g : 8 * g + stop]
                     else:
-                        pieces = []
-                        for t in range(tiles):
-                            start = pl.multiple_of(((h * tiles + t) * CAP + r) * taus + 8 * g, 8)
-                            pieces.append(late[e][pl.ds(start, 8), :])
+                        pieces = [late[h][e][pl.ds((t * CAP + r) * LAGS + 8 * g, stop), :] for t in range(tiles)]
                         part = jnp.concatenate(pieces, axis=1)
-                    value = value + part * weight[e]
+                    value = value + part * weight[e][:stop]
                 for n, d in enumerate(last):
                     if not from_base and d <= d_late:
                         continue
                     line = jnp.broadcast_to(lines_sum[n, g, pl.ds(target, 1), :], (8, LANES))
-                    line = pltpu.roll(line, 0, 1, stride=CAP, stride_axis=0)
+                    line = pltpu.roll(line, 0, 1, stride=CAP, stride_axis=0)[:stop]
                     line = jnp.concatenate([line] * tiles, axis=1)
-                    value = jnp.where(block_of == jnp.bitwise_xor(me, d), line, value)
-                stop = min(8, lags - 8 * g)
+                    value = jnp.where(block_of[:stop] == jnp.bitwise_xor(me, d), line, value)
                 for t in range(tiles):
-                    part = value[:stop, t * LANES : (t + 1) * LANES]
+                    part = value[:, t * LANES : (t + 1) * LANES]
                     if stop < 8:
                         out_ref[t, 8 * g : 8 * g + stop, pl.ds(target, 1), :] = part.reshape(stop, 1, LANES)
                     else:
@@ -672,14 +674,14 @@
         c.wait()
 
 
-def finish(me, base, late, turned, last, blocks):
+def finish(me, base, turned, late, last, blocks):
     rows, taus, slots = base[0].shape
     groups = slots // rows
     lags = 2 * MAXLAG + 1
     out = pl.pallas_call(
         functools.partial(finish_kernel, last, blocks),
         out_shape=jax.ShapeDtypeStruct((lags, rows, slots), F32),
-        in_specs=[IN_SMEM] + [IN_VMEM] * (3 * groups),
+        in_specs=[IN_SMEM] + [IN_VMEM] * ((2 + len(last)) * groups),
         out_specs=IN_HBM,
         scratch_shapes=[
             pltpu.VMEM((slots // LANES, lags, rows + PITCH_PAD, LANES), F32),
@@ -690,7 +692,7 @@
         cost_estimate=SHORT,
         compiler_params=pltpu.CompilerParams(vmem_limit_bytes=FINISH_LIMIT),
         name="finish",
-    )(me, *base, *late, *turned)
+    )(me, *base, *turned, *[x for rows_of in late for x in rows_of])
     return jnp.transpose(out, (1, 0, 2))
 
 
@@ -769,34 +771,30 @@
     early_rows = filled[0].reshape(groups, rows * taus, slots)
     sent = {e: chan_permute(narrow(early_rows[e]), e) for e in partners}
 
-    kept = []
+    def to_owner(x, e):
+        moves = []
+        for f in range(owners):
+            owner = (f // blocks) ^ (groups - 1)
+            moves.append(((owner ^ e) * owners + f, owner * owners + f))
+        return lax.ppermute(x, ("chan", "fam"), moves)
+
+    kept, late = [], []
     for n, d in enumerate(last):
         result = step(me, inbox[d], table, mask, lags, ms, d, slots, groups, kept, after)
-        kept = result[:2]
-        after = []
+        kept, after = [result[1]], []
+        small = narrow(result[0])
+        late.append([result[0]] + [to_owner(small, e) for e in range(1, groups)])
         if n < len(last) - 1:
             ms = result[2]
-    late = kept[0]
-    (turned,) = hold(kept[1:], [sum(sent[e][:8].astype(F32) for e in partners)])
-
-    def widen_f32(x, shape):
-        return x.astype(F32).reshape(shape)
-
-    base_parts, late_parts, turned_parts = [filled[0][0]], [late], [turned[0]]
-    small = narrow(late)
-    got_late, got_turned = {}, {}
-    for e in partners:
-        to_owner = []
-        for f in range(owners):
-            owner = (f // blocks) ^ (groups - 1)
-            to_owner.append(((owner ^ e) * owners + f, owner * owners + f))
-        got_late[e] = lax.ppermute(small, ("chan", "fam"), to_owner).astype(F32)
-        got_turned[e] = chan_permute(narrow(turned[e]), e).astype(F32)
+    there = [sent[e] for e in partners] + [x for rows_of in late[:-1] for x in rows_of[1:]]
+    (turned,) = hold(kept, [sum(x[:8, :LANES].astype(F32) for x in there)])
+
+    base_parts, turned_parts = [filled[0][0]], [turned[0]]
     for e in range(1, groups):
-        base_parts.append(widen_f32(sent[e], (rows, taus, slots)))
-        late_parts.append(got_late[e])
-        turned_parts.append(got_turned[e])
-    return finish(me, base_parts, late_parts, turned_parts, last, blocks)[None]
+        base_parts.append(sent[e].astype(F32).reshape(rows, taus, slots))
+        turned_parts.append(chan_permute(narrow(turned[e]), e).astype(F32))
+    late = [[x.astype(F32) for x in rows_of] for rows_of in late]
+    return finish(me, base_parts, turned_parts, late, last, blocks)[None]
 
 
 def solution(mesh):

time: 161 us -> 152 us (0.944)
  waiting for transfers between devices: 37.7 us -> 27.6 us
  Pallas kernels: 81.1 us -> 74.6 us
  starting transfers between devices: 23.3 us -> 28.7 us
  other arithmetic: 12 us -> 15.5 us
  local copies, waits for them, and re-layouts: 5.92 us -> 3.99 us
    ppermute x6, waiting for transfers between devices: 11.3 us -> 1.38 us  [chan_permute(): return lax.ppermute(x, 'chan', [(i, i ^ e) for i in range(groups)])]
    pallas_call x2, Pallas kernels: 26 us -> 21.2 us  [step(): pl.pallas_call(functools.partial(step_kernel, new, final), out_shape=[lin...]
    ppermute x3 -> x6, starting transfers between devices: 5.86 us -> 9.85 us  [to_owner(): return lax.ppermute(x, ('chan', 'fam'), moves)]
    unnamed x20 -> x22, local copies, waits for them, and re-layouts: 5.32 us -> 3.36 us
    convert_element_type x6 -> x9, other arithmetic: 0.3 us -> 2.19 us  [the longest x6 2.13 us: local(): late = [[x.astype(F32) for x in rows_of] for rows_of in late]]
    pallas_call x1, Pallas kernels: 22 us -> 20.2 us  [square(): pl.pallas_call(functools.partial(square_kernel, old, new, lines_of, more)...]
    convert_element_type x3 -> x4, other arithmetic: 6.43 us -> 7.94 us  [narrow(): return (x * F16_SCALE).astype(jnp.float16)]
  transfers between devices with their start and end apart: 16 -> 19, of which waited for: 5 -> 3; matrix products, arithmetic and copies ran while one was open for 7% -> 10% of each run, Pallas kernels for 45% -> 44%
where the time goes in v3:
time: 152 us; the launch traced here: 151 us
  Pallas kernels  74.6 us (49%)
  starting transfers between devices  28.7 us (19%)
  waiting for transfers between devices  27.6 us (18%)
  other arithmetic  15.5 us (10%)
  local copies, waits for them, and re-layouts  3.99 us (3%)
    ppermute x7, waiting for transfers between devices, post(): lax.ppermute(sends[d], 'fam', [(i, i ^ d) for i in range(owners)])  26.2 us
    pallas_call x3, Pallas kernels, whiten(): pl.pallas_call(functools.partial(whiten_kernel, ds), out_shape=[jax.Shape...  21.3 us
    pallas_call x2, Pallas kernels, step(): pl.pallas_call(functools.partial(step_kernel, new, final), out_shape=[lin...  21.2 us
    pallas_call x1, Pallas kernels, square(): pl.pallas_call(functools.partial(square_kernel, old, new, lines_of, more)...  20.2 us
    ppermute x7, starting transfers between devices, post(): lax.ppermute(sends[d], 'fam', [(i, i ^ d) for i in range(owners)])  15 us
    ppermute x6, starting transfers between devices, to_owner(): return lax.ppermute(x, ('chan', 'fam'), moves)  9.85 us
    pallas_call x2, Pallas kernels, gather(): pl.pallas_call(functools.partial(gather_kernel, owners, dests), out_shape...  7.99 us
    convert_element_type x4, other arithmetic, narrow(): return (x * F16_SCALE).astype(jnp.float16)  7.94 us
  transfers between devices with their start and end apart: 19, of which 3 were waited for; matrix products, arithmetic and copies ran while one was open for 10% of the time, Pallas kernels for 44%

profile of v3, /device:TPU:0, one launch (start us, length us, event | category | flops | bytes accessed | tf_op | source)
XLA Modules:
  0.0 150.9 jit_solution(2955741260416890710)
XLA Ops:
  0.6 4.5 %gather_slots.2 = (bf16[16,64,256]{2,1,0:T(8,128)(2,1)}, bf16[16,64,256]{2,1,0:T(8,128)(2,1)}, bf16[16,64,256]{2,1,0:T(8,128)(2,1)}, bf16[16,64,256]{2,1,0:T(8,1...) custom-call(s32[4]{0:T(128)} %pad_add_fusion.me_ref, s32[128]{0:T(128)} %family_ref.3, ...), custom_call_target="tpu_custom_call" | custom-call | flops 1 | bytes 1 | tf_op jit(solution)/shard_map/gather_slots/pallas_call | solution.py:113
  5.1 3.0 %collective-permute-start.4 = (bf16[16,64,256]{2,1,0:T(8,128)(2,1)}, bf16[16,64,256]{2,1,0:T(8,128)(2,1)S(1)}, u32[]{:S(2)}, u32[]{:S(2)}) collective-permute-start(bf16[16,64,256]{2,1,0:T(8,128)(2,1)} %get-tuple-element.32), channel_id=1, source_target_pairs={{0,1},{1,0},{2,3},{3,2},{4,5},{5,4},{6,7},{7,6},{8,9},{9,8},{10,11... | collective-permute-start | bytes 1572872 | tf_op jit(solution)/shard_map/ppermute | solution.py:729
  8.1 1.6 %collective-permute-start.2 = (bf16[16,64,256]{2,1,0:T(8,128)(2,1)}, bf16[16,64,256]{2,1,0:T(8,128)(2,1)S(1)}, u32[]{:S(2)}, u32[]{:S(2)}) collective-permute-start(bf16[16,64,256]{2,1,0:T(8,128)(2,1)} %get-tuple-element.30), channel_id=1, source_target_pairs={{0,2},{1,3},{2,0},{3,1},{4,6},{5,7},{6,4},{7,5},{8,10},{9,11},{10,... | collective-permute-start | bytes 1572872 | tf_op jit(solution)/shard_map/ppermute | solution.py:729
  9.7 2.9 %collective-permute-start = (bf16[16,64,256]{2,1,0:T(8,128)(2,1)}, bf16[16,64,256]{2,1,0:T(8,128)(2,1)S(1)}, u32[]{:S(2)}, u32[]{:S(2)}) collective-permute-start(bf16[16,64,256]{2,1,0:T(8,128)(2,1)} %get-tuple-element.28), channel_id=1, source_target_pairs={{0,4},{1,5},{2,6},{3,7},{4,0},{5,1},{6,2},{7,3},{8,12},{9,13},{10,... | collective-permute-start | bytes 1572872 | tf_op jit(solution)/shard_map/ppermute | solution.py:729
  14.6 6.1 %whiten.3 = (bf16[8,128,16,256]{3,2,1,0:T(8,128)(2,1)}, f32[8,128]{1,0:T(8,128)}) custom-call(bf16[512,256]{1,0:T(8,128)(2,1)} %constant.33.clone.table_hbm, f32[1,256]{1,0:T(1,128)} %tile.13.mask_ref, bf16[16,64,256]{2,1,0:T(8,128)(2,1)} %get-tuple-element.33.refs_0_), custom_call_target="tpu_custom_call" | custom-call | flops 1 | bytes 1 | tf_op jit(solution)/shard_map/whiten/pallas_call | solution.py:239
  21.6 6.1 %whiten.4 = (bf16[8,128,16,256]{3,2,1,0:T(8,128)(2,1)}, f32[8,128]{1,0:T(8,128)}) custom-call(bf16[512,256]{1,0:T(8,128)(2,1)} %constant.33.clone.table_hbm, f32[1,256]{1,0:T(1,128)} %tile.13.mask_ref, bf16[16,64,256]{2,1,0:T(8,128)(2,1)} %copy-done.3, bf16[8,128,16,256]{3,2,1,0:T(8,128)(2,1)} %get-tuple-element.34.refs_1_), custom_call_target="tpu_custom_call", output_to_operand_aliasing={{0}: (3, {})} | custom-call | flops 1 | bytes 1 | tf_op jit(solution)/shard_map/whiten/pallas_call | solution.py:239
  27.7 17.8 %collective-permute-done.2.rest_2_.refs_0_ = bf16[16,64,256]{2,1,0:T(8,128)(2,1)S(1)} collective-permute-done((bf16[16,64,256]{2,1,0:T(8,128)(2,1)}, bf16[16,64,256]{2,1,0:T(8,128)(2,1)S(1)}, u32[]{:S(2)}, u32[]{:S(2)}) %collective-permute-start.2) | collective-permute-done | bytes 524320 | tf_op jit(solution)/shard_map/ppermute | solution.py:729
  45.5 8.4 %collective-permute-done.3.rest_3_.refs_1_ = bf16[16,64,256]{2,1,0:T(8,128)(2,1)S(1)} collective-permute-done((bf16[16,64,256]{2,1,0:T(8,128)(2,1)}, bf16[16,64,256]{2,1,0:T(8,128)(2,1)S(1)}, u32[]{:S(2)}, u32[]{:S(2)}) %collective-permute-start.3) | collective-permute-done | bytes 524320 | tf_op jit(solution)/shard_map/ppermute | solution.py:729
  54.7 3.5 %gather_slots.3 = (bf16[16,64,256]{2,1,0:T(8,128)(2,1)}, bf16[16,64,256]{2,1,0:T(8,128)(2,1)}) custom-call(s32[4]{0:T(128)} %pad_add_fusion.me_ref, s32[128]{0:T(128)} %family_ref.3, bf16[128,64,256]{2,1,0:T(8,128)(2,1)} %wave_ref.3, f32[8,128]{1,0:T(8,128)} %get-tuple-element.35.rest_0_.refs_4_, bf16[16,64,256]{2,1,0:T(8,128)(2,1)} %copy-done.3, ...), custom_call_target="tpu_custom_call" | custom-call | flops 1 | bytes 1 | tf_op jit(solution)/shard_map/gather_slots/pallas_call | solution.py:113
  58.2 1.5 %collective-permute-start.9 = (bf16[16,64,256]{2,1,0:T(8,128)(2,1)}, bf16[16,64,256]{2,1,0:T(8,128)(2,1)S(1)}, u32[]{:S(2)}, u32[]{:S(2)}) collective-permute-start(bf16[16,64,256]{2,1,0:T(8,128)(2,1)} %get-tuple-element.36.refs_2_), channel_id=1, source_target_pairs={{0,6},{1,7},{2,4},{3,5},{4,2},{5,3},{6,0},{7,1},{8,14},{9,15},{10,... | collective-permute-start | bytes 1572872 | tf_op jit(solution)/shard_map/ppermute | solution.py:729
  59.7 4.7 %collective-permute-start.8 = (bf16[16,64,256]{2,1,0:T(8,128)(2,1)}, bf16[16,64,256]{2,1,0:T(8,128)(2,1)S(1)}, u32[]{:S(2)}, u32[]{:S(2)}) collective-permute-start(bf16[16,64,256]{2,1,0:T(8,128)(2,1)} %get-tuple-element.43), channel_id=1, source_target_pairs={{0,7},{1,6},{2,5},{3,4},{4,3},{5,2},{6,1},{7,0},{8,15},{9,14},{10,... | collective-permute-start | bytes 1572872 | tf_op jit(solution)/shard_map/ppermute | solution.py:729
  64.4 9.0 %whiten.5 = (bf16[8,128,16,256]{3,2,1,0:T(8,128)(2,1)}, f32[8,128]{1,0:T(8,128)}, f32[8,128]{1,0:T(8,128)}) custom-call(bf16[512,256]{1,0:T(8,128)(2,1)} %constant.33.clone.table_hbm, f32[1,256]{1,0:T(1,128)} %tile.13.mask_ref, bf16[16,64,256]{2,1,0:T(8,128)(2,1)} %copy-done.4, bf16[16,64,256]{2,1,0:T(8,128)(2,1)} %copy-done.5, ...), custom_call_target="tpu_custom_call", output_to_operand_aliasing={{0}: (5, {})} | custom-call | flops 1 | bytes 1 | tf_op jit(solution)/shard_map/whiten/pallas_call | solution.py:239
  74.4 20.2 %square.1 = (f32[4,32,72,128]{3,2,1,0:T(8,128)}, f32[8,128]{1,0:T(8,128)}, f32[8,128]{1,0:T(8,128)}, bf16[8,128,16,256]{3,2,1,0:T(8,128)(2,1)}) custom-call(s32[4]{0:T(128)} %pad_add_fusion.me_ref, bf16[512,256]{1,0:T(8,128)(2,1)} %constant.33.clone.table_hbm, f32[1,256]{1,0:T(1,128)} %tile.13.mask_ref, ...), custom_call_target="tpu_custom_call", output_to_operand_aliasing={{3}: (6, {})} | custom-call | flops 1 | bytes 1 | tf_op jit(solution)/shard_map/square/pallas_call | solution.py:465
  94.6 3.7 %multiply_convert_fusion = (f16[1,32,72,128]{3,2,1,0:T(8,128)(2,1)}, f16[1,32,72,128]{3,2,1,0:T(8,128)(2,1)}, f16[1,32,72,128]{3,2,1,0:T(8,128)(2,1)}, f32[32,72,128]{2,1,0:T(8,128)S(1)}) fusion(f32[4,32,72,128]{3,2,1,0:T(8,128)} %get-tuple-element.42), kind=kLoop, calls=%fused_computation | loop fusion | flops 1769472 | bytes 7667712 | tf_op jit(solution)/shard_map/convert_element_type | solution.py:769
  101.0 10.7 %step.2 = (f32[1040,128]{1,0:T(8,128)}, f32[4,288,128]{2,1,0:T(8,128)}, bf16[8,128,16,256]{3,2,1,0:T(8,128)(2,1)}, f32[8,128]{1,0:T(8,128)}) custom-call(s32[4]{0:T(128)} %pad_add_fusion.me_ref, bf16[512,256]{1,0:T(8,128)(2,1)} %constant.33.clone.table_hbm, f32[1,256]{1,0:T(1,128)} %tile.13.mask_ref, ...), custom_call_target="tpu_custom_call", output_to_operand_aliasing={{2}: (5, {})} | custom-call | flops 1 | bytes 1 | tf_op jit(solution)/shard_map/step/pallas_call | solution.py:533
  111.7 1.8 %multiply_convert_fusion.4 = f16[1040,128]{1,0:T(8,128)(2,1)} fusion(f32[1040,128]{1,0:T(8,128)} %get-tuple-element.49.refs_8_), kind=kLoop, calls=%fused_computation.5 | loop fusion | flops 266240 | bytes 798720 | tf_op jit(solution)/shard_map/convert_element_type | solution.py:769
  113.5 1.4 collective-permute-start.10
  114.9 1.4 collective-permute-start.11
  116.3 10.5 %step.3 = (f32[1040,128]{1,0:T(8,128)}, f32[4,576,128]{2,1,0:T(8,128)}) custom-call(s32[4]{0:T(128)} %pad_add_fusion.me_ref, bf16[512,256]{1,0:T(8,128)(2,1)} %constant.33.clone.table_hbm, f32[1,256]{1,0:T(1,128)} %tile.13.mask_ref, bf16[144,256]{1,0:T(8,128)(2,1)} %constant.34.clone.lag_ref, bf16[16,64,256]{2,1,0:T(8,128)(2,1)} %copy-done.9, ...), custom_call_target="tpu_custom_call" | custom-call | flops 100000000376832 | bytes 1 | tf_op jit(solution)/shard_map/step/pallas_call | solution.py:533
  126.8 3.2 %collective-permute-start.12 = (f16[1040,128]{1,0:T(8,128)(2,1)}, f16[1040,128]{1,0:T(8,128)(2,1)S(1)}, u32[]{:S(2)}, u32[]{:S(2)}) collective-permute-start(f16[1040,128]{1,0:T(8,128)(2,1)} %multiply_convert_fusion.4), channel_id=1, source_target_pairs={{0,24},{1,25},{10,18},{11,19},{20,12},{21,13},{30,6},{31,7}} | collective-permute-start | bytes 798728 | tf_op jit(solution)/shard_map/ppermute | solution.py:779
  132.5 2.5 %collective-permute-start.18 = (f16[1040,128]{1,0:T(8,128)(2,1)S(1)}, f16[1040,128]{1,0:T(8,128)(2,1)S(1)}, u32[]{:S(2)}, u32[]{:S(2)}) collective-permute-start(f16[1040,128]{1,0:T(8,128)(2,1)S(1)} %multiply_convert_fusion.3), channel_id=1, source_target_pairs={{0,24},{1,25},{10,18},{11,19},{20,12},{21,13},{30,6},{31,7}} | collective-permute-start | bytes 798728 | tf_op jit(solution)/shard_map/ppermute | solution.py:779
  137.8 1.3 collective-permute-start.14
  145.4 1.4 collective-permute-done.15
  146.8 3.9 %finish.1 = f32[65,32,128]{2,1,0:T(8,128)} custom-call(s32[4]{0:T(128)S(1)} %copy-done.2, f32[32,72,128]{2,1,0:T(8,128)S(1)} %get-tuple-element.54.refs_0_, f32[32,72,128]{2,1,0:T(8,128)S(1)} %convert.3.refs_1_, f32[32,72,128]{2,1,0:T(8,128)S(1)} %convert.4.refs_2_, f32[32,72,128]{2,1,0:T(8,128)S(1)} %convert.5.refs_3_, ...), custom_call_target="tpu_custom_call" | custom-call | flops 1 | bytes 1 | tf_op jit(solution)/shard_map/finish/pallas_call | solution.py:681
  (67 shorter events, 19.1 us)
Async XLA Ops:
  0.6 13.4 %copy-start.10 = (s32[1,64]{1,0:T(1,128)S(1)}, s32[1,64]{1,0:T(1,128)}, u32[]{:S(2)}) copy-start(s32[1,64]{1,0:T(1,128)} %param.7) | copy-start | bytes 772
  5.1 15.6 %collective-permute-start.4 = (bf16[16,64,256]{2,1,0:T(8,128)(2,1)}, bf16[16,64,256]{2,1,0:T(8,128)(2,1)S(1)}, u32[]{:S(2)}, u32[]{:S(2)}) collective-permute-start(bf16[16,64,256]{2,1,0:T(8,128)(2,1)} %get-tuple-element.32), channel_id=1, source_target_pairs={{0,1},{1,0},{2,3},{3,2},{4,5},{5,4},{6,7},{7,6},{8,9},{9,8},{10,11... | collective-permute-start | bytes 1572872 | tf_op jit(solution)/shard_map/ppermute | solution.py:729
  8.1 37.4 %collective-permute-start.2 = (bf16[16,64,256]{2,1,0:T(8,128)(2,1)}, bf16[16,64,256]{2,1,0:T(8,128)(2,1)S(1)}, u32[]{:S(2)}, u32[]{:S(2)}) collective-permute-start(bf16[16,64,256]{2,1,0:T(8,128)(2,1)} %get-tuple-element.30), channel_id=1, source_target_pairs={{0,2},{1,3},{2,0},{3,1},{4,6},{5,7},{6,4},{7,5},{8,10},{9,11},{10,... | collective-permute-start | bytes 1572872 | tf_op jit(solution)/shard_map/ppermute | solution.py:729
  9.7 44.2 %collective-permute-start.3 = (bf16[16,64,256]{2,1,0:T(8,128)(2,1)}, bf16[16,64,256]{2,1,0:T(8,128)(2,1)S(1)}, u32[]{:S(2)}, u32[]{:S(2)}) collective-permute-start(bf16[16,64,256]{2,1,0:T(8,128)(2,1)} %get-tuple-element.31), channel_id=1, source_target_pairs={{0,3},{1,2},{2,1},{3,0},{4,7},{5,6},{6,5},{7,4},{8,11},{9,10},{10,... | collective-permute-start | bytes 1572872 | tf_op jit(solution)/shard_map/ppermute | solution.py:729
  9.7 63.7 %collective-permute-start = (bf16[16,64,256]{2,1,0:T(8,128)(2,1)}, bf16[16,64,256]{2,1,0:T(8,128)(2,1)S(1)}, u32[]{:S(2)}, u32[]{:S(2)}) collective-permute-start(bf16[16,64,256]{2,1,0:T(8,128)(2,1)} %get-tuple-element.28), channel_id=1, source_target_pairs={{0,4},{1,5},{2,6},{3,7},{4,0},{5,1},{6,2},{7,3},{8,12},{9,13},{10,... | collective-permute-start | bytes 1572872 | tf_op jit(solution)/shard_map/ppermute | solution.py:729
  12.7 60.8 %collective-permute-start.1 = (bf16[16,64,256]{2,1,0:T(8,128)(2,1)}, bf16[16,64,256]{2,1,0:T(8,128)(2,1)S(1)}, u32[]{:S(2)}, u32[]{:S(2)}) collective-permute-start(bf16[16,64,256]{2,1,0:T(8,128)(2,1)} %get-tuple-element.29), channel_id=1, source_target_pairs={{0,5},{1,4},{2,7},{3,6},{4,1},{5,0},{6,3},{7,2},{8,13},{9,12},{10,... | collective-permute-start | bytes 1572872 | tf_op jit(solution)/shard_map/ppermute | solution.py:729
  45.5 8.4 %copy-start.4 = (bf16[16,64,256]{2,1,0:T(8,128)(2,1)}, bf16[16,64,256]{2,1,0:T(8,128)(2,1)S(1)}, u32[]{:S(2)}) copy-start(bf16[16,64,256]{2,1,0:T(8,128)(2,1)S(1)} %collective-permute-done.2.rest_2_.refs_0_) | copy-start | bytes 1572868
  58.2 42.0 %collective-permute-start.9 = (bf16[16,64,256]{2,1,0:T(8,128)(2,1)}, bf16[16,64,256]{2,1,0:T(8,128)(2,1)S(1)}, u32[]{:S(2)}, u32[]{:S(2)}) collective-permute-start(bf16[16,64,256]{2,1,0:T(8,128)(2,1)} %get-tuple-element.36.refs_2_), channel_id=1, source_target_pairs={{0,6},{1,7},{2,4},{3,5},{4,2},{5,3},{6,0},{7,1},{8,14},{9,15},{10,... | collective-permute-start | bytes 1572872 | tf_op jit(solution)/shard_map/ppermute | solution.py:729
  59.7 55.2 %collective-permute-start.8 = (bf16[16,64,256]{2,1,0:T(8,128)(2,1)}, bf16[16,64,256]{2,1,0:T(8,128)(2,1)S(1)}, u32[]{:S(2)}, u32[]{:S(2)}) collective-permute-start(bf16[16,64,256]{2,1,0:T(8,128)(2,1)} %get-tuple-element.43), channel_id=1, source_target_pairs={{0,7},{1,6},{2,5},{3,4},{4,3},{5,2},{6,1},{7,0},{8,15},{9,14},{10,... | collective-permute-start | bytes 1572872 | tf_op jit(solution)/shard_map/ppermute | solution.py:729
  98.3 28.5 %collective-permute-start.5 = (f16[2304,128]{1,0:T(8,128)(2,1)}, f16[2304,128]{1,0:T(8,128)(2,1)}, u32[]{:S(2)}, u32[]{:S(2)}) collective-permute-start(f16[2304,128]{1,0:T(8,128)(2,1)} %bitcast.6), channel_id=1, source_target_pairs={{0,8},{8,0},{16,24},{24,16},{1,9},{9,1},{17,25},{25,17},{2,10},{10... | collective-permute-start | bytes 1769480 | tf_op jit(solution)/shard_map/ppermute | solution.py:732
  98.3 32.8 %collective-permute-start.6 = (f16[2304,128]{1,0:T(8,128)(2,1)}, f16[2304,128]{1,0:T(8,128)(2,1)}, u32[]{:S(2)}, u32[]{:S(2)}) collective-permute-start(f16[2304,128]{1,0:T(8,128)(2,1)} %bitcast.8), channel_id=1, source_target_pairs={{0,16},{8,24},{16,0},{24,8},{1,17},{9,25},{17,1},{25,9},{2,18},{10... | collective-permute-start | bytes 1769480 | tf_op jit(solution)/shard_map/ppermute | solution.py:732
  99.6 32.2 %collective-permute-start.7 = (f16[2304,128]{1,0:T(8,128)(2,1)}, f16[2304,128]{1,0:T(8,128)(2,1)}, u32[]{:S(2)}, u32[]{:S(2)}) collective-permute-start(f16[2304,128]{1,0:T(8,128)(2,1)} %bitcast.10), channel_id=1, source_target_pairs={{0,24},{8,16},{16,8},{24,0},{1,25},{9,17},{17,9},{25,1},{2,26},{10... | collective-permute-start | bytes 1769480 | tf_op jit(solution)/shard_map/ppermute | solution.py:732
  113.5 19.0 %collective-permute-start.10 = (f16[1040,128]{1,0:T(8,128)(2,1)}, f16[1040,128]{1,0:T(8,128)(2,1)}, u32[]{:S(2)}, u32[]{:S(2)}) collective-permute-start(f16[1040,128]{1,0:T(8,128)(2,1)} %multiply_convert_fusion.4), channel_id=1, source_target_pairs={{16,24},{17,25},{26,18},{27,19},{4,12},{5,13},{14,6},{15,7}} | collective-permute-start | bytes 798728 | tf_op jit(solution)/shard_map/ppermute | solution.py:779
  114.9 20.2 %collective-permute-start.11 = (f16[1040,128]{1,0:T(8,128)(2,1)}, f16[1040,128]{1,0:T(8,128)(2,1)}, u32[]{:S(2)}, u32[]{:S(2)}) collective-permute-start(f16[1040,128]{1,0:T(8,128)(2,1)} %multiply_convert_fusion.4), channel_id=1, source_target_pairs={{8,24},{9,25},{2,18},{3,19},{28,12},{29,13},{22,6},{23,7}} | collective-permute-start | bytes 798728 | tf_op jit(solution)/shard_map/ppermute | solution.py:779
  126.8 8.3 %collective-permute-start.12 = (f16[1040,128]{1,0:T(8,128)(2,1)}, f16[1040,128]{1,0:T(8,128)(2,1)S(1)}, u32[]{:S(2)}, u32[]{:S(2)}) collective-permute-start(f16[1040,128]{1,0:T(8,128)(2,1)} %multiply_convert_fusion.4), channel_id=1, source_target_pairs={{0,24},{1,25},{10,18},{11,19},{20,12},{21,13},{30,6},{31,7}} | collective-permute-start | bytes 798728 | tf_op jit(solution)/shard_map/ppermute | solution.py:779
  131.1 8.0 %collective-permute-start.16 = (f16[1040,128]{1,0:T(8,128)(2,1)S(1)}, f16[1040,128]{1,0:T(8,128)(2,1)S(1)}, u32[]{:S(2)}, u32[]{:S(2)}) collective-permute-start(f16[1040,128]{1,0:T(8,128)(2,1)S(1)} %multiply_convert_fusion.3), channel_id=1, source_target_pairs={{16,24},{17,25},{26,18},{27,19},{4,12},{5,13},{14,6},{15,7}} | collective-permute-start | bytes 798728 | tf_op jit(solution)/shard_map/ppermute | solution.py:779
  131.8 13.3 %collective-permute-start.17 = (f16[1040,128]{1,0:T(8,128)(2,1)S(1)}, f16[1040,128]{1,0:T(8,128)(2,1)S(1)}, u32[]{:S(2)}, u32[]{:S(2)}) collective-permute-start(f16[1040,128]{1,0:T(8,128)(2,1)S(1)} %multiply_convert_fusion.3), channel_id=1, source_target_pairs={{8,24},{9,25},{2,18},{3,19},{28,12},{29,13},{22,6},{23,7}} | collective-permute-start | bytes 798728 | tf_op jit(solution)/shard_map/ppermute | solution.py:779
  132.5 12.7 %collective-permute-start.18 = (f16[1040,128]{1,0:T(8,128)(2,1)S(1)}, f16[1040,128]{1,0:T(8,128)(2,1)S(1)}, u32[]{:S(2)}, u32[]{:S(2)}) collective-permute-start(f16[1040,128]{1,0:T(8,128)(2,1)S(1)} %multiply_convert_fusion.3), channel_id=1, source_target_pairs={{0,24},{1,25},{10,18},{11,19},{20,12},{21,13},{30,6},{31,7}} | collective-permute-start | bytes 798728 | tf_op jit(solution)/shard_map/ppermute | solution.py:779
  137.7 7.6 %collective-permute-start.13 = (f16[576,128]{1,0:T(8,128)(2,1)S(1)}, f16[576,128]{1,0:T(8,128)(2,1)S(1)}, u32[]{:S(2)}, u32[]{:S(2)}) collective-permute-start(f16[576,128]{1,0:T(8,128)(2,1)S(1)} %get-tuple-element.57), channel_id=1, source_target_pairs={{0,8},{8,0},{16,24},{24,16},{1,9},{9,1},{17,25},{25,17},{2,10},{10... | collective-permute-start | bytes 442376 | tf_op jit(solution)/shard_map/ppermute | solution.py:732
  137.8 7.6 %collective-permute-start.14 = (f16[576,128]{1,0:T(8,128)(2,1)S(1)}, f16[576,128]{1,0:T(8,128)(2,1)S(1)}, u32[]{:S(2)}, u32[]{:S(2)}) collective-permute-start(f16[576,128]{1,0:T(8,128)(2,1)S(1)} %get-tuple-element.56), channel_id=1, source_target_pairs={{0,16},{8,24},{16,0},{24,8},{1,17},{9,25},{17,1},{25,9},{2,18},{10... | collective-permute-start | bytes 442376 | tf_op jit(solution)/shard_map/ppermute | solution.py:732
  139.1 7.6 %collective-permute-start.15 = (f16[576,128]{1,0:T(8,128)(2,1)S(1)}, f16[576,128]{1,0:T(8,128)(2,1)S(1)}, u32[]{:S(2)}, u32[]{:S(2)}) collective-permute-start(f16[576,128]{1,0:T(8,128)(2,1)S(1)} %get-tuple-element.55), channel_id=1, source_target_pairs={{0,24},{8,16},{16,8},{24,0},{1,25},{9,17},{17,9},{25,1},{2,26},{10... | collective-permute-start | bytes 442376 | tf_op jit(solution)/shard_map/ppermute | solution.py:732
  145.2 1.6 %copy-start = (f32[1040,128]{1,0:T(8,128)S(1)}, f32[1040,128]{1,0:T(8,128)}, u32[]{:S(2)}) copy-start(f32[1040,128]{1,0:T(8,128)} %get-tuple-element.49.refs_8_) | copy-start | bytes 1597444
  145.2 1.6 %copy-start.1 = (f32[1040,128]{1,0:T(8,128)S(1)}, f32[1040,128]{1,0:T(8,128)}, u32[]{:S(2)}) copy-start(f32[1040,128]{1,0:T(8,128)} %get-tuple-element.50.refs_12_) | copy-start | bytes 1597444
  145.2 1.6 %copy-start.2 = (s32[4]{0:T(128)S(1)}, s32[4]{0:T(128)}, u32[]{:S(2)}) copy-start(s32[4]{0:T(128)} %pad_add_fusion.me_ref) | copy-start | bytes 52
  (6 other events, 5.5 us)

commit v4 on v3

--- a/solution.py
+++ b/solution.py
@@ -16,6 +16,7 @@
 F16_SCALE = 16384.0
 TINY = 1.2e-38
 VMEM_LIMIT = 56 * 2**20
+VMEM_MARGIN = 8 * 2**20
 PITCH_PAD = 8
 LOAD_PARTS = 1
 LONG = pl.CostEstimate(flops=10**14, bytes_accessed=1, transcendentals=0)
@@ -28,6 +29,12 @@
 IN_HBM = pl.BlockSpec(memory_space=pltpu.HBM)
 
 
+def room(scratch_shapes):
+    buffers = [x for x in scratch_shapes if getattr(x, "memory_space", None) == pltpu.VMEM]
+    total = sum(math.prod(x.shape) * jnp.dtype(x.dtype).itemsize for x in buffers)
+    return pltpu.CompilerParams(vmem_limit_bytes=min(VMEM_LIMIT, total + VMEM_MARGIN))
+
+
 def split(x):
     high = x.astype(BF16)
     return high, (x - high.astype(F32)).astype(BF16)
@@ -113,7 +120,7 @@
     return pl.pallas_call(
         functools.partial(gather_kernel, owners, dests),
         out_shape=[jax.ShapeDtypeStruct(shape, waveforms.dtype)] * count,
-        in_specs=[IN_SMEM, IN_SMEM, IN_HBM] + [IN_HBM] * len(after),
+        in_specs=[IN_SMEM, IN_SMEM, IN_HBM] + [IN_VMEM] * len(after),
         out_specs=[IN_HBM] * count,
         scratch_shapes=[
             pltpu.SMEM((owners,), jnp.int32),
@@ -123,7 +130,7 @@
             pltpu.SemaphoreType.DMA((count,)),
         ],
         cost_estimate=SHORT,
-        compiler_params=pltpu.CompilerParams(vmem_limit_bytes=VMEM_LIMIT),
+        compiler_params=pltpu.CompilerParams(vmem_limit_bytes=2 * VMEM_MARGIN if after else VMEM_LIMIT),
         name="gather_slots",
     )(me, family_of, waveforms, *after)
 
@@ -198,24 +205,20 @@
 
 def whiten_kernel(ds, table_hbm, mask_ref, *refs):
     count = len(ds)
-    x_hbm = refs[:count]
-    m_hbm, e_ref = refs[-8 - count], refs[-7 - count : -7]
-    x_ref, table_ref, m_ref, scratch, sem, x_sem, out_sem = refs[-7:]
+    x_refs = refs[:count]
+    m_hbm, e_ref = refs[-6 - count], refs[-5 - count : -5]
+    table_ref, m_ref, scratch, sem, out_sem = refs[-5:]
     load = pltpu.make_async_copy(table_hbm, table_ref, sem)
     load.start()
-    loads = [pltpu.make_async_copy(x_hbm[n], x_ref.at[n], x_sem.at[n]) for n in range(count)]
-    for c in loads:
-        c.start()
     load.wait()
     outs = []
     for n, d in enumerate(ds):
-        loads[n].wait()
 
         def write(k, high, low):
             m_ref[n, k, :, :LANES] = high
             m_ref[n, k, :, LANES:] = low
 
-        e_ref[n][...] = whiten_body(x_ref.at[n], table_ref, mask_ref, scratch.at[n % 2], write)
+        e_ref[n][...] = whiten_body(x_refs[n], table_ref, mask_ref, scratch.at[n % 2], write)
         outs.append(pltpu.make_async_copy(m_ref.at[n], m_hbm.at[d], out_sem.at[n]))
         outs[-1].start()
     for c in outs:
@@ -236,23 +239,22 @@
     ds = sorted(xs)
     count = len(ds)
     m, scratch = member_shapes(xs[ds[0]])
+    buffers = [
+        pltpu.VMEM(table.shape, table.dtype),
+        pltpu.VMEM((count,) + m.shape, m.dtype),
+        pltpu.VMEM((2,) + scratch, F32),
+        pltpu.SemaphoreType.DMA,
+        pltpu.SemaphoreType.DMA((count,)),
+    ]
     out = pl.pallas_call(
         functools.partial(whiten_kernel, ds),
         out_shape=[jax.ShapeDtypeStruct((owners,) + m.shape, m.dtype)] + [ENERGY] * count,
-        in_specs=[IN_HBM, IN_VMEM] + [IN_HBM] * (count + len(after) + len(filled)),
+        in_specs=[IN_HBM, IN_VMEM] + [IN_VMEM] * (count + len(after)) + [IN_HBM] * len(filled),
         out_specs=[IN_HBM] + [IN_VMEM] * count,
-        scratch_shapes=[
-            pltpu.VMEM((count,) + xs[ds[0]].shape, xs[ds[0]].dtype),
-            pltpu.VMEM(table.shape, table.dtype),
-            pltpu.VMEM((count,) + m.shape, m.dtype),
-            pltpu.VMEM((2,) + scratch, F32),
-            pltpu.SemaphoreType.DMA,
-            pltpu.SemaphoreType.DMA((count,)),
-            pltpu.SemaphoreType.DMA((count,)),
-        ],
+        scratch_shapes=buffers,
         cost_estimate=SHORT,
         input_output_aliases={2 + count + len(after): 0} if filled else {},
-        compiler_params=pltpu.CompilerParams(vmem_limit_bytes=VMEM_LIMIT),
+        compiler_params=room(buffers),
         name="whiten",
     )(table, mask, *[xs[d] for d in ds], *after, *filled)
     return out[0], dict(zip(ds, out[1:]))
@@ -361,26 +363,22 @@
         ref[t * LANES : (t + 1) * LANES] = part.T
 
 
-def whiten_and_load(new, count, me, x_hbm, m_hbm, tables, buffers, sems, keep):
+def whiten_and_load(new, count, x_refs, m_hbm, tables, buffers, sems, keep):
     table_hbm, mask_ref = tables
-    x_ref, table_ref, scratch, members = buffers
-    load, x_sem, sem = sems
+    table_ref, scratch, members = buffers
+    load, sem = sems
     table_load = pltpu.make_async_copy(table_hbm, table_ref, load)
     table_load.start()
-    loads = [pltpu.make_async_copy(x_hbm[n], x_ref.at[n], x_sem.at[n]) for n in range(len(new))]
-    for c in loads:
-        c.start()
     copies = load_members(m_hbm, count, members, sem)
     table_load.wait()
     tiles = {}
     for n, d in enumerate(new):
-        loads[n].wait()
 
         def write(k, high, low):
             members[d, k, :, :LANES] = high
             members[d, k, :, LANES:] = low
 
-        tiles[d] = whiten_body(x_ref.at[n], table_ref, mask_ref, scratch.at[n % 2], write)
+        tiles[d] = whiten_body(x_refs[n], table_ref, mask_ref, scratch.at[n % 2], write)
         keep(d, members.at[d])
     return tiles, copies
 
@@ -389,13 +387,11 @@
     m, scratch = member_shapes(x)
     bins = m.shape[0]
     return [
-        pltpu.VMEM((len(new),) + x.shape, x.dtype),
         pltpu.VMEM(table.shape, table.dtype),
         pltpu.VMEM((min(2, len(new)),) + scratch, F32),
         pltpu.VMEM((slots // CAP, bins, CAP, 2 * LANES), BF16),
         pltpu.VMEM((slots // LANES, n * (2 * bins + PITCH_PAD), LANES), F32),
         pltpu.SemaphoreType.DMA,
-        pltpu.SemaphoreType.DMA((len(new),)),
         pltpu.SemaphoreType.DMA((LOAD_PARTS,)),
         pltpu.SemaphoreType.DMA((24,)),
     ]
@@ -403,11 +399,11 @@
 
 def square_kernel(old, new, lines_of, more, me_ref, table_hbm, mask_ref, lag_ref, *refs):
     count = len(new)
-    x_hbm, refs = refs[:count], refs[count:]
+    x_refs, refs = refs[:count], refs[count:]
     m_hbm, refs = refs[0], refs[1:]
     given, refs = refs[: len(old)], refs[len(old) :]
-    x_ref, table_ref, scratch, members, cross_ref, load, x_sem, sem, out_sem, rows_ref = refs[-10:]
-    outs = refs[-10 - 1 - count - more : -10]
+    table_ref, scratch, members, cross_ref, load, sem, out_sem, rows_ref = refs[-8:]
+    outs = refs[-8 - 1 - count - more : -8]
     me, own = me_ref[0], me_ref[2]
     slots = members.shape[0] * CAP
     done = []
@@ -417,10 +413,9 @@
             done.append(pltpu.make_async_copy(block, outs[1 + count].at[d], out_sem.at[8 + len(done)]))
             done[-1].start()
 
-    buffers = (x_ref, table_ref, scratch, members)
-    sems = (load, x_sem, sem)
+    buffers = (table_ref, scratch, members)
     tables = (table_hbm, mask_ref)
-    tiles, copies = whiten_and_load(new, len(old), me, x_hbm, m_hbm, tables, buffers, sems, keep)
+    tiles, copies = whiten_and_load(new, len(old), x_refs, m_hbm, tables, buffers, (load, sem), keep)
     for n, d in enumerate(new):
         outs[1 + n][...] = tiles[d]
     for d, ref in zip(old, given):
@@ -462,26 +457,28 @@
     aliases = {4 + len(new): 1 + len(new)} if more else {}
     if filled:
         aliases[5 + len(new) + len(old) + len(after)] = 0
+    buffers = shared_scratch(x, new, table, slots, n) + [pltpu.VMEM((n, taus, slots), F32)]
     return pl.pallas_call(
         functools.partial(square_kernel, old, new, lines_of, more),
         out_shape=[rows] + [ENERGY] * len(new) + [members] * more,
         in_specs=[IN_SMEM, IN_HBM, IN_VMEM, IN_VMEM]
-        + [IN_HBM] * (len(new) + 1)
+        + [IN_VMEM] * len(new)
+        + [IN_HBM]
         + [IN_VMEM] * len(old)
         + [IN_HBM] * (len(after) + len(filled)),
         out_specs=[IN_HBM] + [IN_VMEM] * len(new) + [IN_HBM] * more,
-        scratch_shapes=shared_scratch(x, new, table, slots, n) + [pltpu.VMEM((n, taus, slots), F32)],
+        scratch_shapes=buffers,
         cost_estimate=SHORT,
         input_output_aliases=aliases,
-        compiler_params=pltpu.CompilerParams(vmem_limit_bytes=VMEM_LIMIT),
+        compiler_params=room(buffers),
         name="square",
     )(me, table, mask, lags, *[xs[d] for d in new], ms, *[energy[d] for d in old], *after, *filled)
 
 
-def step_kernel(new, final, me_ref, table_hbm, mask_ref, lag_ref, x_hbm, m_hbm, *refs):
+def step_kernel(new, final, me_ref, table_hbm, mask_ref, lag_ref, x_ref, m_hbm, *refs):
     lines, turned_ref = refs[-2:]
-    x_ref, table_ref, scratch, members, cross_ref, load, x_sem, sem, out_sem = refs[-11:-2]
-    outs = refs[-11 - (2 if final else 4) : -11]
+    table_ref, scratch, members, cross_ref, load, sem, out_sem = refs[-9:-2]
+    outs = refs[-9 - (2 if final else 4) : -9]
     me, chan = me_ref[0], me_ref[1]
     slots = members.shape[0] * CAP
     taus = lag_ref.shape[0] // 2
@@ -501,9 +498,8 @@
         turned_cut = kept_turned.shape[1]
         start(kept_turned, turned_ref.at[:, :turned_cut])
         turned_ref = turned_ref.at[:, turned_cut:]
-    buffers = (x_ref, table_ref, scratch, members)
-    sems = (load, x_sem, sem)
-    tiles, copies = whiten_and_load([new], new, me, [x_hbm], m_hbm, (table_hbm, mask_ref), buffers, sems, keep)
+    buffers = (table_ref, scratch, members)
+    tiles, copies = whiten_and_load([new], new, [x_ref], m_hbm, (table_hbm, mask_ref), buffers, (load, sem), keep)
     tile = tiles[new]
     column = jnp.broadcast_to(tile[0:1], (LANES, LANES)).T[:CAP]
 
@@ -530,16 +526,17 @@
     lines = jax.ShapeDtypeStruct((slots // LANES * CAP * LAGS, LANES), F32)
     turned = jax.ShapeDtypeStruct((groups, parts + (kept[0].shape[1] if final else 0), LANES), F32)
     members = jax.ShapeDtypeStruct(ms.shape, ms.dtype)
+    buffers = shared_scratch(x, [new], table, slots, CAP)
+    buffers += [pltpu.VMEM(lines.shape, F32), pltpu.VMEM(turned.shape, F32)]
     return pl.pallas_call(
         functools.partial(step_kernel, new, final),
         out_shape=[lines, turned] + ([] if final else [members, ENERGY]),
-        in_specs=[IN_SMEM, IN_HBM, IN_VMEM, IN_VMEM] + [IN_HBM] * (2 + len(kept) + len(after)),
+        in_specs=[IN_SMEM, IN_HBM, IN_VMEM, IN_VMEM, IN_VMEM] + [IN_HBM] * (1 + len(kept) + len(after)),
         out_specs=[IN_HBM] * 2 + ([] if final else [IN_HBM, IN_VMEM]),
-        scratch_shapes=shared_scratch(x, [new], table, slots, CAP)
-        + [pltpu.VMEM(lines.shape, F32), pltpu.VMEM(turned.shape, F32)],
+        scratch_shapes=buffers,
         cost_estimate=LONG if final else SHORT,
         input_output_aliases={} if final else {5: 2},
-        compiler_params=pltpu.CompilerParams(vmem_limit_bytes=VMEM_LIMIT),
+        compiler_params=room(buffers),
         name="step",
     )(me, table, mask, lags, x, ms, *kept, *after)
 
@@ -553,7 +550,7 @@
     return pl.pallas_call(
         hold_kernel,
         out_shape=[jax.ShapeDtypeStruct(x.shape, x.dtype) for x in xs],
-        in_specs=[IN_HBM] * (n + len(after)),
+        in_specs=[IN_HBM] * n + [IN_VMEM] * len(after),
         out_specs=[IN_HBM] * n,
         input_output_aliases={i: i for i in range(n)},
         cost_estimate=SHORT,
@@ -745,13 +742,7 @@
     for d in remaining:
         post(d)
     after = [sends[remaining[0]]]
-    for start in range(2, half, 4):
-        ds = range(start, min(start + 4, half))
-        ms, got = whiten({d: inbox[d] for d in ds}, table, mask, owners, [ms], after)
-        energy.update(got)
-        after = []
-
-    middle = [d for d in early if d >= half]
+    middle = [d for d in early if d not in energy]
     limit = max(1, 16 * 2**20 // (CAP * length * slots * 4))
     per_call = max(n for n in range(blocks, len(early) + 1, blocks) if len(early) % n == 0 and n <= max(limit, blocks))
     filled = []

time: 152 us -> 141 us (0.928)
  Pallas kernels: 74.6 us -> 60.9 us
  waiting for transfers between devices: 27.6 us -> 35.2 us
  other arithmetic: 15.5 us -> 11.2 us
  local copies, waits for them, and re-layouts: 3.99 us -> 2.2 us
  starting transfers between devices: 28.7 us -> 30.4 us
    pallas_call x3 -> x2, Pallas kernels: 21.3 us -> 5.85 us  [whiten(): pl.pallas_call(functools.partial(whiten_kernel, ds), out_shape=[jax.Shape...]
    ppermute x7, waiting for transfers between devices: 26.2 us -> 33.2 us  [post(): lax.ppermute(sends[d], 'fam', [(i, i ^ d) for i in range(owners)])]
    convert_element_type x4, other arithmetic: 7.94 us -> 3.6 us  [narrow(): return (x * F16_SCALE).astype(jnp.float16)]
    pallas_call x1, Pallas kernels: 20.2 us -> 24.4 us  [square(): pl.pallas_call(functools.partial(square_kernel, old, new, lines_of, more)...]
    pallas_call x2, Pallas kernels: 21.2 us -> 17.8 us  [step(): pl.pallas_call(functools.partial(step_kernel, new, final), out_shape=[lin...]
    ppermute x6, starting transfers between devices: 9.85 us -> 11.6 us  [to_owner(): return lax.ppermute(x, ('chan', 'fam'), moves)]
    unnamed x22 -> x20, local copies, waits for them, and re-layouts: 3.36 us -> 2.11 us
  transfers between devices with their start and end apart: 19 -> 19, of which waited for: 3 -> 5; matrix products, arithmetic and copies ran while one was open for 10% -> 8% of each run, Pallas kernels for 44% -> 37%
where the time goes in v4:
time: 141 us; the launch traced here: 140 us
  Pallas kernels  60.9 us (43%)
  waiting for transfers between devices  35.2 us (25%)
  starting transfers between devices  30.4 us (22%)
  other arithmetic  11.2 us (8%)
  local copies, waits for them, and re-layouts  2.2 us (2%)
    ppermute x7, waiting for transfers between devices, post(): lax.ppermute(sends[d], 'fam', [(i, i ^ d) for i in range(owners)])  33.2 us
    pallas_call x1, Pallas kernels, square(): pl.pallas_call(functools.partial(square_kernel, old, new, lines_of, more)...  24.4 us
    pallas_call x2, Pallas kernels, step(): pl.pallas_call(functools.partial(step_kernel, new, final), out_shape=[lin...  17.8 us
    ppermute x7, starting transfers between devices, post(): lax.ppermute(sends[d], 'fam', [(i, i ^ d) for i in range(owners)])  14.7 us
    ppermute x6, starting transfers between devices, to_owner(): return lax.ppermute(x, ('chan', 'fam'), moves)  11.6 us
    pallas_call x2, Pallas kernels, gather(): pl.pallas_call(functools.partial(gather_kernel, owners, dests), out_shape...  8.28 us
    pallas_call x2, Pallas kernels, whiten(): pl.pallas_call(functools.partial(whiten_kernel, ds), out_shape=[jax.Shape...  5.85 us
    ppermute x6, starting transfers between devices, chan_permute(): return lax.ppermute(x, 'chan', [(i, i ^ e) for i in range(groups)])  4.12 us
  transfers between devices with their start and end apart: 19, of which 5 were waited for; matrix products, arithmetic and copies ran while one was open for 8% of the time, Pallas kernels for 37%

profile of v4, /device:TPU:0, one launch (start us, length us, event | category | flops | bytes accessed | tf_op | source)
XLA Modules:
  0.0 140.4 jit_solution(5531613161856818499)
XLA Ops:
  0.7 4.4 %gather_slots.2 = (bf16[16,64,256]{2,1,0:T(8,128)(2,1)}, bf16[16,64,256]{2,1,0:T(8,128)(2,1)}, bf16[16,64,256]{2,1,0:T(8,128)(2,1)}, bf16[16,64,256]{2,1,0:T(8,1...) custom-call(s32[4]{0:T(128)} %pad_add_fusion.me_ref, s32[128]{0:T(128)} %family_ref.3, ...), custom_call_target="tpu_custom_call" | custom-call | flops 1 | bytes 1 | tf_op jit(solution)/shard_map/gather_slots/pallas_call | solution.py:120
  5.1 3.0 %collective-permute-start.4 = (bf16[16,64,256]{2,1,0:T(8,128)(2,1)}, bf16[16,64,256]{2,1,0:T(8,128)(2,1)S(1)}, u32[]{:S(2)}, u32[]{:S(2)}) collective-permute-start(bf16[16,64,256]{2,1,0:T(8,128)(2,1)} %get-tuple-element.29), channel_id=1, source_target_pairs={{0,1},{1,0},{2,3},{3,2},{4,5},{5,4},{6,7},{7,6},{8,9},{9,8},{10,11... | collective-permute-start | bytes 1572872 | tf_op jit(solution)/shard_map/ppermute | solution.py:726
  8.1 1.7 %collective-permute-start = (bf16[16,64,256]{2,1,0:T(8,128)(2,1)}, bf16[16,64,256]{2,1,0:T(8,128)(2,1)S(1)}, u32[]{:S(2)}, u32[]{:S(2)}) collective-permute-start(bf16[16,64,256]{2,1,0:T(8,128)(2,1)} %get-tuple-element.25), channel_id=1, source_target_pairs={{0,2},{1,3},{2,0},{3,1},{4,6},{5,7},{6,4},{7,5},{8,10},{9,11},{10,... | collective-permute-start | bytes 1572872 | tf_op jit(solution)/shard_map/ppermute | solution.py:726
  9.8 3.0 %collective-permute-start.2 = (bf16[16,64,256]{2,1,0:T(8,128)(2,1)}, bf16[16,64,256]{2,1,0:T(8,128)(2,1)S(1)}, u32[]{:S(2)}, u32[]{:S(2)}) collective-permute-start(bf16[16,64,256]{2,1,0:T(8,128)(2,1)} %get-tuple-element.27), channel_id=1, source_target_pairs={{0,4},{1,5},{2,6},{3,7},{4,0},{5,1},{6,2},{7,3},{8,12},{9,13},{10,... | collective-permute-start | bytes 1572872 | tf_op jit(solution)/shard_map/ppermute | solution.py:726
  15.1 2.9 %whiten.2 = (bf16[8,128,16,256]{3,2,1,0:T(8,128)(2,1)S(1)}, f32[8,128]{1,0:T(8,128)S(1)}) custom-call(bf16[512,256]{1,0:T(8,128)(2,1)S(1)} %copy-done.2, f32[1,256]{1,0:T(1,128)S(1)} %tile.13.mask_ref, bf16[16,64,256]{2,1,0:T(8,128)(2,1)S(1)} %copy-done.5), custom_call_target="tpu_custom_call" | custom-call | flops 1 | bytes 1 | tf_op jit(solution)/shard_map/whiten/pallas_call | solution.py:249
  18.0 2.2 %collective-permute-done.4.refs_0_.rest_1_ = bf16[16,64,256]{2,1,0:T(8,128)(2,1)S(1)} collective-permute-done((bf16[16,64,256]{2,1,0:T(8,128)(2,1)}, bf16[16,64,256]{2,1,0:T(8,128)(2,1)S(1)}, u32[]{:S(2)}, u32[]{:S(2)}) %collective-permute-start.4) | collective-permute-done | bytes 524320 | tf_op jit(solution)/shard_map/ppermute | solution.py:726
  20.2 2.9 %whiten.3 = (bf16[8,128,16,256]{3,2,1,0:T(8,128)(2,1)S(1)}, f32[8,128]{1,0:T(8,128)S(1)}) custom-call(bf16[512,256]{1,0:T(8,128)(2,1)S(1)} %copy-done.2, f32[1,256]{1,0:T(1,128)S(1)} %tile.13.mask_ref, bf16[16,64,256]{2,1,0:T(8,128)(2,1)S(1)} %collective-permute-done.4.refs_0_.rest_1_, ...), custom_call_target="tpu_custom_call", output_to_operand_aliasing={{0}: (3, {})} | custom-call | flops 1 | bytes 1 | tf_op jit(solution)/shard_map/whiten/pallas_call | solution.py:249
  23.2 22.3 %collective-permute-done.rest_2_.refs_0_ = bf16[16,64,256]{2,1,0:T(8,128)(2,1)S(1)} collective-permute-done((bf16[16,64,256]{2,1,0:T(8,128)(2,1)}, bf16[16,64,256]{2,1,0:T(8,128)(2,1)S(1)}, u32[]{:S(2)}, u32[]{:S(2)}) %collective-permute-start) | collective-permute-done | bytes 524320 | tf_op jit(solution)/shard_map/ppermute | solution.py:726
  45.4 8.7 %collective-permute-done.1.rest_3_.refs_1_ = bf16[16,64,256]{2,1,0:T(8,128)(2,1)S(1)} collective-permute-done((bf16[16,64,256]{2,1,0:T(8,128)(2,1)}, bf16[16,64,256]{2,1,0:T(8,128)(2,1)S(1)}, u32[]{:S(2)}, u32[]{:S(2)}) %collective-permute-start.1) | collective-permute-done | bytes 524320 | tf_op jit(solution)/shard_map/ppermute | solution.py:726
  54.1 3.8 %gather_slots.3 = (bf16[16,64,256]{2,1,0:T(8,128)(2,1)S(1)}, bf16[16,64,256]{2,1,0:T(8,128)(2,1)S(1)}) custom-call(s32[4]{0:T(128)S(1)} %copy-done.7, s32[128]{0:T(128)S(1)} %copy-done.8, bf16[128,64,256]{2,1,0:T(8,128)(2,1)S(1)} %copy-done, f32[8,128]{1,0:T(8,128)S(1)} %get-tuple-element.34.rest_0_.refs_6_, ...), custom_call_target="tpu_custom_call" | custom-call | flops 1 | bytes 1 | tf_op jit(solution)/shard_map/gather_slots/pallas_call | solution.py:120
  58.0 1.4 %collective-permute-start.9 = (bf16[16,64,256]{2,1,0:T(8,128)(2,1)S(1)}, bf16[16,64,256]{2,1,0:T(8,128)(2,1)S(1)}, u32[]{:S(2)}, u32[]{:S(2)}) collective-permute-start(bf16[16,64,256]{2,1,0:T(8,128)(2,1)S(1)} %get-tuple-element.35.refs_7_), channel_id=1, source_target_pairs={{0,6},{1,7},{2,4},{3,5},{4,2},{5,3},{6,0},{7,1},{8,14},{9,15},{10,... | collective-permute-start | bytes 1572872 | tf_op jit(solution)/shard_map/ppermute | solution.py:726
  59.4 4.4 %collective-permute-start.8 = (bf16[16,64,256]{2,1,0:T(8,128)(2,1)S(1)}, bf16[16,64,256]{2,1,0:T(8,128)(2,1)S(1)}, u32[]{:S(2)}, u32[]{:S(2)}) collective-permute-start(bf16[16,64,256]{2,1,0:T(8,128)(2,1)S(1)} %get-tuple-element.37), channel_id=1, source_target_pairs={{0,7},{1,6},{2,5},{3,4},{4,3},{5,2},{6,1},{7,0},{8,15},{9,14},{10,... | collective-permute-start | bytes 1572872 | tf_op jit(solution)/shard_map/ppermute | solution.py:726
  63.9 24.4 %square.1 = (f32[4,32,72,128]{3,2,1,0:T(8,128)S(1)}, f32[8,128]{1,0:T(8,128)S(1)}, f32[8,128]{1,0:T(8,128)}, f32[8,128]{1,0:T(8,128)}, f32[8,128]{1,0:T(8,128)}, /*index=5*/bf16[8,128,16,256]{3,2,1,0:T(8,128)(2,1)S(1)}) custom-call(s32[4]{0:T(128)S(1)} %copy-done.7, bf16[512,256]{1,0:T(8,128)(2,1)S(1)} %copy-done.2, ...), custom_call_target="tpu_custom_call", output_to_operand_aliasing={{5}: (8, {})} | custom-call | flops 1 | bytes 1 | tf_op jit(solution)/shard_map/square/pallas_call | solution.py:461
  88.3 1.4 multiply_convert_fusion
  89.7 1.5 %collective-permute-start.6 = (f16[2304,128]{1,0:T(8,128)(2,1)}, f16[2304,128]{1,0:T(8,128)(2,1)}, u32[]{:S(2)}, u32[]{:S(2)}) collective-permute-start(f16[2304,128]{1,0:T(8,128)(2,1)} %bitcast.8), channel_id=1, source_target_pairs={{0,16},{8,24},{16,0},{24,8},{1,17},{9,25},{17,1},{25,9},{2,18},{10... | collective-permute-start | bytes 1769480 | tf_op jit(solution)/shard_map/ppermute | solution.py:729
  91.5 9.1 %step.2 = (f32[1040,128]{1,0:T(8,128)S(1)}, f32[4,288,128]{2,1,0:T(8,128)S(1)}, bf16[8,128,16,256]{3,2,1,0:T(8,128)(2,1)S(1)}, f32[8,128]{1,0:T(8,128)}) custom-call(s32[4]{0:T(128)S(1)} %copy-done.7, bf16[512,256]{1,0:T(8,128)(2,1)S(1)} %copy-done.2, f32[1,256]{1,0:T(1,128)S(1)} %tile.13.mask_ref, ...), custom_call_target="tpu_custom_call", output_to_operand_aliasing={{2}: (5, {})} | custom-call | flops 1 | bytes 1 | tf_op jit(solution)/shard_map/step/pallas_call | solution.py:531
  101.5 1.4 collective-permute-start.10
  102.9 1.4 collective-permute-start.11
  104.2 8.7 %step.3 = (f32[1040,128]{1,0:T(8,128)S(1)}, f32[4,576,128]{2,1,0:T(8,128)S(1)}) custom-call(s32[4]{0:T(128)S(1)} %copy-done.7, bf16[512,256]{1,0:T(8,128)(2,1)S(1)} %copy-done.2, f32[1,256]{1,0:T(1,128)S(1)} %tile.13.mask_ref, bf16[144,256]{1,0:T(8,128)(2,1)S(1)} %copy-done.6, bf16[16,64,256]{2,1,0:T(8,128)(2,1)S(1)} %collective-permute-done.8.x_ref, ...), custom_call_target="tpu_custom_call" | custom-call | flops 100000000376832 | bytes 1 | tf_op jit(solution)/shard_map/step/pallas_call | solution.py:531
  114.0 3.4 %collective-permute-start.12 = (f16[1040,128]{1,0:T(8,128)(2,1)}, f16[1040,128]{1,0:T(8,128)(2,1)S(1)}, u32[]{:S(2)}, u32[]{:S(2)}) collective-permute-start(f16[1040,128]{1,0:T(8,128)(2,1)} %multiply_convert_fusion.4), channel_id=1, source_target_pairs={{0,24},{1,25},{10,18},{11,19},{20,12},{21,13},{30,6},{31,7}} | collective-permute-start | bytes 798728 | tf_op jit(solution)/shard_map/ppermute | solution.py:770
  118.8 4.1 %collective-permute-start.18 = (f16[1040,128]{1,0:T(8,128)(2,1)S(1)}, f16[1040,128]{1,0:T(8,128)(2,1)S(1)}, u32[]{:S(2)}, u32[]{:S(2)}) collective-permute-start(f16[1040,128]{1,0:T(8,128)(2,1)S(1)} %multiply_convert_fusion.3), channel_id=1, source_target_pairs={{0,24},{1,25},{10,18},{11,19},{20,12},{21,13},{30,6},{31,7}} | collective-permute-start | bytes 798728 | tf_op jit(solution)/shard_map/ppermute | solution.py:770
  125.9 1.3 fusion.5
  127.3 2.2 %collective-permute-start.14 = (f16[576,128]{1,0:T(8,128)(2,1)S(1)}, f16[576,128]{1,0:T(8,128)(2,1)S(1)}, u32[]{:S(2)}, u32[]{:S(2)}) collective-permute-start(f16[576,128]{1,0:T(8,128)(2,1)S(1)} %get-tuple-element.50), channel_id=1, source_target_pairs={{0,16},{8,24},{16,0},{24,8},{1,17},{9,25},{17,1},{25,9},{2,18},{10... | collective-permute-start | bytes 442376 | tf_op jit(solution)/shard_map/ppermute | solution.py:729
  136.3 3.9 %finish.1 = f32[65,32,128]{2,1,0:T(8,128)} custom-call(s32[4]{0:T(128)S(1)} %copy-done.7, f32[32,72,128]{2,1,0:T(8,128)S(1)} %get-tuple-element.48.refs_0_, f32[32,72,128]{2,1,0:T(8,128)S(1)} %convert.3.refs_1_, f32[32,72,128]{2,1,0:T(8,128)S(1)} %convert.4.refs_2_, f32[32,72,128]{2,1,0:T(8,128)S(1)} %convert.5.refs_3_, ...), custom_call_target="tpu_custom_call" | custom-call | flops 1 | bytes 1 | tf_op jit(solution)/shard_map/finish/pallas_call | solution.py:678
  (64 shorter events, 16.4 us)
Async XLA Ops:
  0.7 13.3 %copy-start.9 = (s32[1,64]{1,0:T(1,128)S(1)}, s32[1,64]{1,0:T(1,128)}, u32[]{:S(2)}) copy-start(s32[1,64]{1,0:T(1,128)} %param.7) | copy-start | bytes 772
  0.7 13.4 %copy-start.2 = (bf16[512,256]{1,0:T(8,128)(2,1)S(1)}, bf16[512,256]{1,0:T(8,128)(2,1)}, u32[]{:S(2)}) copy-start(bf16[512,256]{1,0:T(8,128)(2,1)} %constant.33.clone.table_hbm) | copy-start | bytes 786436
  5.1 15.1 %collective-permute-start.4 = (bf16[16,64,256]{2,1,0:T(8,128)(2,1)}, bf16[16,64,256]{2,1,0:T(8,128)(2,1)S(1)}, u32[]{:S(2)}, u32[]{:S(2)}) collective-permute-start(bf16[16,64,256]{2,1,0:T(8,128)(2,1)} %get-tuple-element.29), channel_id=1, source_target_pairs={{0,1},{1,0},{2,3},{3,2},{4,5},{5,4},{6,7},{7,6},{8,9},{9,8},{10,11... | collective-permute-start | bytes 1572872 | tf_op jit(solution)/shard_map/ppermute | solution.py:726
  8.1 37.3 %collective-permute-start = (bf16[16,64,256]{2,1,0:T(8,128)(2,1)}, bf16[16,64,256]{2,1,0:T(8,128)(2,1)S(1)}, u32[]{:S(2)}, u32[]{:S(2)}) collective-permute-start(bf16[16,64,256]{2,1,0:T(8,128)(2,1)} %get-tuple-element.25), channel_id=1, source_target_pairs={{0,2},{1,3},{2,0},{3,1},{4,6},{5,7},{6,4},{7,5},{8,10},{9,11},{10,... | collective-permute-start | bytes 1572872 | tf_op jit(solution)/shard_map/ppermute | solution.py:726
  9.8 44.3 %collective-permute-start.1 = (bf16[16,64,256]{2,1,0:T(8,128)(2,1)}, bf16[16,64,256]{2,1,0:T(8,128)(2,1)S(1)}, u32[]{:S(2)}, u32[]{:S(2)}) collective-permute-start(bf16[16,64,256]{2,1,0:T(8,128)(2,1)} %get-tuple-element.26), channel_id=1, source_target_pairs={{0,3},{1,2},{2,1},{3,0},{4,7},{5,6},{6,5},{7,4},{8,11},{9,10},{10,... | collective-permute-start | bytes 1572872 | tf_op jit(solution)/shard_map/ppermute | solution.py:726
  9.8 54.1 %collective-permute-start.2 = (bf16[16,64,256]{2,1,0:T(8,128)(2,1)}, bf16[16,64,256]{2,1,0:T(8,128)(2,1)S(1)}, u32[]{:S(2)}, u32[]{:S(2)}) collective-permute-start(bf16[16,64,256]{2,1,0:T(8,128)(2,1)} %get-tuple-element.27), channel_id=1, source_target_pairs={{0,4},{1,5},{2,6},{3,7},{4,0},{5,1},{6,2},{7,3},{8,12},{9,13},{10,... | collective-permute-start | bytes 1572872 | tf_op jit(solution)/shard_map/ppermute | solution.py:726
  12.8 51.1 %collective-permute-start.3 = (bf16[16,64,256]{2,1,0:T(8,128)(2,1)}, bf16[16,64,256]{2,1,0:T(8,128)(2,1)S(1)}, u32[]{:S(2)}, u32[]{:S(2)}) collective-permute-start(bf16[16,64,256]{2,1,0:T(8,128)(2,1)} %get-tuple-element.28), channel_id=1, source_target_pairs={{0,5},{1,4},{2,7},{3,6},{4,1},{5,0},{6,3},{7,2},{8,13},{9,12},{10,... | collective-permute-start | bytes 1572872 | tf_op jit(solution)/shard_map/ppermute | solution.py:726
  20.2 33.9 %copy-start = (bf16[128,64,256]{2,1,0:T(8,128)(2,1)S(1)}, bf16[128,64,256]{2,1,0:T(8,128)(2,1)}, u32[]{:S(2)}) copy-start(bf16[128,64,256]{2,1,0:T(8,128)(2,1)} %wave_ref.3) | copy-start | bytes 12582916
  20.2 33.9 %copy-start.7 = (s32[4]{0:T(128)S(1)}, s32[4]{0:T(128)}, u32[]{:S(2)}) copy-start(s32[4]{0:T(128)} %pad_add_fusion.me_ref) | copy-start | bytes 52
  20.2 33.9 %copy-start.8 = (s32[128]{0:T(128)S(1)}, s32[128]{0:T(128)}, u32[]{:S(2)}) copy-start(s32[128]{0:T(128)} %family_ref.3) | copy-start | bytes 1540
  58.0 33.6 %collective-permute-start.9 = (bf16[16,64,256]{2,1,0:T(8,128)(2,1)S(1)}, bf16[16,64,256]{2,1,0:T(8,128)(2,1)S(1)}, u32[]{:S(2)}, u32[]{:S(2)}) collective-permute-start(bf16[16,64,256]{2,1,0:T(8,128)(2,1)S(1)} %get-tuple-element.35.refs_7_), channel_id=1, source_target_pairs={{0,6},{1,7},{2,4},{3,5},{4,2},{5,3},{6,0},{7,1},{8,14},{9,15},{10,... | collective-permute-start | bytes 1572872 | tf_op jit(solution)/shard_map/ppermute | solution.py:726
  59.4 43.4 %collective-permute-start.8 = (bf16[16,64,256]{2,1,0:T(8,128)(2,1)S(1)}, bf16[16,64,256]{2,1,0:T(8,128)(2,1)S(1)}, u32[]{:S(2)}, u32[]{:S(2)}) collective-permute-start(bf16[16,64,256]{2,1,0:T(8,128)(2,1)S(1)} %get-tuple-element.37), channel_id=1, source_target_pairs={{0,7},{1,6},{2,5},{3,4},{4,3},{5,2},{6,1},{7,0},{8,15},{9,14},{10,... | collective-permute-start | bytes 1572872 | tf_op jit(solution)/shard_map/ppermute | solution.py:726
  89.7 24.3 %collective-permute-start.5 = (f16[2304,128]{1,0:T(8,128)(2,1)}, f16[2304,128]{1,0:T(8,128)(2,1)}, u32[]{:S(2)}, u32[]{:S(2)}) collective-permute-start(f16[2304,128]{1,0:T(8,128)(2,1)} %bitcast.6), channel_id=1, source_target_pairs={{0,8},{8,0},{16,24},{24,16},{1,9},{9,1},{17,25},{25,17},{2,10},{10... | collective-permute-start | bytes 1769480 | tf_op jit(solution)/shard_map/ppermute | solution.py:729
  89.7 27.7 %collective-permute-start.6 = (f16[2304,128]{1,0:T(8,128)(2,1)}, f16[2304,128]{1,0:T(8,128)(2,1)}, u32[]{:S(2)}, u32[]{:S(2)}) collective-permute-start(f16[2304,128]{1,0:T(8,128)(2,1)} %bitcast.8), channel_id=1, source_target_pairs={{0,16},{8,24},{16,0},{24,8},{1,17},{9,25},{17,1},{25,9},{2,18},{10... | collective-permute-start | bytes 1769480 | tf_op jit(solution)/shard_map/ppermute | solution.py:729
  91.2 26.9 %collective-permute-start.7 = (f16[2304,128]{1,0:T(8,128)(2,1)}, f16[2304,128]{1,0:T(8,128)(2,1)}, u32[]{:S(2)}, u32[]{:S(2)}) collective-permute-start(f16[2304,128]{1,0:T(8,128)(2,1)} %bitcast.10), channel_id=1, source_target_pairs={{0,24},{8,16},{16,8},{24,0},{1,25},{9,17},{17,9},{25,1},{2,26},{10... | collective-permute-start | bytes 1769480 | tf_op jit(solution)/shard_map/ppermute | solution.py:729
  101.5 17.3 %collective-permute-start.10 = (f16[1040,128]{1,0:T(8,128)(2,1)}, f16[1040,128]{1,0:T(8,128)(2,1)}, u32[]{:S(2)}, u32[]{:S(2)}) collective-permute-start(f16[1040,128]{1,0:T(8,128)(2,1)} %multiply_convert_fusion.4), channel_id=1, source_target_pairs={{16,24},{17,25},{26,18},{27,19},{4,12},{5,13},{14,6},{15,7}} | collective-permute-start | bytes 798728 | tf_op jit(solution)/shard_map/ppermute | solution.py:770
  102.9 20.0 %collective-permute-start.11 = (f16[1040,128]{1,0:T(8,128)(2,1)}, f16[1040,128]{1,0:T(8,128)(2,1)}, u32[]{:S(2)}, u32[]{:S(2)}) collective-permute-start(f16[1040,128]{1,0:T(8,128)(2,1)} %multiply_convert_fusion.4), channel_id=1, source_target_pairs={{8,24},{9,25},{2,18},{3,19},{28,12},{29,13},{22,6},{23,7}} | collective-permute-start | bytes 798728 | tf_op jit(solution)/shard_map/ppermute | solution.py:770
  114.0 10.0 %collective-permute-start.12 = (f16[1040,128]{1,0:T(8,128)(2,1)}, f16[1040,128]{1,0:T(8,128)(2,1)S(1)}, u32[]{:S(2)}, u32[]{:S(2)}) collective-permute-start(f16[1040,128]{1,0:T(8,128)(2,1)} %multiply_convert_fusion.4), channel_id=1, source_target_pairs={{0,24},{1,25},{10,18},{11,19},{20,12},{21,13},{30,6},{31,7}} | collective-permute-start | bytes 798728 | tf_op jit(solution)/shard_map/ppermute | solution.py:770
  117.4 12.1 %collective-permute-start.16 = (f16[1040,128]{1,0:T(8,128)(2,1)S(1)}, f16[1040,128]{1,0:T(8,128)(2,1)S(1)}, u32[]{:S(2)}, u32[]{:S(2)}) collective-permute-start(f16[1040,128]{1,0:T(8,128)(2,1)S(1)} %multiply_convert_fusion.3), channel_id=1, source_target_pairs={{16,24},{17,25},{26,18},{27,19},{4,12},{5,13},{14,6},{15,7}} | collective-permute-start | bytes 798728 | tf_op jit(solution)/shard_map/ppermute | solution.py:770
  118.1 16.9 %collective-permute-start.17 = (f16[1040,128]{1,0:T(8,128)(2,1)S(1)}, f16[1040,128]{1,0:T(8,128)(2,1)S(1)}, u32[]{:S(2)}, u32[]{:S(2)}) collective-permute-start(f16[1040,128]{1,0:T(8,128)(2,1)S(1)} %multiply_convert_fusion.3), channel_id=1, source_target_pairs={{8,24},{9,25},{2,18},{3,19},{28,12},{29,13},{22,6},{23,7}} | collective-permute-start | bytes 798728 | tf_op jit(solution)/shard_map/ppermute | solution.py:770
  118.8 16.3 %collective-permute-start.18 = (f16[1040,128]{1,0:T(8,128)(2,1)S(1)}, f16[1040,128]{1,0:T(8,128)(2,1)S(1)}, u32[]{:S(2)}, u32[]{:S(2)}) collective-permute-start(f16[1040,128]{1,0:T(8,128)(2,1)S(1)} %multiply_convert_fusion.3), channel_id=1, source_target_pairs={{0,24},{1,25},{10,18},{11,19},{20,12},{21,13},{30,6},{31,7}} | collective-permute-start | bytes 798728 | tf_op jit(solution)/shard_map/ppermute | solution.py:770
  127.3 7.9 %collective-permute-start.13 = (f16[576,128]{1,0:T(8,128)(2,1)S(1)}, f16[576,128]{1,0:T(8,128)(2,1)S(1)}, u32[]{:S(2)}, u32[]{:S(2)}) collective-permute-start(f16[576,128]{1,0:T(8,128)(2,1)S(1)} %get-tuple-element.51), channel_id=1, source_target_pairs={{0,8},{8,0},{16,24},{24,16},{1,9},{9,1},{17,25},{25,17},{2,10},{10... | collective-permute-start | bytes 442376 | tf_op jit(solution)/shard_map/ppermute | solution.py:729
  127.3 7.9 %collective-permute-start.14 = (f16[576,128]{1,0:T(8,128)(2,1)S(1)}, f16[576,128]{1,0:T(8,128)(2,1)S(1)}, u32[]{:S(2)}, u32[]{:S(2)}) collective-permute-start(f16[576,128]{1,0:T(8,128)(2,1)S(1)} %get-tuple-element.50), channel_id=1, source_target_pairs={{0,16},{8,24},{16,0},{24,8},{1,17},{9,25},{17,1},{25,9},{2,18},{10... | collective-permute-start | bytes 442376 | tf_op jit(solution)/shard_map/ppermute | solution.py:729
  129.5 6.7 %collective-permute-start.15 = (f16[576,128]{1,0:T(8,128)(2,1)S(1)}, f16[576,128]{1,0:T(8,128)(2,1)S(1)}, u32[]{:S(2)}, u32[]{:S(2)}) collective-permute-start(f16[576,128]{1,0:T(8,128)(2,1)S(1)} %get-tuple-element.49), channel_id=1, source_target_pairs={{0,24},{8,16},{16,8},{24,0},{1,25},{9,17},{17,9},{25,1},{2,26},{10... | collective-permute-start | bytes 442376 | tf_op jit(solution)/shard_map/ppermute | solution.py:729
  (5 other events, 16.6 us)
